TPU v7x, 32 devices: a whole 2x2x4 slice. The times are simulated.
32 devices in a mesh: dp: 4 (over z), seq: 8 (over y, x, core).
Axes of the slice: x: 2, y: 2, z: 4, core: 2. Of those that a mesh axis runs over, the one named last changes fastest.
Arguments:
- values: bfloat16 [4, 65536, 512], P('dp', 'seq'), may hold values from -6 to 6
- cotangent: bfloat16 [4, 65536, 512], P('dp', 'seq'), may hold values from -6 to 6
- kernel: bfloat16 [65536, 512], P('seq'), may hold values from -6 to 6
- left_factor: bfloat16 [256, 256, 256], P('seq'), may hold values from -0.375 to 0.375
- right_factor: bfloat16 [256, 256, 256], P('seq'), may hold values from -0.375 to 0.375
Outputs:
- mixed: bfloat16 [4, 65536, 512], P('dp', 'seq')
- values_grad: bfloat16 [4, 65536, 512], P('dp', 'seq')
- kernel_grad: float32 [65536, 512], P(('seq', 'dp'))
All inputs are finite; a program needn't handle non-finite values.
Results may differ from a plain program's by a relative error of at most 0.018.
Values may be sent and summed in bfloat16 or wider, within the bound.
No kernel may reach another device: no remote copies, remote signals or barrier semaphores. Data moves between devices by JAX's collectives and lax.ppermute only.
A program may use at most 192 MiB of HBM per device.

v0:
```python
import functools

import jax
import jax.numpy as jnp
from jax import lax
from jax.experimental import pallas as pl
from jax.experimental.pallas import tpu as pltpu
from jax.sharding import PartitionSpec as P

WIDTH = 128
ROWS = 16
VMEM_LIMIT = 60 * 1024 * 1024
COST = pl.CostEstimate(flops=1024, bytes_accessed=1024, transcendentals=0)
EARLY = 3
UNROLL = 4
TOKEN = (8, 128)


def moves_of(ranks):
    return [0] + list(range(2, ranks, 2)) + list(range(3, ranks, 2)) + [1]


def left_forward_kernel(ranks, rank_ref, values_ref, cotangent_ref, left_ref, *refs):
    moves = moves_of(ranks)
    *sends, token_ref = refs[-ranks - 1 :]
    token_ref[...] = jnp.zeros_like(token_ref)
    blocks, order, _ = left_ref.shape
    share = order // ranks
    rank = rank_ref[0]
    for i in range(blocks):
        rows = slice(i * order, (i + 1) * order)
        source = values_ref[0, rows, :]
        gated = source.astype(jnp.float32) * cotangent_ref[0, rows, :].astype(jnp.float32)
        both = jnp.concatenate([source, gated.astype(jnp.bfloat16)], axis=1)
        factor = jnp.concatenate(
            [left_ref[i, pl.ds(pl.multiple_of((rank ^ m) * share, share), share), :] for m in moves],
            axis=0,
        )
        first = jnp.dot(factor, both, preferred_element_type=jnp.float32).astype(jnp.bfloat16)
        for m in range(ranks):
            sends[m][i] = first[m * share : (m + 1) * share]


def right_kernel(ranks, rank_ref, kernel_ref, right_ref, *refs):
    arrived = refs[:ranks]
    *sends, term_ref, token_ref, gathered, scattered = refs[-ranks - 4 :]
    token_ref[...] = jnp.zeros_like(token_ref)
    share, rows, lanes = arrived[0].shape
    order = right_ref.shape[1]
    width = lanes // 2
    rank = rank_ref[0]
    halves = [slice(0, width), slice(width, lanes)]

    moves = moves_of(ranks)

    def span(n):
        m = moves[n]
        return pl.ds(pl.multiple_of((rank ^ m) * (share * rows), share * rows), share * rows)

    for m in range(ranks):
        for half in range(2):
            block = arrived[m][:, :, halves[half]].astype(jnp.float32)
            gathered[half, span(m), :] = block.reshape(share * rows, width)

    def step(k, carry):
        both = jnp.concatenate(
            [gathered[half, pl.ds(k, order, stride=rows), :] for half in range(2)], axis=1
        ).astype(jnp.bfloat16)
        factor = right_ref[k]
        result = jnp.dot(factor, both, preferred_element_type=jnp.float32)
        spectrum = result[:, :width].astype(jnp.bfloat16).astype(jnp.float32)
        spectrum_grad = result[:, width:]
        here = pl.ds(pl.multiple_of(k * order, order), order)
        kernel_wide = kernel_ref[here, :].astype(jnp.float32)
        term_ref[here, :] = (spectrum_grad * spectrum).astype(jnp.bfloat16)
        domain = jnp.concatenate(
            [
                (kernel_wide * spectrum).astype(jnp.bfloat16),
                (kernel_wide * spectrum_grad).astype(jnp.bfloat16),
            ],
            axis=1,
        )
        back = lax.dot_general(
            factor, domain, (((0,), (0,)), ((), ())), preferred_element_type=jnp.float32
        )
        for half in range(2):
            scattered[half, pl.ds(k, order, stride=rows), :] = back[:, halves[half]]
        return carry

    def several(g, carry):
        for n in range(UNROLL):
            step(g * UNROLL + n, carry)
        return carry

    lax.fori_loop(0, rows // UNROLL, several, 0)

    for m in range(ranks):
        for half in range(2):
            block = scattered[half, span(m), :].astype(jnp.bfloat16)
            sends[m][:, :, halves[half]] = block.reshape(share, rows, width)


def gate_kernel(*refs):
    pass


def left_back_kernel(ranks, terms, rank_ref, values_ref, cotangent_ref, left_ref, *refs):
    moves = moves_of(ranks)
    arrived, reduced = refs[:ranks], refs[ranks : ranks + terms]
    mixed_ref, values_grad_ref, kernel_grad_ref, token_ref = refs[-4:]
    token_ref[...] = jnp.zeros_like(token_ref)
    blocks, order, _ = left_ref.shape
    share = order // ranks
    width = values_ref.shape[2]
    rank = rank_ref[0]
    for i in range(blocks):
        rows = slice(i * order, (i + 1) * order)
        factor = jnp.concatenate(
            [left_ref[i, pl.ds(pl.multiple_of((rank ^ m) * share, share), share), :] for m in moves],
            axis=0,
        )
        back = jnp.concatenate([arrived[m][i] for m in range(ranks)], axis=0)
        result = lax.dot_general(
            factor, back, (((0,), (0,)), ((), ())), preferred_element_type=jnp.float32
        )
        convolved, carried = result[:, :width], result[:, width:]
        source = values_ref[0, rows, :].astype(jnp.float32)
        upstream = cotangent_ref[0, rows, :].astype(jnp.float32)
        mixed_ref[0, rows, :] = (source * convolved).astype(jnp.bfloat16)
        values_grad_ref[0, rows, :] = (upstream * convolved + carried).astype(jnp.bfloat16)
    for n in range(terms):
        lanes = reduced[n].shape[1]
        kernel_grad_ref[:, n * lanes : (n + 1) * lanes] = reduced[n][...].astype(jnp.float32)


def per_device(values, cotangent, kernel, left_factor, right_factor, ranks, groups):
    sequences, row_count, channels = values.shape
    local, order, _ = left_factor.shape
    width = WIDTH
    lanes = 2 * width
    blocks = min(4, local)
    rows = min(ROWS, local)
    chunks = channels // width
    moves = moves_of(ranks)
    rank = lax.axis_index("seq").astype(jnp.int32).reshape(1)
    params = pltpu.CompilerParams(vmem_limit_bytes=VMEM_LIMIT)
    buffer = jax.ShapeDtypeStruct((local, local, lanes), jnp.bfloat16)

    def field_spec(q):
        return pl.BlockSpec((1, blocks * order, width), lambda g, rank: (0, g, q))

    def factor_spec(size):
        return pl.BlockSpec((size, order, order), lambda g, rank: (g, 0, 0))

    token = jax.ShapeDtypeStruct(TOKEN, jnp.float32)
    token_spec = pl.BlockSpec(TOKEN, lambda g, rank: (0, 0))

    def unread(after):
        return [pl.BlockSpec(memory_space=pl.ANY)] * len(after)

    def left_forward(q, after):
        return pl.pallas_call(
            functools.partial(left_forward_kernel, ranks),
            out_shape=[buffer] * ranks + [token],
            grid_spec=pltpu.PrefetchScalarGridSpec(
                num_scalar_prefetch=1,
                grid=(local // blocks,),
                in_specs=[field_spec(q), field_spec(q), factor_spec(blocks)] + unread(after),
                out_specs=[pl.BlockSpec((blocks, local, lanes), lambda g, rank: (g, 0, 0))] * ranks
                + [token_spec],
            ),
            compiler_params=params,
            cost_estimate=COST,
        )(rank, values, cotangent, left_factor, *after)

    def exchange(sends):
        return [sends[0]] + [
            lax.ppermute(sends[n], "seq", [(r, r ^ moves[n]) for r in range(ranks)])
            for n in range(1, ranks)
        ]

    def right_both(q, arrived, terms, after):
        held = [] if terms is None else [terms]
        moved = pl.BlockSpec((local, rows, lanes), lambda g, rank: (0, g, 0))
        return pl.pallas_call(
            functools.partial(right_kernel, ranks),
            out_shape=[buffer] * ranks
            + [jax.ShapeDtypeStruct((row_count, channels), jnp.bfloat16), token],
            grid_spec=pltpu.PrefetchScalarGridSpec(
                num_scalar_prefetch=1,
                grid=(local // rows,),
                in_specs=[
                    pl.BlockSpec((rows * order, width), lambda g, rank: (g, q)),
                    factor_spec(rows),
                ]
                + [moved] * ranks
                + unread(held)
                + unread(after),
                out_specs=[moved] * ranks
                + [pl.BlockSpec((rows * order, width), lambda g, rank: (g, q)), token_spec],
                scratch_shapes=[
                    pltpu.VMEM((2, order * rows, width), jnp.float32),
                    pltpu.VMEM((2, order * rows, width), jnp.float32),
                ],
            ),
            input_output_aliases={3 + ranks: ranks} if held else {},
            compiler_params=params,
            cost_estimate=COST,
        )(rank, kernel, right_factor, *arrived, *held, *after)

    def gate(held, after):
        return list(
            pl.pallas_call(
                gate_kernel,
                out_shape=[jax.ShapeDtypeStruct(x.shape, x.dtype) for x in held],
                in_specs=unread(held) + unread(after),
                out_specs=unread(held),
                input_output_aliases={n: n for n in range(len(held))},
                compiler_params=params,
                cost_estimate=COST,
            )(*held, *after)
        )

    def left_back(q, arrived, reduced, outputs, after):
        steps = local // blocks
        shard = row_count // groups
        out_shape = [
            jax.ShapeDtypeStruct(values.shape, jnp.bfloat16),
            jax.ShapeDtypeStruct(values.shape, jnp.bfloat16),
            jax.ShapeDtypeStruct((shard, channels), jnp.float32),
            token,
        ]
        earlier = list(outputs) if outputs else []
        terms = len(reduced)
        aliases = {4 + ranks + terms + n: n for n in range(len(earlier))}
        grad_spec = pl.BlockSpec((shard // steps, channels), lambda g, rank: (g, 0))
        return pl.pallas_call(
            functools.partial(left_back_kernel, ranks, terms),
            out_shape=out_shape,
            grid_spec=pltpu.PrefetchScalarGridSpec(
                num_scalar_prefetch=1,
                grid=(steps,),
                in_specs=[
                    field_spec(q),
                    field_spec(q),
                    factor_spec(blocks),
                ]
                + [pl.BlockSpec((blocks, local, lanes), lambda g, rank: (g, 0, 0))] * ranks
                + [pl.BlockSpec((shard // steps, channels), lambda g, rank: (g, 0))] * terms
                + unread(earlier)
                + unread(after),
                out_specs=[
                    field_spec(q),
                    field_spec(q),
                    grad_spec if terms else pl.BlockSpec(memory_space=pl.ANY),
                    token_spec,
                ],
            ),
            input_output_aliases=aliases,
            compiler_params=params,
            cost_estimate=COST,
        )(rank, values, cotangent, left_factor, *arrived, *reduced, *earlier, *after)

    received, sent, returned = {}, {}, {}
    left_tokens, right_tokens, back_tokens = {}, {}, {}
    terms, outputs = None, []

    def do_left(q):
        after = [left_tokens[q - 1]] if q else []
        if q >= 2:
            after.append(right_tokens[q - 2])
        *sends, left_tokens[q] = left_forward(q, after)
        received[q] = exchange(sends)

    for q in range(min(2, chunks)):
        do_left(q)
    for q in range(chunks):
        after = [right_tokens[q - 1]] if q else []
        *sent[q], terms, right_tokens[q] = right_both(q, received[q], terms, after)
        if q + 2 < chunks:
            do_left(q + 2)

    def back_step(q):
        last = [reduced] if q == chunks - 1 else []
        *outputs[:], back_tokens[q] = left_back(q, returned[q], last, outputs, [right_tokens[chunks - 1]])

    for q in range(chunks):
        after = []
        if 1 <= q < chunks - 1:
            after.append(right_tokens[chunks - 1])
        if q >= 2:
            after.append(back_tokens[q - 2])
        returned[q] = exchange(sent[q][:1] + gate(sent[q][1:], after) if after else sent[q])
        if q == 0:
            (terms,) = gate([terms], returned[0][1 : 1 + EARLY])
            reduced = lax.psum_scatter(terms, "dp", scatter_dimension=0, tiled=True)
        if q >= 1:
            back_step(q - 1)
    back_step(chunks - 1)
    return tuple(outputs)


def solution(mesh):
    in_specs = (
        P("dp", "seq", None),
        P("dp", "seq", None),
        P("seq", None),
        P("seq", None, None),
        P("seq", None, None),
    )
    out_specs = (P("dp", "seq", None), P("dp", "seq", None), P(("seq", "dp"), None))
    return jax.shard_map(
        functools.partial(per_device, ranks=mesh.shape["seq"], groups=mesh.shape["dp"]),
        mesh=mesh,
        in_specs=in_specs,
        out_specs=out_specs,
        check_vma=False,
    )
```

profile of v0, /device:TPU:0, one launch (start us, length us, event | category | flops | bytes accessed | tf_op | source)
XLA Modules:
  0.0 419.8 jit_solution(4936140700951689753)
XLA Ops:
  7.2 8.2 %shard_map.76 = (bf16[32,32,256]{2,1,0:T(8,128)(2,1)}, bf16[32,32,256]{2,1,0:T(8,128)(2,1)}, bf16[32,32,256]{2,1,0:T(8,128)(2,1)}, bf16[32,32,256]{2,1,0:T(8,128...) custom-call(s32[1]{0:T(128)} %bitcast.rank_ref, ...), custom_call_target="tpu_custom_call" | custom-call | flops 1024 | bytes 1024 | tf_op jit(solution)/shard_map/pallas_call | solution.py:162
  23.2 8.2 %collective-permute-done.refs_1_ = bf16[32,32,256]{2,1,0:T(8,128)(2,1)S(1)} collective-permute-done((bf16[32,32,256]{2,1,0:T(8,128)(2,1)}, bf16[32,32,256]{2,1,0:T(8,128)(2,1)S(1)}, u32[]{:S(2)}, u32[]{:S(2)}) %collective-permute-start) | collective-permute-done | bytes 524320 | tf_op jit(solution)/shard_map/ppermute | solution.py:178
  31.8 12.9 %collective-permute-done.1.refs_2_ = bf16[32,32,256]{2,1,0:T(8,128)(2,1)S(1)} collective-permute-done((bf16[32,32,256]{2,1,0:T(8,128)(2,1)}, bf16[32,32,256]{2,1,0:T(8,128)(2,1)S(1)}, u32[]{:S(2)}, u32[]{:S(2)}) %collective-permute-start.1) | collective-permute-done | bytes 524320 | tf_op jit(solution)/shard_map/ppermute | solution.py:178
  44.8 8.4 %shard_map.77 = (bf16[32,32,256]{2,1,0:T(8,128)(2,1)}, bf16[32,32,256]{2,1,0:T(8,128)(2,1)}, bf16[32,32,256]{2,1,0:T(8,128)(2,1)}, bf16[32,32,256]{2,1,0:T(8,128...) custom-call(s32[1]{0:T(128)} %bitcast.rank_ref, ...), custom_call_target="tpu_custom_call" | custom-call | flops 1024 | bytes 1024 | tf_op jit(solution)/shard_map/pallas_call | solution.py:162
  55.3 10.8 %collective-permute-done.4.refs_5_ = bf16[32,32,256]{2,1,0:T(8,128)(2,1)S(1)} collective-permute-done((bf16[32,32,256]{2,1,0:T(8,128)(2,1)}, bf16[32,32,256]{2,1,0:T(8,128)(2,1)S(1)}, u32[]{:S(2)}, u32[]{:S(2)}) %collective-permute-start.4) | collective-permute-done | bytes 524320 | tf_op jit(solution)/shard_map/ppermute | solution.py:178
  70.3 15.1 %shard_map.78 = (bf16[32,32,256]{2,1,0:T(8,128)(2,1)}, bf16[32,32,256]{2,1,0:T(8,128)(2,1)}, bf16[32,32,256]{2,1,0:T(8,128)(2,1)}, bf16[32,32,256]{2,1,0:T(8,128...) custom-call(s32[1]{0:T(128)} %bitcast.rank_ref, ...), custom_call_target="tpu_custom_call" | custom-call | flops 1024 | bytes 1024 | tf_op jit(solution)/shard_map/pallas_call | solution.py:185
  85.4 8.2 %shard_map.79 = (bf16[32,32,256]{2,1,0:T(8,128)(2,1)}, bf16[32,32,256]{2,1,0:T(8,128)(2,1)}, bf16[32,32,256]{2,1,0:T(8,128)(2,1)}, bf16[32,32,256]{2,1,0:T(8,128...) custom-call(s32[1]{0:T(128)} %bitcast.rank_ref, ...), custom_call_target="tpu_custom_call" | custom-call | flops 1024 | bytes 1024 | tf_op jit(solution)/shard_map/pallas_call | solution.py:162
  100.9 10.1 %collective-permute-done.11.refs_5_ = bf16[32,32,256]{2,1,0:T(8,128)(2,1)S(1)} collective-permute-done((bf16[32,32,256]{2,1,0:T(8,128)(2,1)}, bf16[32,32,256]{2,1,0:T(8,128)(2,1)S(1)}, u32[]{:S(2)}, u32[]{:S(2)}) %collective-permute-start.11) | collective-permute-done | bytes 524320 | tf_op jit(solution)/shard_map/ppermute | solution.py:178
  121.9 11.6 %collective-permute-done.22.refs_2_ = bf16[32,32,256]{2,1,0:T(8,128)(2,1)S(1)} collective-permute-done((bf16[32,32,256]{2,1,0:T(8,128)(2,1)}, bf16[32,32,256]{2,1,0:T(8,128)(2,1)S(1)}, u32[]{:S(2)}, u32[]{:S(2)}) %collective-permute-start.22) | collective-permute-done | bytes 524320 | tf_op jit(solution)/shard_map/ppermute | solution.py:178
  133.6 15.1 %shard_map.80 = (bf16[32,32,256]{2,1,0:T(8,128)(2,1)}, bf16[32,32,256]{2,1,0:T(8,128)(2,1)}, bf16[32,32,256]{2,1,0:T(8,128)(2,1)}, bf16[32,32,256]{2,1,0:T(8,128...) custom-call(s32[1]{0:T(128)} %bitcast.rank_ref, ...), custom_call_target="tpu_custom_call", output_to_operand_aliasing={{8}: (11, {})} | custom-call | flops 1024 | bytes 1024 | tf_op jit(solution)/shard_map/pallas_call | solution.py:185
  148.7 8.3 %shard_map.81 = (bf16[32,32,256]{2,1,0:T(8,128)(2,1)}, bf16[32,32,256]{2,1,0:T(8,128)(2,1)}, bf16[32,32,256]{2,1,0:T(8,128)(2,1)}, bf16[32,32,256]{2,1,0:T(8,128...) custom-call(s32[1]{0:T(128)} %bitcast.rank_ref, ...), custom_call_target="tpu_custom_call" | custom-call | flops 1024 | bytes 1024 | tf_op jit(solution)/shard_map/pallas_call | solution.py:162
  162.8 9.2 %collective-permute-done.14.refs_1_ = bf16[32,32,256]{2,1,0:T(8,128)(2,1)S(1)} collective-permute-done((bf16[32,32,256]{2,1,0:T(8,128)(2,1)}, bf16[32,32,256]{2,1,0:T(8,128)(2,1)S(1)}, u32[]{:S(2)}, u32[]{:S(2)}) %collective-permute-start.14) | collective-permute-done | bytes 524320 | tf_op jit(solution)/shard_map/ppermute | solution.py:178
  173.0 10.4 %collective-permute-done.15.refs_2_ = bf16[32,32,256]{2,1,0:T(8,128)(2,1)S(1)} collective-permute-done((bf16[32,32,256]{2,1,0:T(8,128)(2,1)}, bf16[32,32,256]{2,1,0:T(8,128)(2,1)S(1)}, u32[]{:S(2)}, u32[]{:S(2)}) %collective-permute-start.15) | collective-permute-done | bytes 524320 | tf_op jit(solution)/shard_map/ppermute | solution.py:178
  185.7 7.7 %collective-permute-done.17.refs_4_ = bf16[32,32,256]{2,1,0:T(8,128)(2,1)S(1)} collective-permute-done((bf16[32,32,256]{2,1,0:T(8,128)(2,1)}, bf16[32,32,256]{2,1,0:T(8,128)(2,1)S(1)}, u32[]{:S(2)}, u32[]{:S(2)}) %collective-permute-start.17) | collective-permute-done | bytes 524320 | tf_op jit(solution)/shard_map/ppermute | solution.py:178
  195.8 10.0 %collective-permute-done.18.refs_5_ = bf16[32,32,256]{2,1,0:T(8,128)(2,1)S(1)} collective-permute-done((bf16[32,32,256]{2,1,0:T(8,128)(2,1)}, bf16[32,32,256]{2,1,0:T(8,128)(2,1)S(1)}, u32[]{:S(2)}, u32[]{:S(2)}) %collective-permute-start.18) | collective-permute-done | bytes 524320 | tf_op jit(solution)/shard_map/ppermute | solution.py:178
  207.9 14.9 %shard_map.82 = (bf16[32,32,256]{2,1,0:T(8,128)(2,1)}, bf16[32,32,256]{2,1,0:T(8,128)(2,1)}, bf16[32,32,256]{2,1,0:T(8,128)(2,1)}, bf16[32,32,256]{2,1,0:T(8,128...) custom-call(s32[1]{0:T(128)} %bitcast.rank_ref, ...), custom_call_target="tpu_custom_call", output_to_operand_aliasing={{8}: (11, {})} | custom-call | flops 1024 | bytes 1024 | tf_op jit(solution)/shard_map/pallas_call | solution.py:185
  222.9 15.1 %shard_map.83 = (bf16[32,32,256]{2,1,0:T(8,128)(2,1)}, bf16[32,32,256]{2,1,0:T(8,128)(2,1)}, bf16[32,32,256]{2,1,0:T(8,128)(2,1)}, bf16[32,32,256]{2,1,0:T(8,128...) custom-call(s32[1]{0:T(128)} %bitcast.rank_ref, ...), custom_call_target="tpu_custom_call", output_to_operand_aliasing={{8}: (11, {})} | custom-call | flops 1024 | bytes 1024 | tf_op jit(solution)/shard_map/pallas_call | solution.py:185
  245.2 8.5 %collective-permute-done.38.refs_4_ = bf16[32,32,256]{2,1,0:T(8,128)(2,1)S(1)} collective-permute-done((bf16[32,32,256]{2,1,0:T(8,128)(2,1)S(1)}, bf16[32,32,256]{2,1,0:T(8,128)(2,1)S(1)}, u32[]{:S(2)}, u32[]{:S(2)}) %collective-permute-start.38) | collective-permute-done | bytes 524320 | tf_op jit(solution)/shard_map/ppermute | solution.py:178
  255.8 8.4 %collective-permute-start.30 = (bf16[32,32,256]{2,1,0:T(8,128)(2,1)}, bf16[32,32,256]{2,1,0:T(8,128)(2,1)S(1)}, u32[]{:S(2)}, u32[]{:S(2)}) collective-permute-start(bf16[32,32,256]{2,1,0:T(8,128)(2,1)} %get-tuple-element.173), channel_id=1, source_target_pairs={{0,6},{1,7},{2,4},{3,5},{4,2},{5,3},{6,0},{7,1},{8,14},{9,15},{10,... | collective-permute-start | bytes 1572872 | tf_op jit(solution)/shard_map/ppermute | solution.py:178
  269.6 9.1 %collective-permute-done.28.refs_1_ = bf16[32,32,256]{2,1,0:T(8,128)(2,1)S(1)} collective-permute-done((bf16[32,32,256]{2,1,0:T(8,128)(2,1)}, bf16[32,32,256]{2,1,0:T(8,128)(2,1)S(1)}, u32[]{:S(2)}, u32[]{:S(2)}) %collective-permute-start.28) | collective-permute-done | bytes 524320 | tf_op jit(solution)/shard_map/ppermute | solution.py:178
  278.8 10.9 %collective-permute-done.29.refs_2_ = bf16[32,32,256]{2,1,0:T(8,128)(2,1)S(1)} collective-permute-done((bf16[32,32,256]{2,1,0:T(8,128)(2,1)}, bf16[32,32,256]{2,1,0:T(8,128)(2,1)S(1)}, u32[]{:S(2)}, u32[]{:S(2)}) %collective-permute-start.29) | collective-permute-done | bytes 524320 | tf_op jit(solution)/shard_map/ppermute | solution.py:178
  289.7 9.5 %shard_map.85 = (bf16[1,8192,512]{2,1,0:T(8,128)(2,1)}, bf16[1,8192,512]{2,1,0:T(8,128)(2,1)}, f32[2048,512]{1,0:T(8,128)}, f32[8,128]{1,0:T(8,128)}) custom-call(s32[1]{0:T(128)} %bitcast.rank_ref, bf16[1,8192,512]{2,1,0:T(8,128)(2,1)} %values_ref.15, bf16[1,8192,512]{2,1,0:T(8,128)(2,1)} %cotangent_ref.15, bf16[32,256,256]{2,1,0:T(8,128)(2,1)} %left_ref.15, ...), custom_call_target="tpu_custom_call" | custom-call | flops 1024 | bytes 1024 | tf_op jit(solution)/shard_map/pallas_call | solution.py:237
  301.9 8.0 %collective-permute-start.51 = (bf16[32,32,256]{2,1,0:T(8,128)(2,1)}, bf16[32,32,256]{2,1,0:T(8,128)(2,1)S(1)}, u32[]{:S(2)}, u32[]{:S(2)}) collective-permute-start(bf16[32,32,256]{2,1,0:T(8,128)(2,1)} %get-tuple-element.209), channel_id=1, source_target_pairs={{0,6},{1,7},{2,4},{3,5},{4,2},{5,3},{6,0},{7,1},{8,14},{9,15},{10,... | collective-permute-start | bytes 1572872 | tf_op jit(solution)/shard_map/ppermute | solution.py:178
  313.9 9.4 %shard_map.86 = (bf16[1,8192,512]{2,1,0:T(8,128)(2,1)}, bf16[1,8192,512]{2,1,0:T(8,128)(2,1)}, f32[2048,512]{1,0:T(8,128)}, f32[8,128]{1,0:T(8,128)}) custom-call(s32[1]{0:T(128)} %bitcast.rank_ref, bf16[1,8192,512]{2,1,0:T(8,128)(2,1)} %values_ref.15, ...), custom_call_target="tpu_custom_call", output_to_operand_aliasing={{0}: (12, {}), {1}: (13, {}), {2}: (14, {})} | custom-call | flops 1024 | bytes 1024 | tf_op jit(solution)/shard_map/pallas_call | solution.py:237
  326.7 7.9 %collective-permute-done.50.refs_2_ = bf16[32,32,256]{2,1,0:T(8,128)(2,1)S(1)} collective-permute-done((bf16[32,32,256]{2,1,0:T(8,128)(2,1)}, bf16[32,32,256]{2,1,0:T(8,128)(2,1)S(1)}, u32[]{:S(2)}, u32[]{:S(2)}) %collective-permute-start.50) | collective-permute-done | bytes 524320 | tf_op jit(solution)/shard_map/ppermute | solution.py:178
  336.5 7.3 %collective-permute-done.52.refs_4_ = bf16[32,32,256]{2,1,0:T(8,128)(2,1)S(1)} collective-permute-done((bf16[32,32,256]{2,1,0:T(8,128)(2,1)}, bf16[32,32,256]{2,1,0:T(8,128)(2,1)S(1)}, u32[]{:S(2)}, u32[]{:S(2)}) %collective-permute-start.52) | collective-permute-done | bytes 524320 | tf_op jit(solution)/shard_map/ppermute | solution.py:178
  347.4 9.2 %collective-permute-done.54.refs_6_ = bf16[32,32,256]{2,1,0:T(8,128)(2,1)S(1)} collective-permute-done((bf16[32,32,256]{2,1,0:T(8,128)(2,1)}, bf16[32,32,256]{2,1,0:T(8,128)(2,1)S(1)}, u32[]{:S(2)}, u32[]{:S(2)}) %collective-permute-start.54) | collective-permute-done | bytes 524320 | tf_op jit(solution)/shard_map/ppermute | solution.py:178
  358.6 10.3 %collective-permute-done.42.refs_1_ = bf16[32,32,256]{2,1,0:T(8,128)(2,1)S(1)} collective-permute-done((bf16[32,32,256]{2,1,0:T(8,128)(2,1)}, bf16[32,32,256]{2,1,0:T(8,128)(2,1)S(1)}, u32[]{:S(2)}, u32[]{:S(2)}) %collective-permute-start.42) | collective-permute-done | bytes 524320 | tf_op jit(solution)/shard_map/ppermute | solution.py:178
  368.8 10.6 %collective-permute-done.43.refs_2_ = bf16[32,32,256]{2,1,0:T(8,128)(2,1)S(1)} collective-permute-done((bf16[32,32,256]{2,1,0:T(8,128)(2,1)}, bf16[32,32,256]{2,1,0:T(8,128)(2,1)S(1)}, u32[]{:S(2)}, u32[]{:S(2)}) %collective-permute-start.43) | collective-permute-done | bytes 524320 | tf_op jit(solution)/shard_map/ppermute | solution.py:178
  379.5 9.5 %shard_map.90 = (bf16[1,8192,512]{2,1,0:T(8,128)(2,1)}, bf16[1,8192,512]{2,1,0:T(8,128)(2,1)}, f32[2048,512]{1,0:T(8,128)}, f32[8,128]{1,0:T(8,128)}) custom-call(s32[1]{0:T(128)} %bitcast.rank_ref, bf16[1,8192,512]{2,1,0:T(8,128)(2,1)} %values_ref.15, ...), custom_call_target="tpu_custom_call", output_to_operand_aliasing={{0}: (12, {}), {1}: (13, {}), {2}: (14, {})} | custom-call | flops 1024 | bytes 1024 | tf_op jit(solution)/shard_map/pallas_call | solution.py:237
  390.5 11.2 %collective-permute-done.47.refs_6_ = bf16[32,32,256]{2,1,0:T(8,128)(2,1)} collective-permute-done((bf16[32,32,256]{2,1,0:T(8,128)(2,1)}, bf16[32,32,256]{2,1,0:T(8,128)(2,1)}, u32[]{:S(2)}, u32[]{:S(2)}) %collective-permute-start.47) | collective-permute-done | bytes 524320 | tf_op jit(solution)/shard_map/ppermute | solution.py:178
  401.7 11.2 %shard_map.91 = (bf16[1,8192,512]{2,1,0:T(8,128)(2,1)}, bf16[1,8192,512]{2,1,0:T(8,128)(2,1)}, f32[2048,512]{1,0:T(8,128)}, f32[8,128]{1,0:T(8,128)}) custom-call(s32[1]{0:T(128)} %bitcast.rank_ref, bf16[1,8192,512]{2,1,0:T(8,128)(2,1)} %values_ref.15, ...), custom_call_target="tpu_custom_call", output_to_operand_aliasing={{0}: (13, {}), {1}: (14, {}), {2}: (15, {})} | custom-call | flops 1024 | bytes 1024 | tf_op jit(solution)/shard_map/pallas_call | solution.py:237
  (189 shorter events, 79.9 us)
Async XLA Ops:
  7.2 394.6 %reduce-scatter.2.cloned.1.call-start = ((), (), s32[]{:S(2)}) async-start(), calls=%async_computation.1 | async-start | bytes 10485760 | tf_op jit(solution)/shard_map/reduce_scatter | solution.py:296
  20.0 33.3 %collective-permute-start.2 = (bf16[32,32,256]{2,1,0:T(8,128)(2,1)}, bf16[32,32,256]{2,1,0:T(8,128)(2,1)S(1)}, u32[]{:S(2)}, u32[]{:S(2)}) collective-permute-start(bf16[32,32,256]{2,1,0:T(8,128)(2,1)} %get-tuple-element.118), channel_id=1, source_target_pairs={{0,6},{1,7},{2,4},{3,5},{4,2},{5,3},{6,0},{7,1},{8,14},{9,15},{10,... | collective-permute-start | bytes 1572872 | tf_op jit(solution)/shard_map/ppermute | solution.py:178
  20.0 33.6 %collective-permute-start.3 = (bf16[32,32,256]{2,1,0:T(8,128)(2,1)}, bf16[32,32,256]{2,1,0:T(8,128)(2,1)S(1)}, u32[]{:S(2)}, u32[]{:S(2)}) collective-permute-start(bf16[32,32,256]{2,1,0:T(8,128)(2,1)} %get-tuple-element.119), channel_id=1, source_target_pairs={{0,3},{1,2},{2,1},{3,0},{4,7},{5,6},{6,5},{7,4},{8,11},{9,10},{10,... | collective-permute-start | bytes 1572872 | tf_op jit(solution)/shard_map/ppermute | solution.py:178
  20.5 45.7 %collective-permute-start.4 = (bf16[32,32,256]{2,1,0:T(8,128)(2,1)}, bf16[32,32,256]{2,1,0:T(8,128)(2,1)S(1)}, u32[]{:S(2)}, u32[]{:S(2)}) collective-permute-start(bf16[32,32,256]{2,1,0:T(8,128)(2,1)} %get-tuple-element.120), channel_id=1, source_target_pairs={{0,5},{1,4},{2,7},{3,6},{4,1},{5,0},{6,3},{7,2},{8,13},{9,12},{10,... | collective-permute-start | bytes 1572872 | tf_op jit(solution)/shard_map/ppermute | solution.py:178
  31.4 35.6 %collective-permute-start.5 = (bf16[32,32,256]{2,1,0:T(8,128)(2,1)}, bf16[32,32,256]{2,1,0:T(8,128)(2,1)}, u32[]{:S(2)}, u32[]{:S(2)}) collective-permute-start(bf16[32,32,256]{2,1,0:T(8,128)(2,1)} %get-tuple-element.121), channel_id=1, source_target_pairs={{0,7},{1,6},{2,5},{3,4},{4,3},{5,2},{6,1},{7,0},{8,15},{9,14},{10,... | collective-permute-start | bytes 1572872 | tf_op jit(solution)/shard_map/ppermute | solution.py:178
  53.2 40.4 %collective-permute-start.7 = (bf16[32,32,256]{2,1,0:T(8,128)(2,1)}, bf16[32,32,256]{2,1,0:T(8,128)(2,1)S(1)}, u32[]{:S(2)}, u32[]{:S(2)}) collective-permute-start(bf16[32,32,256]{2,1,0:T(8,128)(2,1)} %get-tuple-element.126), channel_id=1, source_target_pairs={{0,2},{1,3},{2,0},{3,1},{4,6},{5,7},{6,4},{7,5},{8,10},{9,11},{10,... | collective-permute-start | bytes 1572872 | tf_op jit(solution)/shard_map/ppermute | solution.py:178
  53.6 40.1 %collective-permute-start.8 = (bf16[32,32,256]{2,1,0:T(8,128)(2,1)}, bf16[32,32,256]{2,1,0:T(8,128)(2,1)S(1)}, u32[]{:S(2)}, u32[]{:S(2)}) collective-permute-start(bf16[32,32,256]{2,1,0:T(8,128)(2,1)} %get-tuple-element.127), channel_id=1, source_target_pairs={{0,4},{1,5},{2,6},{3,7},{4,0},{5,1},{6,2},{7,3},{8,12},{9,13},{10,... | collective-permute-start | bytes 1572872 | tf_op jit(solution)/shard_map/ppermute | solution.py:178
  70.3 40.7 %collective-permute-start.11 = (bf16[32,32,256]{2,1,0:T(8,128)(2,1)}, bf16[32,32,256]{2,1,0:T(8,128)(2,1)S(1)}, u32[]{:S(2)}, u32[]{:S(2)}) collective-permute-start(bf16[32,32,256]{2,1,0:T(8,128)(2,1)} %get-tuple-element.130), channel_id=1, source_target_pairs={{0,5},{1,4},{2,7},{3,6},{4,1},{5,0},{6,3},{7,2},{8,13},{9,12},{10,... | collective-permute-start | bytes 1572872 | tf_op jit(solution)/shard_map/ppermute | solution.py:178
  99.4 34.1 %collective-permute-start.22 = (bf16[32,32,256]{2,1,0:T(8,128)(2,1)}, bf16[32,32,256]{2,1,0:T(8,128)(2,1)S(1)}, u32[]{:S(2)}, u32[]{:S(2)}) collective-permute-start(bf16[32,32,256]{2,1,0:T(8,128)(2,1)} %get-tuple-element.145), channel_id=1, source_target_pairs={{0,4},{1,5},{2,6},{3,7},{4,0},{5,1},{6,2},{7,3},{8,12},{9,13},{10,... | collective-permute-start | bytes 1572872 | tf_op jit(solution)/shard_map/ppermute | solution.py:178
  111.9 45.1 %collective-permute-start.23 = (bf16[32,32,256]{2,1,0:T(8,128)(2,1)}, bf16[32,32,256]{2,1,0:T(8,128)(2,1)S(1)}, u32[]{:S(2)}, u32[]{:S(2)}) collective-permute-start(bf16[32,32,256]{2,1,0:T(8,128)(2,1)} %get-tuple-element.146), channel_id=1, source_target_pairs={{0,6},{1,7},{2,4},{3,5},{4,2},{5,3},{6,0},{7,1},{8,14},{9,15},{10,... | collective-permute-start | bytes 1572872 | tf_op jit(solution)/shard_map/ppermute | solution.py:178
  111.9 45.2 %collective-permute-start.24 = (bf16[32,32,256]{2,1,0:T(8,128)(2,1)}, bf16[32,32,256]{2,1,0:T(8,128)(2,1)S(1)}, u32[]{:S(2)}, u32[]{:S(2)}) collective-permute-start(bf16[32,32,256]{2,1,0:T(8,128)(2,1)} %get-tuple-element.147), channel_id=1, source_target_pairs={{0,3},{1,2},{2,1},{3,0},{4,7},{5,6},{6,5},{7,4},{8,11},{9,10},{10,... | collective-permute-start | bytes 1572872 | tf_op jit(solution)/shard_map/ppermute | solution.py:178
  115.1 44.4 %collective-permute-start.25 = (bf16[32,32,256]{2,1,0:T(8,128)(2,1)}, bf16[32,32,256]{2,1,0:T(8,128)(2,1)S(1)}, u32[]{:S(2)}, u32[]{:S(2)}) collective-permute-start(bf16[32,32,256]{2,1,0:T(8,128)(2,1)} %get-tuple-element.148), channel_id=1, source_target_pairs={{0,5},{1,4},{2,7},{3,6},{4,1},{5,0},{6,3},{7,2},{8,13},{9,12},{10,... | collective-permute-start | bytes 1572872 | tf_op jit(solution)/shard_map/ppermute | solution.py:178
  121.5 39.5 %collective-permute-start.26 = (bf16[32,32,256]{2,1,0:T(8,128)(2,1)}, bf16[32,32,256]{2,1,0:T(8,128)(2,1)}, u32[]{:S(2)}, u32[]{:S(2)}) collective-permute-start(bf16[32,32,256]{2,1,0:T(8,128)(2,1)} %get-tuple-element.149), channel_id=1, source_target_pairs={{0,7},{1,6},{2,5},{3,4},{4,3},{5,2},{6,1},{7,0},{8,15},{9,14},{10,... | collective-permute-start | bytes 1572872 | tf_op jit(solution)/shard_map/ppermute | solution.py:178
  161.0 44.8 %collective-permute-start.18 = (bf16[32,32,256]{2,1,0:T(8,128)(2,1)}, bf16[32,32,256]{2,1,0:T(8,128)(2,1)S(1)}, u32[]{:S(2)}, u32[]{:S(2)}) collective-permute-start(bf16[32,32,256]{2,1,0:T(8,128)(2,1)} %get-tuple-element.140), channel_id=1, source_target_pairs={{0,5},{1,4},{2,7},{3,6},{4,1},{5,0},{6,3},{7,2},{8,13},{9,12},{10,... | collective-permute-start | bytes 1572872 | tf_op jit(solution)/shard_map/ppermute | solution.py:178
  172.0 50.9 %collective-permute-start.19 = (bf16[32,32,256]{2,1,0:T(8,128)(2,1)}, bf16[32,32,256]{2,1,0:T(8,128)(2,1)}, u32[]{:S(2)}, u32[]{:S(2)}) collective-permute-start(bf16[32,32,256]{2,1,0:T(8,128)(2,1)} %get-tuple-element.141), channel_id=1, source_target_pairs={{0,7},{1,6},{2,5},{3,4},{4,3},{5,2},{6,1},{7,0},{8,15},{9,14},{10,... | collective-permute-start | bytes 1572872 | tf_op jit(solution)/shard_map/ppermute | solution.py:178
  183.4 39.6 %collective-permute-start.20 = (bf16[32,32,256]{2,1,0:T(8,128)(2,1)}, bf16[32,32,256]{2,1,0:T(8,128)(2,1)}, u32[]{:S(2)}, u32[]{:S(2)}) collective-permute-start(bf16[32,32,256]{2,1,0:T(8,128)(2,1)} %get-tuple-element.142), channel_id=1, source_target_pairs={{0,1},{1,0},{2,3},{3,2},{4,5},{5,4},{6,7},{7,6},{8,9},{9,8},{10,11... | collective-permute-start | bytes 1572872 | tf_op jit(solution)/shard_map/ppermute | solution.py:178
  185.1 52.9 %collective-permute-start.35 = (bf16[32,32,256]{2,1,0:T(8,128)(2,1)}, bf16[32,32,256]{2,1,0:T(8,128)(2,1)S(1)}, u32[]{:S(2)}, u32[]{:S(2)}) collective-permute-start(bf16[32,32,256]{2,1,0:T(8,128)(2,1)} %get-tuple-element.179), channel_id=1, source_target_pairs={{0,2},{1,3},{2,0},{3,1},{4,6},{5,7},{6,4},{7,5},{8,10},{9,11},{10,... | collective-permute-start | bytes 1572872 | tf_op jit(solution)/shard_map/ppermute | solution.py:178
  193.4 44.6 %collective-permute-start.36 = (bf16[32,32,256]{2,1,0:T(8,128)(2,1)}, bf16[32,32,256]{2,1,0:T(8,128)(2,1)S(1)}, u32[]{:S(2)}, u32[]{:S(2)}) collective-permute-start(bf16[32,32,256]{2,1,0:T(8,128)(2,1)} %get-tuple-element.180), channel_id=1, source_target_pairs={{0,4},{1,5},{2,6},{3,7},{4,0},{5,1},{6,2},{7,3},{8,12},{9,13},{10,... | collective-permute-start | bytes 1572872 | tf_op jit(solution)/shard_map/ppermute | solution.py:178
  244.6 34.2 %collective-permute-start.28 = (bf16[32,32,256]{2,1,0:T(8,128)(2,1)}, bf16[32,32,256]{2,1,0:T(8,128)(2,1)S(1)}, u32[]{:S(2)}, u32[]{:S(2)}) collective-permute-start(bf16[32,32,256]{2,1,0:T(8,128)(2,1)} %get-tuple-element.171), channel_id=1, source_target_pairs={{0,2},{1,3},{2,0},{3,1},{4,6},{5,7},{6,4},{7,5},{8,10},{9,11},{10,... | collective-permute-start | bytes 1572872 | tf_op jit(solution)/shard_map/ppermute | solution.py:178
  253.7 36.0 %collective-permute-start.29 = (bf16[32,32,256]{2,1,0:T(8,128)(2,1)}, bf16[32,32,256]{2,1,0:T(8,128)(2,1)S(1)}, u32[]{:S(2)}, u32[]{:S(2)}) collective-permute-start(bf16[32,32,256]{2,1,0:T(8,128)(2,1)} %get-tuple-element.172), channel_id=1, source_target_pairs={{0,4},{1,5},{2,6},{3,7},{4,0},{5,1},{6,2},{7,3},{8,12},{9,13},{10,... | collective-permute-start | bytes 1572872 | tf_op jit(solution)/shard_map/ppermute | solution.py:178
  255.8 43.5 %collective-permute-start.30 = (bf16[32,32,256]{2,1,0:T(8,128)(2,1)}, bf16[32,32,256]{2,1,0:T(8,128)(2,1)S(1)}, u32[]{:S(2)}, u32[]{:S(2)}) collective-permute-start(bf16[32,32,256]{2,1,0:T(8,128)(2,1)} %get-tuple-element.173), channel_id=1, source_target_pairs={{0,6},{1,7},{2,4},{3,5},{4,2},{5,3},{6,0},{7,1},{8,14},{9,15},{10,... | collective-permute-start | bytes 1572872 | tf_op jit(solution)/shard_map/ppermute | solution.py:178
  266.5 34.5 %collective-permute-start.31 = (bf16[32,32,256]{2,1,0:T(8,128)(2,1)}, bf16[32,32,256]{2,1,0:T(8,128)(2,1)S(1)}, u32[]{:S(2)}, u32[]{:S(2)}) collective-permute-start(bf16[32,32,256]{2,1,0:T(8,128)(2,1)} %get-tuple-element.174), channel_id=1, source_target_pairs={{0,3},{1,2},{2,1},{3,0},{4,7},{5,6},{6,5},{7,4},{8,11},{9,10},{10,... | collective-permute-start | bytes 1572872 | tf_op jit(solution)/shard_map/ppermute | solution.py:178
  268.0 33.1 %collective-permute-start.32 = (bf16[32,32,256]{2,1,0:T(8,128)(2,1)}, bf16[32,32,256]{2,1,0:T(8,128)(2,1)S(1)}, u32[]{:S(2)}, u32[]{:S(2)}) collective-permute-start(bf16[32,32,256]{2,1,0:T(8,128)(2,1)} %get-tuple-element.175), channel_id=1, source_target_pairs={{0,5},{1,4},{2,7},{3,6},{4,1},{5,0},{6,3},{7,2},{8,13},{9,12},{10,... | collective-permute-start | bytes 1572872 | tf_op jit(solution)/shard_map/ppermute | solution.py:178
  278.8 32.9 %collective-permute-start.33 = (bf16[32,32,256]{2,1,0:T(8,128)(2,1)}, bf16[32,32,256]{2,1,0:T(8,128)(2,1)}, u32[]{:S(2)}, u32[]{:S(2)}) collective-permute-start(bf16[32,32,256]{2,1,0:T(8,128)(2,1)} %get-tuple-element.176), channel_id=1, source_target_pairs={{0,7},{1,6},{2,5},{3,4},{4,3},{5,2},{6,1},{7,0},{8,15},{9,14},{10,... | collective-permute-start | bytes 1572872 | tf_op jit(solution)/shard_map/ppermute | solution.py:178
  301.0 33.5 %collective-permute-start.50 = (bf16[32,32,256]{2,1,0:T(8,128)(2,1)}, bf16[32,32,256]{2,1,0:T(8,128)(2,1)S(1)}, u32[]{:S(2)}, u32[]{:S(2)}) collective-permute-start(bf16[32,32,256]{2,1,0:T(8,128)(2,1)} %get-tuple-element.208), channel_id=1, source_target_pairs={{0,4},{1,5},{2,6},{3,7},{4,0},{5,1},{6,2},{7,3},{8,12},{9,13},{10,... | collective-permute-start | bytes 1572872 | tf_op jit(solution)/shard_map/ppermute | solution.py:178
  301.9 32.6 %collective-permute-start.51 = (bf16[32,32,256]{2,1,0:T(8,128)(2,1)}, bf16[32,32,256]{2,1,0:T(8,128)(2,1)S(1)}, u32[]{:S(2)}, u32[]{:S(2)}) collective-permute-start(bf16[32,32,256]{2,1,0:T(8,128)(2,1)} %get-tuple-element.209), channel_id=1, source_target_pairs={{0,6},{1,7},{2,4},{3,5},{4,2},{5,3},{6,0},{7,1},{8,14},{9,15},{10,... | collective-permute-start | bytes 1572872 | tf_op jit(solution)/shard_map/ppermute | solution.py:178
  313.1 32.7 %collective-permute-start.53 = (bf16[32,32,256]{2,1,0:T(8,128)(2,1)}, bf16[32,32,256]{2,1,0:T(8,128)(2,1)S(1)}, u32[]{:S(2)}, u32[]{:S(2)}) collective-permute-start(bf16[32,32,256]{2,1,0:T(8,128)(2,1)} %get-tuple-element.211), channel_id=1, source_target_pairs={{0,5},{1,4},{2,7},{3,6},{4,1},{5,0},{6,3},{7,2},{8,13},{9,12},{10,... | collective-permute-start | bytes 1572872 | tf_op jit(solution)/shard_map/ppermute | solution.py:178
  323.8 32.8 %collective-permute-start.54 = (bf16[32,32,256]{2,1,0:T(8,128)(2,1)}, bf16[32,32,256]{2,1,0:T(8,128)(2,1)S(1)}, u32[]{:S(2)}, u32[]{:S(2)}) collective-permute-start(bf16[32,32,256]{2,1,0:T(8,128)(2,1)} %get-tuple-element.212), channel_id=1, source_target_pairs={{0,7},{1,6},{2,5},{3,4},{4,3},{5,2},{6,1},{7,0},{8,15},{9,14},{10,... | collective-permute-start | bytes 1572872 | tf_op jit(solution)/shard_map/ppermute | solution.py:178
  334.5 34.3 %collective-permute-start.42 = (bf16[32,32,256]{2,1,0:T(8,128)(2,1)}, bf16[32,32,256]{2,1,0:T(8,128)(2,1)S(1)}, u32[]{:S(2)}, u32[]{:S(2)}) collective-permute-start(bf16[32,32,256]{2,1,0:T(8,128)(2,1)} %get-tuple-element.190), channel_id=1, source_target_pairs={{0,2},{1,3},{2,0},{3,1},{4,6},{5,7},{6,4},{7,5},{8,10},{9,11},{10,... | collective-permute-start | bytes 1572872 | tf_op jit(solution)/shard_map/ppermute | solution.py:178
  343.8 35.6 %collective-permute-start.43 = (bf16[32,32,256]{2,1,0:T(8,128)(2,1)}, bf16[32,32,256]{2,1,0:T(8,128)(2,1)S(1)}, u32[]{:S(2)}, u32[]{:S(2)}) collective-permute-start(bf16[32,32,256]{2,1,0:T(8,128)(2,1)} %get-tuple-element.191), channel_id=1, source_target_pairs={{0,4},{1,5},{2,6},{3,7},{4,0},{5,1},{6,2},{7,3},{8,12},{9,13},{10,... | collective-permute-start | bytes 1572872 | tf_op jit(solution)/shard_map/ppermute | solution.py:178
  345.8 43.2 %collective-permute-start.44 = (bf16[32,32,256]{2,1,0:T(8,128)(2,1)}, bf16[32,32,256]{2,1,0:T(8,128)(2,1)}, u32[]{:S(2)}, u32[]{:S(2)}) collective-permute-start(bf16[32,32,256]{2,1,0:T(8,128)(2,1)} %get-tuple-element.192), channel_id=1, source_target_pairs={{0,6},{1,7},{2,4},{3,5},{4,2},{5,3},{6,0},{7,1},{8,14},{9,15},{10,... | collective-permute-start | bytes 1572872 | tf_op jit(solution)/shard_map/ppermute | solution.py:178
  368.8 32.9 %collective-permute-start.47 = (bf16[32,32,256]{2,1,0:T(8,128)(2,1)}, bf16[32,32,256]{2,1,0:T(8,128)(2,1)}, u32[]{:S(2)}, u32[]{:S(2)}) collective-permute-start(bf16[32,32,256]{2,1,0:T(8,128)(2,1)} %get-tuple-element.195), channel_id=1, source_target_pairs={{0,7},{1,6},{2,5},{3,4},{4,3},{5,2},{6,1},{7,0},{8,15},{9,14},{10,... | collective-permute-start | bytes 1572872 | tf_op jit(solution)/shard_map/ppermute | solution.py:178
  (70 other events, 1553.0 us)
Sparse Core Ops, SparseCore 0:
  239.3 145.2 reduce-scatter.1
where the time goes:
time: 421 us; the launch traced here: 420 us
  waiting for transfers between devices  192 us (46%)
  Pallas kernels  133 us (32%)
  starting transfers between devices  74.6 us (18%)
  between operations  14.6 us (3%)
  local copies, waits for them, and re-layouts  5.49 us (1%)
    ppermute x56, waiting for transfers between devices, exchange(): lax.ppermute(sends[n], 'seq', [(r, r ^ moves[n]) for r in range(ranks)])  192 us
    ppermute x56, starting transfers between devices, exchange(): lax.ppermute(sends[n], 'seq', [(r, r ^ moves[n]) for r in range(ranks)])  74.5 us
    pallas_call x4, Pallas kernels, right_both(): pl.pallas_call(functools.partial(right_kernel, ranks), out_shape=[buffer]...  60.2 us
    pallas_call x4, Pallas kernels, left_back(): pl.pallas_call(functools.partial(left_back_kernel, ranks, terms), out_sha...  39.6 us
    pallas_call x4, Pallas kernels, left_forward(): pl.pallas_call(functools.partial(left_forward_kernel, ranks), out_shape=[...  33.2 us
  transfers between devices with their start and end apart: 57, of which 26 were waited for; matrix products, arithmetic and copies ran while one was open for 0% of the time, Pallas kernels for 27%

commit v1 on v0

--- a/solution.py
+++ b/solution.py
@@ -265,20 +265,28 @@
     left_tokens, right_tokens, back_tokens = {}, {}, {}
     terms, outputs = None, []
 
-    def do_left(q):
-        after = [left_tokens[q - 1]] if q else []
+    parts = {}
+    for q in range(chunks):
+        *parts[q], left_tokens[q] = left_forward(q, [left_tokens[q - 1]] if q else [])
+
+    def send_left(q):
+        sends = parts[q]
+        after = []
+        if q == 1:
+            after.append(left_tokens[chunks - 1])
         if q >= 2:
             after.append(right_tokens[q - 2])
-        *sends, left_tokens[q] = left_forward(q, after)
+        if after:
+            sends[1 + EARLY :] = gate(sends[1 + EARLY :], after)
         received[q] = exchange(sends)
 
     for q in range(min(2, chunks)):
-        do_left(q)
+        send_left(q)
     for q in range(chunks):
         after = [right_tokens[q - 1]] if q else []
         *sent[q], terms, right_tokens[q] = right_both(q, received[q], terms, after)
         if q + 2 < chunks:
-            do_left(q + 2)
+            send_left(q + 2)
 
     def back_step(q):
         last = [reduced] if q == chunks - 1 else []
@@ -290,7 +298,12 @@
             after.append(right_tokens[chunks - 1])
         if q >= 2:
             after.append(back_tokens[q - 2])
-        returned[q] = exchange(sent[q][:1] + gate(sent[q][1:], after) if after else sent[q])
+        sends = list(sent[q])
+        if q == 0 and chunks > 2:
+            sends[1 : 1 + EARLY] = gate(sends[1 : 1 + EARLY], [right_tokens[chunks - 2]])
+        if after:
+            sends[1:] = gate(sends[1:], after)
+        returned[q] = exchange(sends)
         if q == 0:
             (terms,) = gate([terms], returned[0][1 : 1 + EARLY])
             reduced = lax.psum_scatter(terms, "dp", scatter_dimension=0, tiled=True)

time: 421 us -> 407 us (0.967)
  starting transfers between devices: 74.6 us -> 60.7 us
    ppermute x56, starting transfers between devices: 74.5 us -> 60.6 us  [exchange(): lax.ppermute(sends[n], 'seq', [(r, r ^ moves[n]) for r in range(ranks)])]
  transfers between devices with their start and end apart: 57 -> 57, of which waited for: 26 -> 24; matrix products, arithmetic and copies ran while one was open for 0% -> 0% of each run, Pallas kernels for 27% -> 28%
where the time goes in v1:
time: 407 us; the launch traced here: 404 us
  waiting for transfers between devices  189 us (46%)
  Pallas kernels  133 us (33%)
  starting transfers between devices  60.7 us (15%)
  between operations  14.5 us (4%)
  local copies, waits for them, and re-layouts  7.02 us (2%)
    ppermute x56, waiting for transfers between devices, exchange(): lax.ppermute(sends[n], 'seq', [(r, r ^ moves[n]) for r in range(ranks)])  189 us
    ppermute x56, starting transfers between devices, exchange(): lax.ppermute(sends[n], 'seq', [(r, r ^ moves[n]) for r in range(ranks)])  60.6 us
    pallas_call x4, Pallas kernels, right_both(): pl.pallas_call(functools.partial(right_kernel, ranks), out_shape=[buffer]...  60 us
    pallas_call x4, Pallas kernels, left_back(): pl.pallas_call(functools.partial(left_back_kernel, ranks, terms), out_sha...  39.6 us
    pallas_call x4, Pallas kernels, left_forward(): pl.pallas_call(functools.partial(left_forward_kernel, ranks), out_shape=[...  33.2 us
  transfers between devices with their start and end apart: 57, of which 24 were waited for; matrix products, arithmetic and copies ran while one was open for 0% of the time, Pallas kernels for 28%

profile of v1, /device:TPU:0, one launch (start us, length us, event | category | flops | bytes accessed | tf_op | source)
XLA Modules:
  0.0 404.4 jit_solution(15415519083020605228)
XLA Ops:
  7.2 8.3 %shard_map.76 = (bf16[32,32,256]{2,1,0:T(8,128)(2,1)}, bf16[32,32,256]{2,1,0:T(8,128)(2,1)}, bf16[32,32,256]{2,1,0:T(8,128)(2,1)}, bf16[32,32,256]{2,1,0:T(8,128...) custom-call(s32[1]{0:T(128)} %bitcast.rank_ref, ...), custom_call_target="tpu_custom_call" | custom-call | flops 1024 | bytes 1024 | tf_op jit(solution)/shard_map/pallas_call | solution.py:162
  23.2 8.2 %collective-permute-done.10.refs_1_ = bf16[32,32,256]{2,1,0:T(8,128)(2,1)S(1)} collective-permute-done((bf16[32,32,256]{2,1,0:T(8,128)(2,1)}, bf16[32,32,256]{2,1,0:T(8,128)(2,1)S(1)}, u32[]{:S(2)}, u32[]{:S(2)}) %collective-permute-start.10) | collective-permute-done | bytes 524320 | tf_op jit(solution)/shard_map/ppermute | solution.py:178
  31.9 8.3 %shard_map.77 = (bf16[32,32,256]{2,1,0:T(8,128)(2,1)}, bf16[32,32,256]{2,1,0:T(8,128)(2,1)}, bf16[32,32,256]{2,1,0:T(8,128)(2,1)}, bf16[32,32,256]{2,1,0:T(8,128...) custom-call(s32[1]{0:T(128)} %bitcast.rank_ref, ...), custom_call_target="tpu_custom_call" | custom-call | flops 1024 | bytes 1024 | tf_op jit(solution)/shard_map/pallas_call | solution.py:162
  40.1 8.2 %shard_map.78 = (bf16[32,32,256]{2,1,0:T(8,128)(2,1)}, bf16[32,32,256]{2,1,0:T(8,128)(2,1)}, bf16[32,32,256]{2,1,0:T(8,128)(2,1)}, bf16[32,32,256]{2,1,0:T(8,128...) custom-call(s32[1]{0:T(128)} %bitcast.rank_ref, ...), custom_call_target="tpu_custom_call" | custom-call | flops 1024 | bytes 1024 | tf_op jit(solution)/shard_map/pallas_call | solution.py:162
  56.0 10.2 %collective-permute-done.14.refs_5_ = bf16[32,32,256]{2,1,0:T(8,128)(2,1)S(1)} collective-permute-done((bf16[32,32,256]{2,1,0:T(8,128)(2,1)}, bf16[32,32,256]{2,1,0:T(8,128)(2,1)S(1)}, u32[]{:S(2)}, u32[]{:S(2)}) %collective-permute-start.14) | collective-permute-done | bytes 524320 | tf_op jit(solution)/shard_map/ppermute | solution.py:178
  67.1 8.4 %shard_map.79 = (bf16[32,32,256]{2,1,0:T(8,128)(2,1)}, bf16[32,32,256]{2,1,0:T(8,128)(2,1)}, bf16[32,32,256]{2,1,0:T(8,128)(2,1)}, bf16[32,32,256]{2,1,0:T(8,128...) custom-call(s32[1]{0:T(128)} %bitcast.rank_ref, ...), custom_call_target="tpu_custom_call" | custom-call | flops 1024 | bytes 1024 | tf_op jit(solution)/shard_map/pallas_call | solution.py:162
  79.0 9.7 %collective-permute-done.4.refs_2_ = bf16[32,32,256]{2,1,0:T(8,128)(2,1)S(1)} collective-permute-done((bf16[32,32,256]{2,1,0:T(8,128)(2,1)}, bf16[32,32,256]{2,1,0:T(8,128)(2,1)S(1)}, u32[]{:S(2)}, u32[]{:S(2)}) %collective-permute-start.4) | collective-permute-done | bytes 524320 | tf_op jit(solution)/shard_map/ppermute | solution.py:178
  89.3 9.7 %collective-permute-done.21.refs_1_ = bf16[32,32,256]{2,1,0:T(8,128)(2,1)S(1)} collective-permute-done((bf16[32,32,256]{2,1,0:T(8,128)(2,1)}, bf16[32,32,256]{2,1,0:T(8,128)(2,1)S(1)}, u32[]{:S(2)}, u32[]{:S(2)}) %collective-permute-start.21) | collective-permute-done | bytes 524320 | tf_op jit(solution)/shard_map/ppermute | solution.py:178
  99.0 15.2 %shard_map.81 = (bf16[32,32,256]{2,1,0:T(8,128)(2,1)}, bf16[32,32,256]{2,1,0:T(8,128)(2,1)}, bf16[32,32,256]{2,1,0:T(8,128)(2,1)}, bf16[32,32,256]{2,1,0:T(8,128...) custom-call(s32[1]{0:T(128)} %bitcast.rank_ref, ...), custom_call_target="tpu_custom_call" | custom-call | flops 1024 | bytes 1024 | tf_op jit(solution)/shard_map/pallas_call | solution.py:185
  117.6 16.0 %collective-permute-done.7.refs_5_ = bf16[32,32,256]{2,1,0:T(8,128)(2,1)S(1)} collective-permute-done((bf16[32,32,256]{2,1,0:T(8,128)(2,1)}, bf16[32,32,256]{2,1,0:T(8,128)(2,1)S(1)}, u32[]{:S(2)}, u32[]{:S(2)}) %collective-permute-start.7) | collective-permute-done | bytes 524320 | tf_op jit(solution)/shard_map/ppermute | solution.py:178
  136.6 14.9 %shard_map.82 = (bf16[32,32,256]{2,1,0:T(8,128)(2,1)}, bf16[32,32,256]{2,1,0:T(8,128)(2,1)}, bf16[32,32,256]{2,1,0:T(8,128)(2,1)}, bf16[32,32,256]{2,1,0:T(8,128...) custom-call(s32[1]{0:T(128)} %bitcast.rank_ref, ...), custom_call_target="tpu_custom_call", output_to_operand_aliasing={{8}: (11, {})} | custom-call | flops 1024 | bytes 1024 | tf_op jit(solution)/shard_map/pallas_call | solution.py:185
  158.3 14.9 %shard_map.85 = (bf16[32,32,256]{2,1,0:T(8,128)(2,1)}, bf16[32,32,256]{2,1,0:T(8,128)(2,1)}, bf16[32,32,256]{2,1,0:T(8,128)(2,1)}, bf16[32,32,256]{2,1,0:T(8,128...) custom-call(s32[1]{0:T(128)} %bitcast.rank_ref, ...), custom_call_target="tpu_custom_call", output_to_operand_aliasing={{8}: (11, {})} | custom-call | flops 1024 | bytes 1024 | tf_op jit(solution)/shard_map/pallas_call | solution.py:185
  174.6 4.7 %collective-permute-done.1.refs_2_ = bf16[32,32,256]{2,1,0:T(8,128)(2,1)S(1)} collective-permute-done((bf16[32,32,256]{2,1,0:T(8,128)(2,1)}, bf16[32,32,256]{2,1,0:T(8,128)(2,1)S(1)}, u32[]{:S(2)}, u32[]{:S(2)}) %collective-permute-start.1) | collective-permute-done | bytes 524320 | tf_op jit(solution)/shard_map/ppermute | solution.py:178
  180.8 7.4 %collective-permute-done.17.refs_4_ = bf16[32,32,256]{2,1,0:T(8,128)(2,1)S(1)} collective-permute-done((bf16[32,32,256]{2,1,0:T(8,128)(2,1)}, bf16[32,32,256]{2,1,0:T(8,128)(2,1)S(1)}, u32[]{:S(2)}, u32[]{:S(2)}) %collective-permute-start.17) | collective-permute-done | bytes 524320 | tf_op jit(solution)/shard_map/ppermute | solution.py:178
  191.0 10.3 %collective-permute-done.18.refs_5_ = bf16[32,32,256]{2,1,0:T(8,128)(2,1)} collective-permute-done((bf16[32,32,256]{2,1,0:T(8,128)(2,1)}, bf16[32,32,256]{2,1,0:T(8,128)(2,1)}, u32[]{:S(2)}, u32[]{:S(2)}) %collective-permute-start.18) | collective-permute-done | bytes 524320 | tf_op jit(solution)/shard_map/ppermute | solution.py:178
  202.1 15.0 %shard_map.86 = (bf16[32,32,256]{2,1,0:T(8,128)(2,1)}, bf16[32,32,256]{2,1,0:T(8,128)(2,1)}, bf16[32,32,256]{2,1,0:T(8,128)(2,1)}, bf16[32,32,256]{2,1,0:T(8,128...) custom-call(s32[1]{0:T(128)} %bitcast.rank_ref, ...), custom_call_target="tpu_custom_call", output_to_operand_aliasing={{8}: (11, {})} | custom-call | flops 1024 | bytes 1024 | tf_op jit(solution)/shard_map/pallas_call | solution.py:185
  217.1 6.2 %collective-permute-done.36.refs_2_ = bf16[32,32,256]{2,1,0:T(8,128)(2,1)S(1)} collective-permute-done((bf16[32,32,256]{2,1,0:T(8,128)(2,1)}, bf16[32,32,256]{2,1,0:T(8,128)(2,1)S(1)}, u32[]{:S(2)}, u32[]{:S(2)}) %collective-permute-start.36) | collective-permute-done | bytes 524320 | tf_op jit(solution)/shard_map/ppermute | solution.py:178
  230.0 9.4 %collective-permute-done.38.refs_4_ = bf16[32,32,256]{2,1,0:T(8,128)(2,1)S(1)} collective-permute-done((bf16[32,32,256]{2,1,0:T(8,128)(2,1)S(1)}, bf16[32,32,256]{2,1,0:T(8,128)(2,1)S(1)}, u32[]{:S(2)}, u32[]{:S(2)}) %collective-permute-start.38) | collective-permute-done | bytes 524320 | tf_op jit(solution)/shard_map/ppermute | solution.py:178
  241.2 9.0 %collective-permute-done.39.refs_5_ = bf16[32,32,256]{2,1,0:T(8,128)(2,1)S(1)} collective-permute-done((bf16[32,32,256]{2,1,0:T(8,128)(2,1)S(1)}, bf16[32,32,256]{2,1,0:T(8,128)(2,1)S(1)}, u32[]{:S(2)}, u32[]{:S(2)}) %collective-permute-start.39) | collective-permute-done | bytes 524320 | tf_op jit(solution)/shard_map/ppermute | solution.py:178
  254.3 8.0 %collective-permute-done.28.refs_1_ = bf16[32,32,256]{2,1,0:T(8,128)(2,1)S(1)} collective-permute-done((bf16[32,32,256]{2,1,0:T(8,128)(2,1)}, bf16[32,32,256]{2,1,0:T(8,128)(2,1)S(1)}, u32[]{:S(2)}, u32[]{:S(2)}) %collective-permute-start.28) | collective-permute-done | bytes 524320 | tf_op jit(solution)/shard_map/ppermute | solution.py:178
  263.2 9.5 %collective-permute-done.29.refs_2_ = bf16[32,32,256]{2,1,0:T(8,128)(2,1)S(1)} collective-permute-done((bf16[32,32,256]{2,1,0:T(8,128)(2,1)}, bf16[32,32,256]{2,1,0:T(8,128)(2,1)S(1)}, u32[]{:S(2)}, u32[]{:S(2)}) %collective-permute-start.29) | collective-permute-done | bytes 524320 | tf_op jit(solution)/shard_map/ppermute | solution.py:178
  272.7 9.5 %shard_map.89 = (bf16[1,8192,512]{2,1,0:T(8,128)(2,1)}, bf16[1,8192,512]{2,1,0:T(8,128)(2,1)}, f32[2048,512]{1,0:T(8,128)}, f32[8,128]{1,0:T(8,128)}) custom-call(s32[1]{0:T(128)} %bitcast.rank_ref, bf16[1,8192,512]{2,1,0:T(8,128)(2,1)} %values_ref.15, bf16[1,8192,512]{2,1,0:T(8,128)(2,1)} %cotangent_ref.15, bf16[32,256,256]{2,1,0:T(8,128)(2,1)} %left_ref.15, ...), custom_call_target="tpu_custom_call" | custom-call | flops 1024 | bytes 1024 | tf_op jit(solution)/shard_map/pallas_call | solution.py:237
  288.2 8.9 %collective-permute-done.33.refs_6_ = bf16[32,32,256]{2,1,0:T(8,128)(2,1)} collective-permute-done((bf16[32,32,256]{2,1,0:T(8,128)(2,1)}, bf16[32,32,256]{2,1,0:T(8,128)(2,1)}, u32[]{:S(2)}, u32[]{:S(2)}) %collective-permute-start.33) | collective-permute-done | bytes 524320 | tf_op jit(solution)/shard_map/ppermute | solution.py:178
  299.5 9.4 %shard_map.90 = (bf16[1,8192,512]{2,1,0:T(8,128)(2,1)}, bf16[1,8192,512]{2,1,0:T(8,128)(2,1)}, f32[2048,512]{1,0:T(8,128)}, f32[8,128]{1,0:T(8,128)}) custom-call(s32[1]{0:T(128)} %bitcast.rank_ref, bf16[1,8192,512]{2,1,0:T(8,128)(2,1)} %values_ref.15, ...), custom_call_target="tpu_custom_call", output_to_operand_aliasing={{0}: (12, {}), {1}: (13, {}), {2}: (14, {})} | custom-call | flops 1024 | bytes 1024 | tf_op jit(solution)/shard_map/pallas_call | solution.py:237
  310.9 7.1 %collective-permute-done.51.refs_3_ = bf16[32,32,256]{2,1,0:T(8,128)(2,1)S(1)} collective-permute-done((bf16[32,32,256]{2,1,0:T(8,128)(2,1)}, bf16[32,32,256]{2,1,0:T(8,128)(2,1)S(1)}, u32[]{:S(2)}, u32[]{:S(2)}) %collective-permute-start.51) | collective-permute-done | bytes 524320 | tf_op jit(solution)/shard_map/ppermute | solution.py:178
  320.1 9.4 %collective-permute-done.52.refs_4_ = bf16[32,32,256]{2,1,0:T(8,128)(2,1)S(1)} collective-permute-done((bf16[32,32,256]{2,1,0:T(8,128)(2,1)}, bf16[32,32,256]{2,1,0:T(8,128)(2,1)S(1)}, u32[]{:S(2)}, u32[]{:S(2)}) %collective-permute-start.52) | collective-permute-done | bytes 524320 | tf_op jit(solution)/shard_map/ppermute | solution.py:178
  332.4 9.6 %collective-permute-done.54.refs_6_ = bf16[32,32,256]{2,1,0:T(8,128)(2,1)S(1)} collective-permute-done((bf16[32,32,256]{2,1,0:T(8,128)(2,1)}, bf16[32,32,256]{2,1,0:T(8,128)(2,1)S(1)}, u32[]{:S(2)}, u32[]{:S(2)}) %collective-permute-start.54) | collective-permute-done | bytes 524320 | tf_op jit(solution)/shard_map/ppermute | solution.py:178
  343.5 8.8 %collective-permute-done.42.refs_1_ = bf16[32,32,256]{2,1,0:T(8,128)(2,1)S(1)} collective-permute-done((bf16[32,32,256]{2,1,0:T(8,128)(2,1)}, bf16[32,32,256]{2,1,0:T(8,128)(2,1)S(1)}, u32[]{:S(2)}, u32[]{:S(2)}) %collective-permute-start.42) | collective-permute-done | bytes 524320 | tf_op jit(solution)/shard_map/ppermute | solution.py:178
  354.1 9.4 %shard_map.94 = (bf16[1,8192,512]{2,1,0:T(8,128)(2,1)}, bf16[1,8192,512]{2,1,0:T(8,128)(2,1)}, f32[2048,512]{1,0:T(8,128)}, f32[8,128]{1,0:T(8,128)}) custom-call(s32[1]{0:T(128)} %bitcast.rank_ref, bf16[1,8192,512]{2,1,0:T(8,128)(2,1)} %values_ref.15, ...), custom_call_target="tpu_custom_call", output_to_operand_aliasing={{0}: (12, {}), {1}: (13, {}), {2}: (14, {})} | custom-call | flops 1024 | bytes 1024 | tf_op jit(solution)/shard_map/pallas_call | solution.py:237
  363.5 11.1 %collective-permute-done.45.refs_4_ = bf16[32,32,256]{2,1,0:T(8,128)(2,1)} collective-permute-done((bf16[32,32,256]{2,1,0:T(8,128)(2,1)}, bf16[32,32,256]{2,1,0:T(8,128)(2,1)}, u32[]{:S(2)}, u32[]{:S(2)}) %collective-permute-start.45) | collective-permute-done | bytes 524320 | tf_op jit(solution)/shard_map/ppermute | solution.py:178
  375.6 10.7 %collective-permute-done.47.refs_6_ = bf16[32,32,256]{2,1,0:T(8,128)(2,1)} collective-permute-done((bf16[32,32,256]{2,1,0:T(8,128)(2,1)}, bf16[32,32,256]{2,1,0:T(8,128)(2,1)}, u32[]{:S(2)}, u32[]{:S(2)}) %collective-permute-start.47) | collective-permute-done | bytes 524320 | tf_op jit(solution)/shard_map/ppermute | solution.py:178
  386.3 11.2 %shard_map.95 = (bf16[1,8192,512]{2,1,0:T(8,128)(2,1)}, bf16[1,8192,512]{2,1,0:T(8,128)(2,1)}, f32[2048,512]{1,0:T(8,128)}, f32[8,128]{1,0:T(8,128)}) custom-call(s32[1]{0:T(128)} %bitcast.rank_ref, bf16[1,8192,512]{2,1,0:T(8,128)(2,1)} %values_ref.15, ...), custom_call_target="tpu_custom_call", output_to_operand_aliasing={{0}: (13, {}), {1}: (14, {}), {2}: (15, {})} | custom-call | flops 1024 | bytes 1024 | tf_op jit(solution)/shard_map/pallas_call | solution.py:237
  (191 shorter events, 73.0 us)
Async XLA Ops:
  7.2 379.1 %reduce-scatter.2.cloned.1.call-start = ((), (), s32[]{:S(2)}) async-start(), calls=%async_computation.1 | async-start | bytes 10485760 | tf_op jit(solution)/shard_map/reduce_scatter | solution.py:309
  20.0 33.6 %collective-permute-start.13 = (bf16[32,32,256]{2,1,0:T(8,128)(2,1)}, bf16[32,32,256]{2,1,0:T(8,128)(2,1)S(1)}, u32[]{:S(2)}, u32[]{:S(2)}) collective-permute-start(bf16[32,32,256]{2,1,0:T(8,128)(2,1)} %get-tuple-element.157), channel_id=1, source_target_pairs={{0,3},{1,2},{2,1},{3,0},{4,7},{5,6},{6,5},{7,4},{8,11},{9,10},{10,... | collective-permute-start | bytes 1572872 | tf_op jit(solution)/shard_map/ppermute | solution.py:178
  20.6 45.7 %collective-permute-start.14 = (bf16[32,32,256]{2,1,0:T(8,128)(2,1)}, bf16[32,32,256]{2,1,0:T(8,128)(2,1)S(1)}, u32[]{:S(2)}, u32[]{:S(2)}) collective-permute-start(bf16[32,32,256]{2,1,0:T(8,128)(2,1)} %get-tuple-element.158), channel_id=1, source_target_pairs={{0,5},{1,4},{2,7},{3,6},{4,1},{5,0},{6,3},{7,2},{8,13},{9,12},{10,... | collective-permute-start | bytes 1572872 | tf_op jit(solution)/shard_map/ppermute | solution.py:178
  31.4 34.8 %collective-permute-start.15 = (bf16[32,32,256]{2,1,0:T(8,128)(2,1)}, bf16[32,32,256]{2,1,0:T(8,128)(2,1)S(1)}, u32[]{:S(2)}, u32[]{:S(2)}) collective-permute-start(bf16[32,32,256]{2,1,0:T(8,128)(2,1)} %get-tuple-element.159), channel_id=1, source_target_pairs={{0,7},{1,6},{2,5},{3,4},{4,3},{5,2},{6,1},{7,0},{8,15},{9,14},{10,... | collective-permute-start | bytes 1572872 | tf_op jit(solution)/shard_map/ppermute | solution.py:178
  54.4 34.3 %collective-permute-start.4 = (bf16[32,32,256]{2,1,0:T(8,128)(2,1)}, bf16[32,32,256]{2,1,0:T(8,128)(2,1)S(1)}, u32[]{:S(2)}, u32[]{:S(2)}) collective-permute-start(bf16[32,32,256]{2,1,0:T(8,128)(2,1)} %get-tuple-element.142), channel_id=1, source_target_pairs={{0,4},{1,5},{2,6},{3,7},{4,0},{5,1},{6,2},{7,3},{8,12},{9,13},{10,... | collective-permute-start | bytes 1572872 | tf_op jit(solution)/shard_map/ppermute | solution.py:178
  67.1 31.9 %collective-permute-start.21 = (bf16[32,32,256]{2,1,0:T(8,128)(2,1)}, bf16[32,32,256]{2,1,0:T(8,128)(2,1)S(1)}, u32[]{:S(2)}, u32[]{:S(2)}) collective-permute-start(bf16[32,32,256]{2,1,0:T(8,128)(2,1)} %get-tuple-element.169), channel_id=1, source_target_pairs={{0,2},{1,3},{2,0},{3,1},{4,6},{5,7},{6,4},{7,5},{8,10},{9,11},{10,... | collective-permute-start | bytes 1572872 | tf_op jit(solution)/shard_map/ppermute | solution.py:178
  75.6 38.7 %collective-permute-start.22 = (bf16[32,32,256]{2,1,0:T(8,128)(2,1)}, bf16[32,32,256]{2,1,0:T(8,128)(2,1)S(1)}, u32[]{:S(2)}, u32[]{:S(2)}) collective-permute-start(bf16[32,32,256]{2,1,0:T(8,128)(2,1)} %get-tuple-element.170), channel_id=1, source_target_pairs={{0,4},{1,5},{2,6},{3,7},{4,0},{5,1},{6,2},{7,3},{8,12},{9,13},{10,... | collective-permute-start | bytes 1572872 | tf_op jit(solution)/shard_map/ppermute | solution.py:178
  78.1 39.3 %collective-permute-start.6 = (bf16[32,32,256]{2,1,0:T(8,128)(2,1)}, bf16[32,32,256]{2,1,0:T(8,128)(2,1)S(1)}, u32[]{:S(2)}, u32[]{:S(2)}) collective-permute-start(bf16[32,32,256]{2,1,0:T(8,128)(2,1)} %get-tuple-element.149), channel_id=1, source_target_pairs={{0,3},{1,2},{2,1},{3,0},{4,7},{5,6},{6,5},{7,4},{8,11},{9,10},{10,... | collective-permute-start | bytes 1572872 | tf_op jit(solution)/shard_map/ppermute | solution.py:178
  88.7 44.9 %collective-permute-start.7 = (bf16[32,32,256]{2,1,0:T(8,128)(2,1)}, bf16[32,32,256]{2,1,0:T(8,128)(2,1)S(1)}, u32[]{:S(2)}, u32[]{:S(2)}) collective-permute-start(bf16[32,32,256]{2,1,0:T(8,128)(2,1)} %get-tuple-element.150), channel_id=1, source_target_pairs={{0,5},{1,4},{2,7},{3,6},{4,1},{5,0},{6,3},{7,2},{8,13},{9,12},{10,... | collective-permute-start | bytes 1572872 | tf_op jit(solution)/shard_map/ppermute | solution.py:178
  89.3 47.2 %collective-permute-start.8 = (bf16[32,32,256]{2,1,0:T(8,128)(2,1)}, bf16[32,32,256]{2,1,0:T(8,128)(2,1)}, u32[]{:S(2)}, u32[]{:S(2)}) collective-permute-start(bf16[32,32,256]{2,1,0:T(8,128)(2,1)} %get-tuple-element.151), channel_id=1, source_target_pairs={{0,7},{1,6},{2,5},{3,4},{4,3},{5,2},{6,1},{7,0},{8,15},{9,14},{10,... | collective-permute-start | bytes 1572872 | tf_op jit(solution)/shard_map/ppermute | solution.py:178
  99.0 37.5 %collective-permute-start.9 = (bf16[32,32,256]{2,1,0:T(8,128)(2,1)}, bf16[32,32,256]{2,1,0:T(8,128)(2,1)}, u32[]{:S(2)}, u32[]{:S(2)}) collective-permute-start(bf16[32,32,256]{2,1,0:T(8,128)(2,1)} %get-tuple-element.152), channel_id=1, source_target_pairs={{0,1},{1,0},{2,3},{3,2},{4,5},{5,4},{6,7},{7,6},{8,9},{9,8},{10,11... | collective-permute-start | bytes 1572872 | tf_op jit(solution)/shard_map/ppermute | solution.py:178
  114.3 37.2 %collective-permute-start.23 = (bf16[32,32,256]{2,1,0:T(8,128)(2,1)}, bf16[32,32,256]{2,1,0:T(8,128)(2,1)S(1)}, u32[]{:S(2)}, u32[]{:S(2)}) collective-permute-start(bf16[32,32,256]{2,1,0:T(8,128)(2,1)} %get-tuple-element.171), channel_id=1, source_target_pairs={{0,6},{1,7},{2,4},{3,5},{4,2},{5,3},{6,0},{7,1},{8,14},{9,15},{10,... | collective-permute-start | bytes 1572872 | tf_op jit(solution)/shard_map/ppermute | solution.py:178
  117.4 35.5 %collective-permute-start.24 = (bf16[32,32,256]{2,1,0:T(8,128)(2,1)}, bf16[32,32,256]{2,1,0:T(8,128)(2,1)S(1)}, u32[]{:S(2)}, u32[]{:S(2)}) collective-permute-start(bf16[32,32,256]{2,1,0:T(8,128)(2,1)} %get-tuple-element.176), channel_id=1, source_target_pairs={{0,3},{1,2},{2,1},{3,0},{4,7},{5,6},{6,5},{7,4},{8,11},{9,10},{10,... | collective-permute-start | bytes 1572872 | tf_op jit(solution)/shard_map/ppermute | solution.py:178
  155.1 33.1 %collective-permute-start.17 = (bf16[32,32,256]{2,1,0:T(8,128)(2,1)}, bf16[32,32,256]{2,1,0:T(8,128)(2,1)S(1)}, u32[]{:S(2)}, u32[]{:S(2)}) collective-permute-start(bf16[32,32,256]{2,1,0:T(8,128)(2,1)} %get-tuple-element.164), channel_id=1, source_target_pairs={{0,3},{1,2},{2,1},{3,0},{4,7},{5,6},{6,5},{7,4},{8,11},{9,10},{10,... | collective-permute-start | bytes 1572872 | tf_op jit(solution)/shard_map/ppermute | solution.py:178
  158.1 43.2 %collective-permute-start.18 = (bf16[32,32,256]{2,1,0:T(8,128)(2,1)}, bf16[32,32,256]{2,1,0:T(8,128)(2,1)}, u32[]{:S(2)}, u32[]{:S(2)}) collective-permute-start(bf16[32,32,256]{2,1,0:T(8,128)(2,1)} %get-tuple-element.165), channel_id=1, source_target_pairs={{0,5},{1,4},{2,7},{3,6},{4,1},{5,0},{6,3},{7,2},{8,13},{9,12},{10,... | collective-permute-start | bytes 1572872 | tf_op jit(solution)/shard_map/ppermute | solution.py:178
  179.3 37.8 %collective-permute-start.35 = (bf16[32,32,256]{2,1,0:T(8,128)(2,1)}, bf16[32,32,256]{2,1,0:T(8,128)(2,1)S(1)}, u32[]{:S(2)}, u32[]{:S(2)}) collective-permute-start(bf16[32,32,256]{2,1,0:T(8,128)(2,1)} %get-tuple-element.211), channel_id=1, source_target_pairs={{0,2},{1,3},{2,0},{3,1},{4,6},{5,7},{6,4},{7,5},{8,10},{9,11},{10,... | collective-permute-start | bytes 1572872 | tf_op jit(solution)/shard_map/ppermute | solution.py:178
  188.9 34.4 %collective-permute-start.36 = (bf16[32,32,256]{2,1,0:T(8,128)(2,1)}, bf16[32,32,256]{2,1,0:T(8,128)(2,1)S(1)}, u32[]{:S(2)}, u32[]{:S(2)}) collective-permute-start(bf16[32,32,256]{2,1,0:T(8,128)(2,1)} %get-tuple-element.212), channel_id=1, source_target_pairs={{0,4},{1,5},{2,6},{3,7},{4,0},{5,1},{6,2},{7,3},{8,12},{9,13},{10,... | collective-permute-start | bytes 1572872 | tf_op jit(solution)/shard_map/ppermute | solution.py:178
  228.7 33.6 %collective-permute-start.28 = (bf16[32,32,256]{2,1,0:T(8,128)(2,1)}, bf16[32,32,256]{2,1,0:T(8,128)(2,1)S(1)}, u32[]{:S(2)}, u32[]{:S(2)}) collective-permute-start(bf16[32,32,256]{2,1,0:T(8,128)(2,1)} %get-tuple-element.200), channel_id=1, source_target_pairs={{0,2},{1,3},{2,0},{3,1},{4,6},{5,7},{6,4},{7,5},{8,10},{9,11},{10,... | collective-permute-start | bytes 1572872 | tf_op jit(solution)/shard_map/ppermute | solution.py:178
  239.4 33.3 %collective-permute-start.29 = (bf16[32,32,256]{2,1,0:T(8,128)(2,1)}, bf16[32,32,256]{2,1,0:T(8,128)(2,1)S(1)}, u32[]{:S(2)}, u32[]{:S(2)}) collective-permute-start(bf16[32,32,256]{2,1,0:T(8,128)(2,1)} %get-tuple-element.201), channel_id=1, source_target_pairs={{0,4},{1,5},{2,6},{3,7},{4,0},{5,1},{6,2},{7,3},{8,12},{9,13},{10,... | collective-permute-start | bytes 1572872 | tf_op jit(solution)/shard_map/ppermute | solution.py:178
  250.2 32.1 %collective-permute-start.30 = (bf16[32,32,256]{2,1,0:T(8,128)(2,1)}, bf16[32,32,256]{2,1,0:T(8,128)(2,1)S(1)}, u32[]{:S(2)}, u32[]{:S(2)}) collective-permute-start(bf16[32,32,256]{2,1,0:T(8,128)(2,1)} %get-tuple-element.202), channel_id=1, source_target_pairs={{0,6},{1,7},{2,4},{3,5},{4,2},{5,3},{6,0},{7,1},{8,14},{9,15},{10,... | collective-permute-start | bytes 1572872 | tf_op jit(solution)/shard_map/ppermute | solution.py:178
  251.9 32.7 %collective-permute-start.31 = (bf16[32,32,256]{2,1,0:T(8,128)(2,1)}, bf16[32,32,256]{2,1,0:T(8,128)(2,1)S(1)}, u32[]{:S(2)}, u32[]{:S(2)}) collective-permute-start(bf16[32,32,256]{2,1,0:T(8,128)(2,1)} %get-tuple-element.203), channel_id=1, source_target_pairs={{0,3},{1,2},{2,1},{3,0},{4,7},{5,6},{6,5},{7,4},{8,11},{9,10},{10,... | collective-permute-start | bytes 1572872 | tf_op jit(solution)/shard_map/ppermute | solution.py:178
  253.9 32.4 %collective-permute-start.32 = (bf16[32,32,256]{2,1,0:T(8,128)(2,1)}, bf16[32,32,256]{2,1,0:T(8,128)(2,1)S(1)}, u32[]{:S(2)}, u32[]{:S(2)}) collective-permute-start(bf16[32,32,256]{2,1,0:T(8,128)(2,1)} %get-tuple-element.204), channel_id=1, source_target_pairs={{0,5},{1,4},{2,7},{3,6},{4,1},{5,0},{6,3},{7,2},{8,13},{9,12},{10,... | collective-permute-start | bytes 1572872 | tf_op jit(solution)/shard_map/ppermute | solution.py:178
  262.3 34.8 %collective-permute-start.33 = (bf16[32,32,256]{2,1,0:T(8,128)(2,1)}, bf16[32,32,256]{2,1,0:T(8,128)(2,1)}, u32[]{:S(2)}, u32[]{:S(2)}) collective-permute-start(bf16[32,32,256]{2,1,0:T(8,128)(2,1)} %get-tuple-element.205), channel_id=1, source_target_pairs={{0,7},{1,6},{2,5},{3,4},{4,3},{5,2},{6,1},{7,0},{8,15},{9,14},{10,... | collective-permute-start | bytes 1572872 | tf_op jit(solution)/shard_map/ppermute | solution.py:178
  297.1 32.4 %collective-permute-start.52 = (bf16[32,32,256]{2,1,0:T(8,128)(2,1)}, bf16[32,32,256]{2,1,0:T(8,128)(2,1)S(1)}, u32[]{:S(2)}, u32[]{:S(2)}) collective-permute-start(bf16[32,32,256]{2,1,0:T(8,128)(2,1)} %get-tuple-element.242), channel_id=1, source_target_pairs={{0,3},{1,2},{2,1},{3,0},{4,7},{5,6},{6,5},{7,4},{8,11},{9,10},{10,... | collective-permute-start | bytes 1572872 | tf_op jit(solution)/shard_map/ppermute | solution.py:178
  309.0 33.0 %collective-permute-start.54 = (bf16[32,32,256]{2,1,0:T(8,128)(2,1)}, bf16[32,32,256]{2,1,0:T(8,128)(2,1)S(1)}, u32[]{:S(2)}, u32[]{:S(2)}) collective-permute-start(bf16[32,32,256]{2,1,0:T(8,128)(2,1)} %get-tuple-element.244), channel_id=1, source_target_pairs={{0,7},{1,6},{2,5},{3,4},{4,3},{5,2},{6,1},{7,0},{8,15},{9,14},{10,... | collective-permute-start | bytes 1572872 | tf_op jit(solution)/shard_map/ppermute | solution.py:178
  309.1 34.4 %collective-permute-start.55 = (bf16[32,32,256]{2,1,0:T(8,128)(2,1)}, bf16[32,32,256]{2,1,0:T(8,128)(2,1)S(1)}, u32[]{:S(2)}, u32[]{:S(2)}) collective-permute-start(bf16[32,32,256]{2,1,0:T(8,128)(2,1)} %get-tuple-element.245), channel_id=1, source_target_pairs={{0,1},{1,0},{2,3},{3,2},{4,5},{5,4},{6,7},{7,6},{8,9},{9,8},{10,11... | collective-permute-start | bytes 1572872 | tf_op jit(solution)/shard_map/ppermute | solution.py:178
  318.0 34.4 %collective-permute-start.42 = (bf16[32,32,256]{2,1,0:T(8,128)(2,1)}, bf16[32,32,256]{2,1,0:T(8,128)(2,1)S(1)}, u32[]{:S(2)}, u32[]{:S(2)}) collective-permute-start(bf16[32,32,256]{2,1,0:T(8,128)(2,1)} %get-tuple-element.222), channel_id=1, source_target_pairs={{0,2},{1,3},{2,0},{3,1},{4,6},{5,7},{6,4},{7,5},{8,10},{9,11},{10,... | collective-permute-start | bytes 1572872 | tf_op jit(solution)/shard_map/ppermute | solution.py:178
  331.3 32.2 %collective-permute-start.44 = (bf16[32,32,256]{2,1,0:T(8,128)(2,1)}, bf16[32,32,256]{2,1,0:T(8,128)(2,1)}, u32[]{:S(2)}, u32[]{:S(2)}) collective-permute-start(bf16[32,32,256]{2,1,0:T(8,128)(2,1)} %get-tuple-element.224), channel_id=1, source_target_pairs={{0,6},{1,7},{2,4},{3,5},{4,2},{5,3},{6,0},{7,1},{8,14},{9,15},{10,... | collective-permute-start | bytes 1572872 | tf_op jit(solution)/shard_map/ppermute | solution.py:178
  342.0 32.6 %collective-permute-start.45 = (bf16[32,32,256]{2,1,0:T(8,128)(2,1)}, bf16[32,32,256]{2,1,0:T(8,128)(2,1)}, u32[]{:S(2)}, u32[]{:S(2)}) collective-permute-start(bf16[32,32,256]{2,1,0:T(8,128)(2,1)} %get-tuple-element.225), channel_id=1, source_target_pairs={{0,3},{1,2},{2,1},{3,0},{4,7},{5,6},{6,5},{7,4},{8,11},{9,10},{10,... | collective-permute-start | bytes 1572872 | tf_op jit(solution)/shard_map/ppermute | solution.py:178
  343.5 32.1 %collective-permute-start.46 = (bf16[32,32,256]{2,1,0:T(8,128)(2,1)}, bf16[32,32,256]{2,1,0:T(8,128)(2,1)}, u32[]{:S(2)}, u32[]{:S(2)}) collective-permute-start(bf16[32,32,256]{2,1,0:T(8,128)(2,1)} %get-tuple-element.226), channel_id=1, source_target_pairs={{0,5},{1,4},{2,7},{3,6},{4,1},{5,0},{6,3},{7,2},{8,13},{9,12},{10,... | collective-permute-start | bytes 1572872 | tf_op jit(solution)/shard_map/ppermute | solution.py:178
  352.3 34.0 %collective-permute-start.47 = (bf16[32,32,256]{2,1,0:T(8,128)(2,1)}, bf16[32,32,256]{2,1,0:T(8,128)(2,1)}, u32[]{:S(2)}, u32[]{:S(2)}) collective-permute-start(bf16[32,32,256]{2,1,0:T(8,128)(2,1)} %get-tuple-element.227), channel_id=1, source_target_pairs={{0,7},{1,6},{2,5},{3,4},{4,3},{5,2},{6,1},{7,0},{8,15},{9,14},{10,... | collective-permute-start | bytes 1572872 | tf_op jit(solution)/shard_map/ppermute | solution.py:178
  353.3 33.0 %collective-permute-start.48 = (bf16[32,32,256]{2,1,0:T(8,128)(2,1)}, bf16[32,32,256]{2,1,0:T(8,128)(2,1)}, u32[]{:S(2)}, u32[]{:S(2)}) collective-permute-start(bf16[32,32,256]{2,1,0:T(8,128)(2,1)} %get-tuple-element.228), channel_id=1, source_target_pairs={{0,1},{1,0},{2,3},{3,2},{4,5},{5,4},{6,7},{7,6},{8,9},{9,8},{10,11... | collective-permute-start | bytes 1572872 | tf_op jit(solution)/shard_map/ppermute | solution.py:178
  (69 other events, 1280.4 us)
Sparse Core Ops, SparseCore 0:
  224.5 146.7 reduce-scatter.1

commit v2 on v0

--- a/solution.py
+++ b/solution.py
@@ -144,7 +144,14 @@
     moves = moves_of(ranks)
     rank = lax.axis_index("seq").astype(jnp.int32).reshape(1)
     params = pltpu.CompilerParams(vmem_limit_bytes=VMEM_LIMIT)
-    buffer = jax.ShapeDtypeStruct((local, local, lanes), jnp.bfloat16)
+    together = [[0], list(range(1, chunks - 1)), [chunks - 1]]
+    group_of = {q: members for members in together for q in members}
+
+    def buffer(q):
+        return jax.ShapeDtypeStruct((local, local, len(group_of[q]) * lanes), jnp.bfloat16)
+
+    def place(q):
+        return group_of[q].index(q)
 
     def field_spec(q):
         return pl.BlockSpec((1, blocks * order, width), lambda g, rank: (0, g, q))
@@ -158,20 +165,23 @@
     def unread(after):
         return [pl.BlockSpec(memory_space=pl.ANY)] * len(after)
 
-    def left_forward(q, after):
+    def left_forward(q, held, after):
         return pl.pallas_call(
             functools.partial(left_forward_kernel, ranks),
-            out_shape=[buffer] * ranks + [token],
+            out_shape=[buffer(q)] * ranks + [token],
             grid_spec=pltpu.PrefetchScalarGridSpec(
                 num_scalar_prefetch=1,
                 grid=(local // blocks,),
-                in_specs=[field_spec(q), field_spec(q), factor_spec(blocks)] + unread(after),
-                out_specs=[pl.BlockSpec((blocks, local, lanes), lambda g, rank: (g, 0, 0))] * ranks
+                in_specs=[field_spec(q), field_spec(q), factor_spec(blocks)]
+                + unread(held)
+                + unread(after),
+                out_specs=[pl.BlockSpec((blocks, local, lanes), lambda g, rank: (g, 0, place(q)))] * ranks
                 + [token_spec],
             ),
+            input_output_aliases={4 + n: n for n in range(len(held))},
             compiler_params=params,
             cost_estimate=COST,
-        )(rank, values, cotangent, left_factor, *after)
+        )(rank, values, cotangent, left_factor, *held, *after)
 
     def exchange(sends):
         return [sends[0]] + [
@@ -179,12 +189,14 @@
             for n in range(1, ranks)
         ]
 
-    def right_both(q, arrived, terms, after):
-        held = [] if terms is None else [terms]
-        moved = pl.BlockSpec((local, rows, lanes), lambda g, rank: (0, g, 0))
+    def right_both(q, arrived, terms, held, after):
+        earlier = [] if terms is None else [terms]
+        aliases = {3 + ranks: ranks} if earlier else {}
+        aliases.update({3 + ranks + len(earlier) + n: n for n in range(len(held))})
+        moved = pl.BlockSpec((local, rows, lanes), lambda g, rank: (0, g, place(q)))
         return pl.pallas_call(
             functools.partial(right_kernel, ranks),
-            out_shape=[buffer] * ranks
+            out_shape=[buffer(q)] * ranks
             + [jax.ShapeDtypeStruct((row_count, channels), jnp.bfloat16), token],
             grid_spec=pltpu.PrefetchScalarGridSpec(
                 num_scalar_prefetch=1,
@@ -194,6 +206,7 @@
                     factor_spec(rows),
                 ]
                 + [moved] * ranks
+                + unread(earlier)
                 + unread(held)
                 + unread(after),
                 out_specs=[moved] * ranks
@@ -203,10 +216,10 @@
                     pltpu.VMEM((2, order * rows, width), jnp.float32),
                 ],
             ),
-            input_output_aliases={3 + ranks: ranks} if held else {},
+            input_output_aliases=aliases,
             compiler_params=params,
             cost_estimate=COST,
-        )(rank, kernel, right_factor, *arrived, *held, *after)
+        )(rank, kernel, right_factor, *arrived, *earlier, *held, *after)
 
     def gate(held, after):
         return list(
@@ -245,7 +258,7 @@
                     field_spec(q),
                     factor_spec(blocks),
                 ]
-                + [pl.BlockSpec((blocks, local, lanes), lambda g, rank: (g, 0, 0))] * ranks
+                + [pl.BlockSpec((blocks, local, lanes), lambda g, rank: (g, 0, place(q)))] * ranks
                 + [pl.BlockSpec((shard // steps, channels), lambda g, rank: (g, 0))] * terms
                 + unread(earlier)
                 + unread(after),
@@ -261,42 +274,46 @@
             cost_estimate=COST,
         )(rank, values, cotangent, left_factor, *arrived, *reduced, *earlier, *after)
 
-    received, sent, returned = {}, {}, {}
+    received, returned = [], []
     left_tokens, right_tokens, back_tokens = {}, {}, {}
     terms, outputs = None, []
 
-    def do_left(q):
-        after = [left_tokens[q - 1]] if q else []
-        if q >= 2:
-            after.append(right_tokens[q - 2])
-        *sends, left_tokens[q] = left_forward(q, after)
-        received[q] = exchange(sends)
-
-    for q in range(min(2, chunks)):
-        do_left(q)
-    for q in range(chunks):
+    parts, sent = [[] for _ in together], [[] for _ in together]
+    for n, members in enumerate(together):
+        for q in members:
+            *parts[n], left_tokens[q] = left_forward(q, parts[n], [left_tokens[q - 1]] if q else [])
+
+    def middle(n, q):
+        nonlocal terms
         after = [right_tokens[q - 1]] if q else []
-        *sent[q], terms, right_tokens[q] = right_both(q, received[q], terms, after)
-        if q + 2 < chunks:
-            do_left(q + 2)
-
-    def back_step(q):
+        *sent[n], terms, right_tokens[q] = right_both(q, received[n], terms, sent[n], after)
+
+    def back(n, q):
         last = [reduced] if q == chunks - 1 else []
-        *outputs[:], back_tokens[q] = left_back(q, returned[q], last, outputs, [right_tokens[chunks - 1]])
-
-    for q in range(chunks):
-        after = []
-        if 1 <= q < chunks - 1:
-            after.append(right_tokens[chunks - 1])
-        if q >= 2:
-            after.append(back_tokens[q - 2])
-        returned[q] = exchange(sent[q][:1] + gate(sent[q][1:], after) if after else sent[q])
-        if q == 0:
-            (terms,) = gate([terms], returned[0][1 : 1 + EARLY])
-            reduced = lax.psum_scatter(terms, "dp", scatter_dimension=0, tiled=True)
-        if q >= 1:
-            back_step(q - 1)
-    back_step(chunks - 1)
+        *outputs[:], back_tokens[q] = left_back(q, returned[n], last, outputs, [right_tokens[chunks - 1]])
+
+    received.append(exchange(parts[0]))
+    middle(0, 0)
+    parts[1][1 + EARLY :] = gate(parts[1][1 + EARLY :], [left_tokens[chunks - 1], right_tokens[0]])
+    received.append(exchange(parts[1]))
+    middle(1, 1)
+    parts[2][1 + EARLY :] = gate(parts[2][1 + EARLY :], [right_tokens[1]])
+    received.append(exchange(parts[2]))
+    for q in together[1][1:]:
+        middle(1, q)
+    sent[0][1 : 1 + EARLY] = gate(sent[0][1 : 1 + EARLY], [right_tokens[chunks - 2]])
+    returned.append(exchange(sent[0]))
+    middle(2, chunks - 1)
+    (terms,) = gate([terms], returned[0][1 : 1 + EARLY])
+    reduced = lax.psum_scatter(terms, "dp", scatter_dimension=0, tiled=True)
+    sent[1][1:] = gate(sent[1][1:], [right_tokens[chunks - 1]])
+    returned.append(exchange(sent[1]))
+    back(0, 0)
+    sent[2][1:] = gate(sent[2][1:], [back_tokens[0]])
+    returned.append(exchange(sent[2]))
+    for q in together[1]:
+        back(1, q)
+    back(2, chunks - 1)
     return tuple(outputs)
 
 

time: 421 us -> 422 us (level)
  waiting for transfers between devices: 192 us -> 225 us
  starting transfers between devices: 74.6 us -> 44.3 us
    ppermute x56 -> x42, waiting for transfers between devices: 192 us -> 225 us  [exchange(): lax.ppermute(sends[n], 'seq', [(r, r ^ moves[n]) for r in range(ranks)])]
    ppermute x56 -> x42, starting transfers between devices: 74.5 us -> 44.2 us  [exchange(): lax.ppermute(sends[n], 'seq', [(r, r ^ moves[n]) for r in range(ranks)])]
  transfers between devices with their start and end apart: 57 -> 43, of which waited for: 26 -> 16; matrix products, arithmetic and copies ran while one was open for 0% -> 0% of each run, Pallas kernels for 27% -> 27%
where the time goes in v2:
time: 422 us; the launch traced here: 420 us
  waiting for transfers between devices  225 us (53%)
  Pallas kernels  132 us (31%)
  starting transfers between devices  44.3 us (10%)
  between operations  14.3 us (3%)
    ppermute x42, waiting for transfers between devices, exchange(): lax.ppermute(sends[n], 'seq', [(r, r ^ moves[n]) for r in range(ranks)])  225 us
    pallas_call x4, Pallas kernels, right_both(): pl.pallas_call(functools.partial(right_kernel, ranks), out_shape=[buffer(...  59.9 us
    ppermute x42, starting transfers between devices, exchange(): lax.ppermute(sends[n], 'seq', [(r, r ^ moves[n]) for r in range(ranks)])  44.2 us
    pallas_call x4, Pallas kernels, left_back(): pl.pallas_call(functools.partial(left_back_kernel, ranks, terms), out_sha...  39.4 us
    pallas_call x4, Pallas kernels, left_forward(): pl.pallas_call(functools.partial(left_forward_kernel, ranks), out_shape=[...  33 us
  transfers between devices with their start and end apart: 43, of which 16 were waited for; matrix products, arithmetic and copies ran while one was open for 0% of the time, Pallas kernels for 27%

profile of v2, /device:TPU:0, one launch (start us, length us, event | category | flops | bytes accessed | tf_op | source)
XLA Modules:
  0.0 420.2 jit_solution(17099996654442967507)
XLA Ops:
  7.2 8.3 %shard_map.76 = (bf16[32,32,256]{2,1,0:T(8,128)(2,1)}, bf16[32,32,256]{2,1,0:T(8,128)(2,1)}, bf16[32,32,256]{2,1,0:T(8,128)(2,1)}, bf16[32,32,256]{2,1,0:T(8,128...) custom-call(s32[1]{0:T(128)} %bitcast.rank_ref, ...), custom_call_target="tpu_custom_call" | custom-call | flops 1024 | bytes 1024 | tf_op jit(solution)/shard_map/pallas_call | solution.py:169
  15.5 3.0 collective-permute-start.6
  20.6 8.2 %shard_map.77 = (bf16[32,32,512]{2,1,0:T(8,128)(2,1)}, bf16[32,32,512]{2,1,0:T(8,128)(2,1)}, bf16[32,32,512]{2,1,0:T(8,128)(2,1)}, bf16[32,32,512]{2,1,0:T(8,128...) custom-call(s32[1]{0:T(128)} %bitcast.rank_ref, ...), custom_call_target="tpu_custom_call" | custom-call | flops 1024 | bytes 1024 | tf_op jit(solution)/shard_map/pallas_call | solution.py:169
  28.8 8.2 %shard_map.78 = (bf16[32,32,512]{2,1,0:T(8,128)(2,1)}, bf16[32,32,512]{2,1,0:T(8,128)(2,1)}, bf16[32,32,512]{2,1,0:T(8,128)(2,1)}, bf16[32,32,512]{2,1,0:T(8,128...) custom-call(s32[1]{0:T(128)} %bitcast.rank_ref, ...), custom_call_target="tpu_custom_call", output_to_operand_aliasing={{0}: (4, {}), {1}: (5, {}), {2}: (6, {}), {3}: (7, {}), {4}... | custom-call | flops 1024 | bytes 1024 | tf_op jit(solution)/shard_map/pallas_call | solution.py:169
  40.0 3.6 collective-permute-done.7.refs_2_
  44.3 9.4 %collective-permute-done.9.refs_4_ = bf16[32,32,256]{2,1,0:T(8,128)(2,1)} collective-permute-done((bf16[32,32,256]{2,1,0:T(8,128)(2,1)}, bf16[32,32,256]{2,1,0:T(8,128)(2,1)}, u32[]{:S(2)}, u32[]{:S(2)}) %collective-permute-start.9) | collective-permute-done | bytes 524320 | tf_op jit(solution)/shard_map/ppermute | solution.py:188
  54.1 8.2 %shard_map.79 = (bf16[32,32,256]{2,1,0:T(8,128)(2,1)}, bf16[32,32,256]{2,1,0:T(8,128)(2,1)}, bf16[32,32,256]{2,1,0:T(8,128)(2,1)}, bf16[32,32,256]{2,1,0:T(8,128...) custom-call(s32[1]{0:T(128)} %bitcast.rank_ref, ...), custom_call_target="tpu_custom_call" | custom-call | flops 1024 | bytes 1024 | tf_op jit(solution)/shard_map/pallas_call | solution.py:169
  62.4 25.9 %collective-permute-done.10.refs_5_ = bf16[32,32,256]{2,1,0:T(8,128)(2,1)} collective-permute-done((bf16[32,32,256]{2,1,0:T(8,128)(2,1)}, bf16[32,32,256]{2,1,0:T(8,128)(2,1)}, u32[]{:S(2)}, u32[]{:S(2)}) %collective-permute-start.10) | collective-permute-done | bytes 524320 | tf_op jit(solution)/shard_map/ppermute | solution.py:188
  89.9 15.1 %shard_map.80 = (bf16[32,32,256]{2,1,0:T(8,128)(2,1)}, bf16[32,32,256]{2,1,0:T(8,128)(2,1)}, bf16[32,32,256]{2,1,0:T(8,128)(2,1)}, bf16[32,32,256]{2,1,0:T(8,128...) custom-call(s32[1]{0:T(128)} %bitcast.rank_ref, ...), custom_call_target="tpu_custom_call" | custom-call | flops 1024 | bytes 1024 | tf_op jit(solution)/shard_map/pallas_call | solution.py:197
  108.5 7.0 %collective-permute-done.5.refs_3_ = bf16[32,32,512]{2,1,0:T(8,128)(2,1)S(1)} collective-permute-done((bf16[32,32,512]{2,1,0:T(8,128)(2,1)}, bf16[32,32,512]{2,1,0:T(8,128)(2,1)S(1)}, u32[]{:S(2)}, u32[]{:S(2)}) %collective-permute-start.5) | collective-permute-done | bytes 1048608 | tf_op jit(solution)/shard_map/ppermute | solution.py:188
  115.5 21.6 %collective-permute-done.13.refs_4_ = bf16[32,32,512]{2,1,0:T(8,128)(2,1)} collective-permute-done((bf16[32,32,512]{2,1,0:T(8,128)(2,1)}, bf16[32,32,512]{2,1,0:T(8,128)(2,1)}, u32[]{:S(2)}, u32[]{:S(2)}) %collective-permute-start.13) | collective-permute-done | bytes 1048608 | tf_op jit(solution)/shard_map/ppermute | solution.py:188
  139.6 19.3 %collective-permute-done.15.refs_6_ = bf16[32,32,512]{2,1,0:T(8,128)(2,1)} collective-permute-done((bf16[32,32,512]{2,1,0:T(8,128)(2,1)}, bf16[32,32,512]{2,1,0:T(8,128)(2,1)}, u32[]{:S(2)}, u32[]{:S(2)}) %collective-permute-start.15) | collective-permute-done | bytes 1048608 | tf_op jit(solution)/shard_map/ppermute | solution.py:188
  159.0 15.0 %shard_map.82 = (bf16[32,32,512]{2,1,0:T(8,128)(2,1)}, bf16[32,32,512]{2,1,0:T(8,128)(2,1)}, bf16[32,32,512]{2,1,0:T(8,128)(2,1)}, bf16[32,32,512]{2,1,0:T(8,128...) custom-call(s32[1]{0:T(128)} %bitcast.rank_ref, ...), custom_call_target="tpu_custom_call", output_to_operand_aliasing={{8}: (11, {})} | custom-call | flops 1024 | bytes 1024 | tf_op jit(solution)/shard_map/pallas_call | solution.py:197
  175.9 14.9 %shard_map.84 = (bf16[32,32,512]{2,1,0:T(8,128)(2,1)}, bf16[32,32,512]{2,1,0:T(8,128)(2,1)}, bf16[32,32,512]{2,1,0:T(8,128)(2,1)}, bf16[32,32,512]{2,1,0:T(8,128...) custom-call(s32[1]{0:T(128)} %bitcast.rank_ref, ...), custom_call_target="tpu_custom_call", output_to_operand_aliasing={{8}: (11, {}), {0}: (12, {}), {1}: (13, {}), {2}: (14, {}),... | custom-call | flops 1024 | bytes 1024 | tf_op jit(solution)/shard_map/pallas_call | solution.py:197
  190.8 2.1 collective-permute-start.21
  196.7 20.1 %collective-permute-done.19.refs_6_ = bf16[32,32,256]{2,1,0:T(8,128)(2,1)S(1)} collective-permute-done((bf16[32,32,256]{2,1,0:T(8,128)(2,1)}, bf16[32,32,256]{2,1,0:T(8,128)(2,1)S(1)}, u32[]{:S(2)}, u32[]{:S(2)}) %collective-permute-start.19) | collective-permute-done | bytes 524320 | tf_op jit(solution)/shard_map/ppermute | solution.py:188
  217.8 14.9 %shard_map.85 = (bf16[32,32,256]{2,1,0:T(8,128)(2,1)}, bf16[32,32,256]{2,1,0:T(8,128)(2,1)}, bf16[32,32,256]{2,1,0:T(8,128)(2,1)}, bf16[32,32,256]{2,1,0:T(8,128...) custom-call(s32[1]{0:T(128)} %bitcast.rank_ref, ...), custom_call_target="tpu_custom_call", output_to_operand_aliasing={{8}: (11, {})} | custom-call | flops 1024 | bytes 1024 | tf_op jit(solution)/shard_map/pallas_call | solution.py:197
  236.7 2.1 collective-permute-start.26
  240.4 7.6 %collective-permute-done.24.refs_4_ = bf16[32,32,256]{2,1,0:T(8,128)(2,1)S(1)} collective-permute-done((bf16[32,32,256]{2,1,0:T(8,128)(2,1)S(1)}, bf16[32,32,256]{2,1,0:T(8,128)(2,1)S(1)}, u32[]{:S(2)}, u32[]{:S(2)}) %collective-permute-start.24) | collective-permute-done | bytes 524320 | tf_op jit(solution)/shard_map/ppermute | solution.py:188
  248.0 3.5 collective-permute-start.36
  251.5 10.7 %collective-permute-done.26.refs_6_ = bf16[32,32,256]{2,1,0:T(8,128)(2,1)S(1)} collective-permute-done((bf16[32,32,256]{2,1,0:T(8,128)(2,1)}, bf16[32,32,256]{2,1,0:T(8,128)(2,1)S(1)}, u32[]{:S(2)}, u32[]{:S(2)}) %collective-permute-start.26) | collective-permute-done | bytes 524320 | tf_op jit(solution)/shard_map/ppermute | solution.py:188
  263.0 9.4 %shard_map.87 = (bf16[1,8192,512]{2,1,0:T(8,128)(2,1)}, bf16[1,8192,512]{2,1,0:T(8,128)(2,1)}, f32[2048,512]{1,0:T(8,128)}, f32[8,128]{1,0:T(8,128)}) custom-call(s32[1]{0:T(128)} %bitcast.rank_ref, bf16[1,8192,512]{2,1,0:T(8,128)(2,1)} %values_ref.15, bf16[1,8192,512]{2,1,0:T(8,128)(2,1)} %cotangent_ref.15, bf16[32,256,256]{2,1,0:T(8,128)(2,1)} %left_ref.15, ...), custom_call_target="tpu_custom_call" | custom-call | flops 1024 | bytes 1024 | tf_op jit(solution)/shard_map/pallas_call | solution.py:250
  276.0 19.4 %collective-permute-done.28.refs_1_ = bf16[32,32,256]{2,1,0:T(8,128)(2,1)S(1)} collective-permute-done((bf16[32,32,256]{2,1,0:T(8,128)(2,1)}, bf16[32,32,256]{2,1,0:T(8,128)(2,1)S(1)}, u32[]{:S(2)}, u32[]{:S(2)}) %collective-permute-start.28) | collective-permute-done | bytes 524320 | tf_op jit(solution)/shard_map/ppermute | solution.py:188
  296.0 21.3 %collective-permute-done.29.refs_2_ = bf16[32,32,256]{2,1,0:T(8,128)(2,1)S(1)} collective-permute-done((bf16[32,32,256]{2,1,0:T(8,128)(2,1)}, bf16[32,32,256]{2,1,0:T(8,128)(2,1)S(1)}, u32[]{:S(2)}, u32[]{:S(2)}) %collective-permute-start.29) | collective-permute-done | bytes 524320 | tf_op jit(solution)/shard_map/ppermute | solution.py:188
  319.5 2.3 collective-permute-start.30
  321.8 16.2 %collective-permute-done.38.refs_4_ = bf16[32,32,512]{2,1,0:T(8,128)(2,1)} collective-permute-done((bf16[32,32,512]{2,1,0:T(8,128)(2,1)}, bf16[32,32,512]{2,1,0:T(8,128)(2,1)}, u32[]{:S(2)}, u32[]{:S(2)}) %collective-permute-start.38) | collective-permute-done | bytes 1048608 | tf_op jit(solution)/shard_map/ppermute | solution.py:188
  338.0 2.2 collective-permute-start.31
  340.2 36.4 %collective-permute-done.39.refs_5_ = bf16[32,32,512]{2,1,0:T(8,128)(2,1)} collective-permute-done((bf16[32,32,512]{2,1,0:T(8,128)(2,1)}, bf16[32,32,512]{2,1,0:T(8,128)(2,1)}, u32[]{:S(2)}, u32[]{:S(2)}) %collective-permute-start.39) | collective-permute-done | bytes 1048608 | tf_op jit(solution)/shard_map/ppermute | solution.py:188
  378.3 9.4 %shard_map.91 = (bf16[1,8192,512]{2,1,0:T(8,128)(2,1)}, bf16[1,8192,512]{2,1,0:T(8,128)(2,1)}, f32[2048,512]{1,0:T(8,128)}, f32[8,128]{1,0:T(8,128)}) custom-call(s32[1]{0:T(128)} %bitcast.rank_ref, bf16[1,8192,512]{2,1,0:T(8,128)(2,1)} %values_ref.15, ...), custom_call_target="tpu_custom_call", output_to_operand_aliasing={{0}: (12, {}), {1}: (13, {}), {2}: (14, {})} | custom-call | flops 1024 | bytes 1024 | tf_op jit(solution)/shard_map/pallas_call | solution.py:250
  387.7 9.4 %shard_map.92 = (bf16[1,8192,512]{2,1,0:T(8,128)(2,1)}, bf16[1,8192,512]{2,1,0:T(8,128)(2,1)}, f32[2048,512]{1,0:T(8,128)}, f32[8,128]{1,0:T(8,128)}) custom-call(s32[1]{0:T(128)} %bitcast.rank_ref, bf16[1,8192,512]{2,1,0:T(8,128)(2,1)} %values_ref.15, ...), custom_call_target="tpu_custom_call", output_to_operand_aliasing={{0}: (12, {}), {1}: (13, {}), {2}: (14, {})} | custom-call | flops 1024 | bytes 1024 | tf_op jit(solution)/shard_map/pallas_call | solution.py:250
  397.1 5.0 %collective-permute-done.32.refs_5_ = bf16[32,32,256]{2,1,0:T(8,128)(2,1)} collective-permute-done((bf16[32,32,256]{2,1,0:T(8,128)(2,1)}, bf16[32,32,256]{2,1,0:T(8,128)(2,1)}, u32[]{:S(2)}, u32[]{:S(2)}) %collective-permute-start.32) | collective-permute-done | bytes 524320 | tf_op jit(solution)/shard_map/ppermute | solution.py:188
  402.1 11.2 %shard_map.93 = (bf16[1,8192,512]{2,1,0:T(8,128)(2,1)}, bf16[1,8192,512]{2,1,0:T(8,128)(2,1)}, f32[2048,512]{1,0:T(8,128)}, f32[8,128]{1,0:T(8,128)}) custom-call(s32[1]{0:T(128)} %bitcast.rank_ref, bf16[1,8192,512]{2,1,0:T(8,128)(2,1)} %values_ref.15, ...), custom_call_target="tpu_custom_call", output_to_operand_aliasing={{0}: (13, {}), {1}: (14, {}), {2}: (15, {})} | custom-call | flops 1024 | bytes 1024 | tf_op jit(solution)/shard_map/pallas_call | solution.py:250
  (119 shorter events, 34.8 us)
Async XLA Ops:
  7.2 394.9 %reduce-scatter.2.cloned.1.call-start = ((), (), s32[]{:S(2)}) async-start(), calls=%async_computation.1 | async-start | bytes 10485760 | tf_op jit(solution)/shard_map/reduce_scatter | solution.py:308
  20.1 33.6 %collective-permute-start.9 = (bf16[32,32,256]{2,1,0:T(8,128)(2,1)}, bf16[32,32,256]{2,1,0:T(8,128)(2,1)}, u32[]{:S(2)}, u32[]{:S(2)}) collective-permute-start(bf16[32,32,256]{2,1,0:T(8,128)(2,1)} %get-tuple-element.149), channel_id=1, source_target_pairs={{0,3},{1,2},{2,1},{3,0},{4,7},{5,6},{6,5},{7,4},{8,11},{9,10},{10,... | collective-permute-start | bytes 1572872 | tf_op jit(solution)/shard_map/ppermute | solution.py:188
  37.1 69.7 %collective-permute-start.3 = (bf16[32,32,512]{2,1,0:T(8,128)(2,1)}, bf16[32,32,512]{2,1,0:T(8,128)(2,1)S(1)}, u32[]{:S(2)}, u32[]{:S(2)}) collective-permute-start(bf16[32,32,512]{2,1,0:T(8,128)(2,1)} %get-tuple-element.137), channel_id=1, source_target_pairs={{0,2},{1,3},{2,0},{3,1},{4,6},{5,7},{6,4},{7,5},{8,10},{9,11},{10,... | collective-permute-start | bytes 3145736 | tf_op jit(solution)/shard_map/ppermute | solution.py:188
  38.5 68.2 %collective-permute-start.4 = (bf16[32,32,512]{2,1,0:T(8,128)(2,1)}, bf16[32,32,512]{2,1,0:T(8,128)(2,1)S(1)}, u32[]{:S(2)}, u32[]{:S(2)}) collective-permute-start(bf16[32,32,512]{2,1,0:T(8,128)(2,1)} %get-tuple-element.138), channel_id=1, source_target_pairs={{0,4},{1,5},{2,6},{3,7},{4,0},{5,1},{6,2},{7,3},{8,12},{9,13},{10,... | collective-permute-start | bytes 3145736 | tf_op jit(solution)/shard_map/ppermute | solution.py:188
  43.6 44.7 %collective-permute-start.10 = (bf16[32,32,256]{2,1,0:T(8,128)(2,1)}, bf16[32,32,256]{2,1,0:T(8,128)(2,1)}, u32[]{:S(2)}, u32[]{:S(2)}) collective-permute-start(bf16[32,32,256]{2,1,0:T(8,128)(2,1)} %get-tuple-element.150), channel_id=1, source_target_pairs={{0,5},{1,4},{2,7},{3,6},{4,1},{5,0},{6,3},{7,2},{8,13},{9,12},{10,... | collective-permute-start | bytes 1572872 | tf_op jit(solution)/shard_map/ppermute | solution.py:188
  44.3 45.6 %collective-permute-start.11 = (bf16[32,32,256]{2,1,0:T(8,128)(2,1)}, bf16[32,32,256]{2,1,0:T(8,128)(2,1)}, u32[]{:S(2)}, u32[]{:S(2)}) collective-permute-start(bf16[32,32,256]{2,1,0:T(8,128)(2,1)} %get-tuple-element.151), channel_id=1, source_target_pairs={{0,7},{1,6},{2,5},{3,4},{4,3},{5,2},{6,1},{7,0},{8,15},{9,14},{10,... | collective-permute-start | bytes 1572872 | tf_op jit(solution)/shard_map/ppermute | solution.py:188
  53.7 36.2 %collective-permute-start.12 = (bf16[32,32,256]{2,1,0:T(8,128)(2,1)}, bf16[32,32,256]{2,1,0:T(8,128)(2,1)}, u32[]{:S(2)}, u32[]{:S(2)}) collective-permute-start(bf16[32,32,256]{2,1,0:T(8,128)(2,1)} %get-tuple-element.152), channel_id=1, source_target_pairs={{0,1},{1,0},{2,3},{3,2},{4,5},{5,4},{6,7},{7,6},{8,9},{9,8},{10,11... | collective-permute-start | bytes 1572872 | tf_op jit(solution)/shard_map/ppermute | solution.py:188
  88.3 27.2 %collective-permute-start.5 = (bf16[32,32,512]{2,1,0:T(8,128)(2,1)}, bf16[32,32,512]{2,1,0:T(8,128)(2,1)S(1)}, u32[]{:S(2)}, u32[]{:S(2)}) collective-permute-start(bf16[32,32,512]{2,1,0:T(8,128)(2,1)} %get-tuple-element.139), channel_id=1, source_target_pairs={{0,6},{1,7},{2,4},{3,5},{4,2},{5,3},{6,0},{7,1},{8,14},{9,15},{10,... | collective-permute-start | bytes 3145736 | tf_op jit(solution)/shard_map/ppermute | solution.py:188
  105.1 32.0 %collective-permute-start.13 = (bf16[32,32,512]{2,1,0:T(8,128)(2,1)}, bf16[32,32,512]{2,1,0:T(8,128)(2,1)}, u32[]{:S(2)}, u32[]{:S(2)}) collective-permute-start(bf16[32,32,512]{2,1,0:T(8,128)(2,1)} %get-tuple-element.154), channel_id=1, source_target_pairs={{0,3},{1,2},{2,1},{3,0},{4,7},{5,6},{6,5},{7,4},{8,11},{9,10},{10,... | collective-permute-start | bytes 3145736 | tf_op jit(solution)/shard_map/ppermute | solution.py:188
  105.8 32.2 %collective-permute-start.14 = (bf16[32,32,512]{2,1,0:T(8,128)(2,1)}, bf16[32,32,512]{2,1,0:T(8,128)(2,1)}, u32[]{:S(2)}, u32[]{:S(2)}) collective-permute-start(bf16[32,32,512]{2,1,0:T(8,128)(2,1)} %get-tuple-element.155), channel_id=1, source_target_pairs={{0,5},{1,4},{2,7},{3,6},{4,1},{5,0},{6,3},{7,2},{8,13},{9,12},{10,... | collective-permute-start | bytes 3145736 | tf_op jit(solution)/shard_map/ppermute | solution.py:188
  106.8 52.2 %collective-permute-start.15 = (bf16[32,32,512]{2,1,0:T(8,128)(2,1)}, bf16[32,32,512]{2,1,0:T(8,128)(2,1)}, u32[]{:S(2)}, u32[]{:S(2)}) collective-permute-start(bf16[32,32,512]{2,1,0:T(8,128)(2,1)} %get-tuple-element.156), channel_id=1, source_target_pairs={{0,7},{1,6},{2,5},{3,4},{4,3},{5,2},{6,1},{7,0},{8,15},{9,14},{10,... | collective-permute-start | bytes 3145736 | tf_op jit(solution)/shard_map/ppermute | solution.py:188
  106.8 52.2 %collective-permute-start.16 = (bf16[32,32,512]{2,1,0:T(8,128)(2,1)}, bf16[32,32,512]{2,1,0:T(8,128)(2,1)}, u32[]{:S(2)}, u32[]{:S(2)}) collective-permute-start(bf16[32,32,512]{2,1,0:T(8,128)(2,1)} %get-tuple-element.157), channel_id=1, source_target_pairs={{0,1},{1,0},{2,3},{3,2},{4,5},{5,4},{6,7},{7,6},{8,9},{9,8},{10,11... | collective-permute-start | bytes 3145736 | tf_op jit(solution)/shard_map/ppermute | solution.py:188
  115.5 75.3 %collective-permute-start = (bf16[32,32,256]{2,1,0:T(8,128)(2,1)}, bf16[32,32,256]{2,1,0:T(8,128)(2,1)S(1)}, u32[]{:S(2)}, u32[]{:S(2)}) collective-permute-start(bf16[32,32,256]{2,1,0:T(8,128)(2,1)} %get-tuple-element.129), channel_id=1, source_target_pairs={{0,2},{1,3},{2,0},{3,1},{4,6},{5,7},{6,4},{7,5},{8,10},{9,11},{10,... | collective-permute-start | bytes 1572872 | tf_op jit(solution)/shard_map/ppermute | solution.py:188
  137.1 55.9 %collective-permute-start.1 = (bf16[32,32,256]{2,1,0:T(8,128)(2,1)}, bf16[32,32,256]{2,1,0:T(8,128)(2,1)}, u32[]{:S(2)}, u32[]{:S(2)}) collective-permute-start(bf16[32,32,256]{2,1,0:T(8,128)(2,1)} %get-tuple-element.130), channel_id=1, source_target_pairs={{0,4},{1,5},{2,6},{3,7},{4,0},{5,1},{6,2},{7,3},{8,12},{9,13},{10,... | collective-permute-start | bytes 1572872 | tf_op jit(solution)/shard_map/ppermute | solution.py:188
  138.0 55.4 %collective-permute-start.2 = (bf16[32,32,256]{2,1,0:T(8,128)(2,1)}, bf16[32,32,256]{2,1,0:T(8,128)(2,1)}, u32[]{:S(2)}, u32[]{:S(2)}) collective-permute-start(bf16[32,32,256]{2,1,0:T(8,128)(2,1)} %get-tuple-element.131), channel_id=1, source_target_pairs={{0,6},{1,7},{2,4},{3,5},{4,2},{5,3},{6,0},{7,1},{8,14},{9,15},{10,... | collective-permute-start | bytes 1572872 | tf_op jit(solution)/shard_map/ppermute | solution.py:188
  190.8 41.9 %collective-permute-start.21 = (bf16[32,32,256]{2,1,0:T(8,128)(2,1)}, bf16[32,32,256]{2,1,0:T(8,128)(2,1)S(1)}, u32[]{:S(2)}, u32[]{:S(2)}) collective-permute-start(bf16[32,32,256]{2,1,0:T(8,128)(2,1)} %get-tuple-element.187), channel_id=1, source_target_pairs={{0,2},{1,3},{2,0},{3,1},{4,6},{5,7},{6,4},{7,5},{8,10},{9,11},{10,... | collective-permute-start | bytes 1572872 | tf_op jit(solution)/shard_map/ppermute | solution.py:188
  193.9 38.8 %collective-permute-start.22 = (bf16[32,32,256]{2,1,0:T(8,128)(2,1)}, bf16[32,32,256]{2,1,0:T(8,128)(2,1)S(1)}, u32[]{:S(2)}, u32[]{:S(2)}) collective-permute-start(bf16[32,32,256]{2,1,0:T(8,128)(2,1)} %get-tuple-element.188), channel_id=1, source_target_pairs={{0,4},{1,5},{2,6},{3,7},{4,0},{5,1},{6,2},{7,3},{8,12},{9,13},{10,... | collective-permute-start | bytes 1572872 | tf_op jit(solution)/shard_map/ppermute | solution.py:188
  195.4 37.4 %collective-permute-start.23 = (bf16[32,32,256]{2,1,0:T(8,128)(2,1)}, bf16[32,32,256]{2,1,0:T(8,128)(2,1)S(1)}, u32[]{:S(2)}, u32[]{:S(2)}) collective-permute-start(bf16[32,32,256]{2,1,0:T(8,128)(2,1)} %get-tuple-element.189), channel_id=1, source_target_pairs={{0,6},{1,7},{2,4},{3,5},{4,2},{5,3},{6,0},{7,1},{8,14},{9,15},{10,... | collective-permute-start | bytes 1572872 | tf_op jit(solution)/shard_map/ppermute | solution.py:188
  236.7 25.5 %collective-permute-start.26 = (bf16[32,32,256]{2,1,0:T(8,128)(2,1)}, bf16[32,32,256]{2,1,0:T(8,128)(2,1)S(1)}, u32[]{:S(2)}, u32[]{:S(2)}) collective-permute-start(bf16[32,32,256]{2,1,0:T(8,128)(2,1)} %get-tuple-element.192), channel_id=1, source_target_pairs={{0,7},{1,6},{2,5},{3,4},{4,3},{5,2},{6,1},{7,0},{8,15},{9,14},{10,... | collective-permute-start | bytes 1572872 | tf_op jit(solution)/shard_map/ppermute | solution.py:188
  238.8 79.9 %collective-permute-start.35 = (bf16[32,32,512]{2,1,0:T(8,128)(2,1)}, bf16[32,32,512]{2,1,0:T(8,128)(2,1)S(1)}, u32[]{:S(2)}, u32[]{:S(2)}) collective-permute-start(bf16[32,32,512]{2,1,0:T(8,128)(2,1)} %get-tuple-element.212), channel_id=1, source_target_pairs={{0,2},{1,3},{2,0},{3,1},{4,6},{5,7},{6,4},{7,5},{8,10},{9,11},{10,... | collective-permute-start | bytes 3145736 | tf_op jit(solution)/shard_map/ppermute | solution.py:188
  248.0 70.7 %collective-permute-start.36 = (bf16[32,32,512]{2,1,0:T(8,128)(2,1)}, bf16[32,32,512]{2,1,0:T(8,128)(2,1)S(1)}, u32[]{:S(2)}, u32[]{:S(2)}) collective-permute-start(bf16[32,32,512]{2,1,0:T(8,128)(2,1)} %get-tuple-element.213), channel_id=1, source_target_pairs={{0,4},{1,5},{2,6},{3,7},{4,0},{5,1},{6,2},{7,3},{8,12},{9,13},{10,... | collective-permute-start | bytes 3145736 | tf_op jit(solution)/shard_map/ppermute | solution.py:188
  273.0 44.4 %collective-permute-start.29 = (bf16[32,32,256]{2,1,0:T(8,128)(2,1)}, bf16[32,32,256]{2,1,0:T(8,128)(2,1)S(1)}, u32[]{:S(2)}, u32[]{:S(2)}) collective-permute-start(bf16[32,32,256]{2,1,0:T(8,128)(2,1)} %get-tuple-element.197), channel_id=1, source_target_pairs={{0,4},{1,5},{2,6},{3,7},{4,0},{5,1},{6,2},{7,3},{8,12},{9,13},{10,... | collective-permute-start | bytes 1572872 | tf_op jit(solution)/shard_map/ppermute | solution.py:188
  274.4 45.1 %collective-permute-start.37 = (bf16[32,32,512]{2,1,0:T(8,128)(2,1)}, bf16[32,32,512]{2,1,0:T(8,128)(2,1)S(1)}, u32[]{:S(2)}, u32[]{:S(2)}) collective-permute-start(bf16[32,32,512]{2,1,0:T(8,128)(2,1)} %get-tuple-element.214), channel_id=1, source_target_pairs={{0,6},{1,7},{2,4},{3,5},{4,2},{5,3},{6,0},{7,1},{8,14},{9,15},{10,... | collective-permute-start | bytes 3145736 | tf_op jit(solution)/shard_map/ppermute | solution.py:188
  295.4 42.7 %collective-permute-start.38 = (bf16[32,32,512]{2,1,0:T(8,128)(2,1)}, bf16[32,32,512]{2,1,0:T(8,128)(2,1)}, u32[]{:S(2)}, u32[]{:S(2)}) collective-permute-start(bf16[32,32,512]{2,1,0:T(8,128)(2,1)} %get-tuple-element.215), channel_id=1, source_target_pairs={{0,3},{1,2},{2,1},{3,0},{4,7},{5,6},{6,5},{7,4},{8,11},{9,10},{10,... | collective-permute-start | bytes 3145736 | tf_op jit(solution)/shard_map/ppermute | solution.py:188
  317.4 59.3 %collective-permute-start.39 = (bf16[32,32,512]{2,1,0:T(8,128)(2,1)}, bf16[32,32,512]{2,1,0:T(8,128)(2,1)}, u32[]{:S(2)}, u32[]{:S(2)}) collective-permute-start(bf16[32,32,512]{2,1,0:T(8,128)(2,1)} %get-tuple-element.216), channel_id=1, source_target_pairs={{0,5},{1,4},{2,7},{3,6},{4,1},{5,0},{6,3},{7,2},{8,13},{9,12},{10,... | collective-permute-start | bytes 3145736 | tf_op jit(solution)/shard_map/ppermute | solution.py:188
  318.7 58.0 %collective-permute-start.40 = (bf16[32,32,512]{2,1,0:T(8,128)(2,1)}, bf16[32,32,512]{2,1,0:T(8,128)(2,1)}, u32[]{:S(2)}, u32[]{:S(2)}) collective-permute-start(bf16[32,32,512]{2,1,0:T(8,128)(2,1)} %get-tuple-element.217), channel_id=1, source_target_pairs={{0,7},{1,6},{2,5},{3,4},{4,3},{5,2},{6,1},{7,0},{8,15},{9,14},{10,... | collective-permute-start | bytes 3145736 | tf_op jit(solution)/shard_map/ppermute | solution.py:188
  318.7 58.0 %collective-permute-start.41 = (bf16[32,32,512]{2,1,0:T(8,128)(2,1)}, bf16[32,32,512]{2,1,0:T(8,128)(2,1)}, u32[]{:S(2)}, u32[]{:S(2)}) collective-permute-start(bf16[32,32,512]{2,1,0:T(8,128)(2,1)} %get-tuple-element.218), channel_id=1, source_target_pairs={{0,1},{1,0},{2,3},{3,2},{4,5},{5,4},{6,7},{7,6},{8,9},{9,8},{10,11... | collective-permute-start | bytes 3145736 | tf_op jit(solution)/shard_map/ppermute | solution.py:188
  319.5 77.5 %collective-permute-start.30 = (bf16[32,32,256]{2,1,0:T(8,128)(2,1)}, bf16[32,32,256]{2,1,0:T(8,128)(2,1)}, u32[]{:S(2)}, u32[]{:S(2)}) collective-permute-start(bf16[32,32,256]{2,1,0:T(8,128)(2,1)} %get-tuple-element.198), channel_id=1, source_target_pairs={{0,6},{1,7},{2,4},{3,5},{4,2},{5,3},{6,0},{7,1},{8,14},{9,15},{10,... | collective-permute-start | bytes 1572872 | tf_op jit(solution)/shard_map/ppermute | solution.py:188
  338.0 59.0 %collective-permute-start.31 = (bf16[32,32,256]{2,1,0:T(8,128)(2,1)}, bf16[32,32,256]{2,1,0:T(8,128)(2,1)}, u32[]{:S(2)}, u32[]{:S(2)}) collective-permute-start(bf16[32,32,256]{2,1,0:T(8,128)(2,1)} %get-tuple-element.199), channel_id=1, source_target_pairs={{0,3},{1,2},{2,1},{3,0},{4,7},{5,6},{6,5},{7,4},{8,11},{9,10},{10,... | collective-permute-start | bytes 1572872 | tf_op jit(solution)/shard_map/ppermute | solution.py:188
  376.7 25.4 %collective-permute-start.32 = (bf16[32,32,256]{2,1,0:T(8,128)(2,1)}, bf16[32,32,256]{2,1,0:T(8,128)(2,1)}, u32[]{:S(2)}, u32[]{:S(2)}) collective-permute-start(bf16[32,32,256]{2,1,0:T(8,128)(2,1)} %get-tuple-element.200), channel_id=1, source_target_pairs={{0,5},{1,4},{2,7},{3,6},{4,1},{5,0},{6,3},{7,2},{8,13},{9,12},{10,... | collective-permute-start | bytes 1572872 | tf_op jit(solution)/shard_map/ppermute | solution.py:188
  376.7 25.4 %collective-permute-start.33 = (bf16[32,32,256]{2,1,0:T(8,128)(2,1)}, bf16[32,32,256]{2,1,0:T(8,128)(2,1)}, u32[]{:S(2)}, u32[]{:S(2)}) collective-permute-start(bf16[32,32,256]{2,1,0:T(8,128)(2,1)} %get-tuple-element.201), channel_id=1, source_target_pairs={{0,7},{1,6},{2,5},{3,4},{4,3},{5,2},{6,1},{7,0},{8,15},{9,14},{10,... | collective-permute-start | bytes 1572872 | tf_op jit(solution)/shard_map/ppermute | solution.py:188
  376.8 25.3 %collective-permute-start.34 = (bf16[32,32,256]{2,1,0:T(8,128)(2,1)}, bf16[32,32,256]{2,1,0:T(8,128)(2,1)}, u32[]{:S(2)}, u32[]{:S(2)}) collective-permute-start(bf16[32,32,256]{2,1,0:T(8,128)(2,1)} %get-tuple-element.202), channel_id=1, source_target_pairs={{0,1},{1,0},{2,3},{3,2},{4,5},{5,4},{6,7},{7,6},{8,9},{9,8},{10,11... | collective-permute-start | bytes 1572872 | tf_op jit(solution)/shard_map/ppermute | solution.py:188
  (34 other events, 796.8 us)
Sparse Core Ops, SparseCore 0:
  234.0 145.7 reduce-scatter.1

commit v3 on v0

--- a/solution.py
+++ b/solution.py
@@ -11,6 +11,7 @@
 ROWS = 16
 VMEM_LIMIT = 60 * 1024 * 1024
 COST = pl.CostEstimate(flops=1024, bytes_accessed=1024, transcendentals=0)
+FIRST = 5
 EARLY = 3
 UNROLL = 4
 TOKEN = (8, 128)
@@ -41,26 +42,29 @@
             sends[m][i] = first[m * share : (m + 1) * share]
 
 
-def right_kernel(ranks, rank_ref, kernel_ref, right_ref, *refs):
-    arrived = refs[:ranks]
-    *sends, term_ref, token_ref, gathered, scattered = refs[-ranks - 4 :]
+def right_kernel(ranks, arrived_parts, sent_parts, rank_ref, kernel_ref, right_ref, *refs):
+    arrived = refs[: arrived_parts * ranks]
+    *sends, term_ref, token_ref, gathered, scattered = refs[-sent_parts * ranks - 4 :]
     token_ref[...] = jnp.zeros_like(token_ref)
-    share, rows, lanes = arrived[0].shape
+    _, rows, lanes = arrived[0].shape
     order = right_ref.shape[1]
+    share = order // ranks
     width = lanes // 2
     rank = rank_ref[0]
     halves = [slice(0, width), slice(width, lanes)]
 
     moves = moves_of(ranks)
 
-    def span(n):
-        m = moves[n]
-        return pl.ds(pl.multiple_of((rank ^ m) * (share * rows), share * rows), share * rows)
-
-    for m in range(ranks):
+    def span(n, part, parts):
+        size = share * rows // parts
+        start = (rank ^ moves[n]) * (share * rows) + part * size
+        return pl.ds(pl.multiple_of(start, size), size)
+
+    for n, block_ref in enumerate(arrived):
+        where = span(n % ranks, n // ranks, arrived_parts)
         for half in range(2):
-            block = arrived[m][:, :, halves[half]].astype(jnp.float32)
-            gathered[half, span(m), :] = block.reshape(share * rows, width)
+            block = block_ref[:, :, halves[half]].astype(jnp.float32)
+            gathered[half, where, :] = block.reshape(where.size, width)
 
     def step(k, carry):
         both = jnp.concatenate(
@@ -94,10 +98,11 @@
 
     lax.fori_loop(0, rows // UNROLL, several, 0)
 
-    for m in range(ranks):
+    for n, block_ref in enumerate(sends):
+        where = span(n % ranks, n // ranks, sent_parts)
         for half in range(2):
-            block = scattered[half, span(m), :].astype(jnp.bfloat16)
-            sends[m][:, :, halves[half]] = block.reshape(share, rows, width)
+            block = scattered[half, where, :].astype(jnp.bfloat16)
+            block_ref[:, :, halves[half]] = block.reshape(share // sent_parts, rows, width)
 
 
 def gate_kernel(*refs):
@@ -144,13 +149,17 @@
     moves = moves_of(ranks)
     rank = lax.axis_index("seq").astype(jnp.int32).reshape(1)
     params = pltpu.CompilerParams(vmem_limit_bytes=VMEM_LIMIT)
-    buffer = jax.ShapeDtypeStruct((local, local, lanes), jnp.bfloat16)
-
-    def field_spec(q):
-        return pl.BlockSpec((1, blocks * order, width), lambda g, rank: (0, g, q))
-
-    def factor_spec(size):
-        return pl.BlockSpec((size, order, order), lambda g, rank: (g, 0, 0))
+    there = {q: 2 if q == 0 else 1 for q in range(chunks)}
+    back = {q: 2 if q == chunks - 1 else 1 for q in range(chunks)}
+
+    def buffer(parts):
+        return jax.ShapeDtypeStruct((local // parts, local, lanes), jnp.bfloat16)
+
+    def field_spec(q, first=0):
+        return pl.BlockSpec((1, blocks * order, width), lambda g, rank: (0, first + g, q))
+
+    def factor_spec(size, first=0):
+        return pl.BlockSpec((size, order, order), lambda g, rank: (first + g, 0, 0))
 
     token = jax.ShapeDtypeStruct(TOKEN, jnp.float32)
     token_spec = pl.BlockSpec(TOKEN, lambda g, rank: (0, 0))
@@ -158,14 +167,17 @@
     def unread(after):
         return [pl.BlockSpec(memory_space=pl.ANY)] * len(after)
 
-    def left_forward(q, after):
+    def left_forward(q, part, after):
+        steps = local // blocks // there[q]
+        first = part * steps
         return pl.pallas_call(
             functools.partial(left_forward_kernel, ranks),
-            out_shape=[buffer] * ranks + [token],
+            out_shape=[buffer(there[q])] * ranks + [token],
             grid_spec=pltpu.PrefetchScalarGridSpec(
                 num_scalar_prefetch=1,
-                grid=(local // blocks,),
-                in_specs=[field_spec(q), field_spec(q), factor_spec(blocks)] + unread(after),
+                grid=(steps,),
+                in_specs=[field_spec(q, first), field_spec(q, first), factor_spec(blocks, first)]
+                + unread(after),
                 out_specs=[pl.BlockSpec((blocks, local, lanes), lambda g, rank: (g, 0, 0))] * ranks
                 + [token_spec],
             ),
@@ -181,10 +193,15 @@
 
     def right_both(q, arrived, terms, after):
         held = [] if terms is None else [terms]
-        moved = pl.BlockSpec((local, rows, lanes), lambda g, rank: (0, g, 0))
+        ins, outs = there[q], back[q]
+
+        def moved(parts):
+            spec = pl.BlockSpec((local // parts, rows, lanes), lambda g, rank: (0, g, 0))
+            return [spec] * (parts * ranks)
+
         return pl.pallas_call(
-            functools.partial(right_kernel, ranks),
-            out_shape=[buffer] * ranks
+            functools.partial(right_kernel, ranks, ins, outs),
+            out_shape=[buffer(outs)] * (outs * ranks)
             + [jax.ShapeDtypeStruct((row_count, channels), jnp.bfloat16), token],
             grid_spec=pltpu.PrefetchScalarGridSpec(
                 num_scalar_prefetch=1,
@@ -193,17 +210,17 @@
                     pl.BlockSpec((rows * order, width), lambda g, rank: (g, q)),
                     factor_spec(rows),
                 ]
-                + [moved] * ranks
+                + moved(ins)
                 + unread(held)
                 + unread(after),
-                out_specs=[moved] * ranks
+                out_specs=moved(outs)
                 + [pl.BlockSpec((rows * order, width), lambda g, rank: (g, q)), token_spec],
                 scratch_shapes=[
                     pltpu.VMEM((2, order * rows, width), jnp.float32),
                     pltpu.VMEM((2, order * rows, width), jnp.float32),
                 ],
             ),
-            input_output_aliases={3 + ranks: ranks} if held else {},
+            input_output_aliases={3 + ins * ranks: outs * ranks} if held else {},
             compiler_params=params,
             cost_estimate=COST,
         )(rank, kernel, right_factor, *arrived, *held, *after)
@@ -221,8 +238,9 @@
             )(*held, *after)
         )
 
-    def left_back(q, arrived, reduced, outputs, after):
-        steps = local // blocks
+    def left_back(q, part, arrived, reduced, outputs, after):
+        steps = local // blocks // back[q]
+        first = part * steps
         shard = row_count // groups
         out_shape = [
             jax.ShapeDtypeStruct(values.shape, jnp.bfloat16),
@@ -233,7 +251,7 @@
         earlier = list(outputs) if outputs else []
         terms = len(reduced)
         aliases = {4 + ranks + terms + n: n for n in range(len(earlier))}
-        grad_spec = pl.BlockSpec((shard // steps, channels), lambda g, rank: (g, 0))
+        grad_spec = pl.BlockSpec((shard * blocks // local, channels), lambda g, rank: (first + g, 0))
         return pl.pallas_call(
             functools.partial(left_back_kernel, ranks, terms),
             out_shape=out_shape,
@@ -241,17 +259,17 @@
                 num_scalar_prefetch=1,
                 grid=(steps,),
                 in_specs=[
-                    field_spec(q),
-                    field_spec(q),
-                    factor_spec(blocks),
+                    field_spec(q, first),
+                    field_spec(q, first),
+                    factor_spec(blocks, first),
                 ]
                 + [pl.BlockSpec((blocks, local, lanes), lambda g, rank: (g, 0, 0))] * ranks
-                + [pl.BlockSpec((shard // steps, channels), lambda g, rank: (g, 0))] * terms
+                + [grad_spec] * terms
                 + unread(earlier)
                 + unread(after),
                 out_specs=[
-                    field_spec(q),
-                    field_spec(q),
+                    field_spec(q, first),
+                    field_spec(q, first),
                     grad_spec if terms else pl.BlockSpec(memory_space=pl.ANY),
                     token_spec,
                 ],
@@ -262,40 +280,60 @@
         )(rank, values, cotangent, left_factor, *arrived, *reduced, *earlier, *after)
 
     received, sent, returned = {}, {}, {}
-    left_tokens, right_tokens, back_tokens = {}, {}, {}
+    left_tokens, right_tokens, back_tokens = [], {}, {}
     terms, outputs = None, []
 
-    def do_left(q):
-        after = [left_tokens[q - 1]] if q else []
-        if q >= 2:
-            after.append(right_tokens[q - 2])
-        *sends, left_tokens[q] = left_forward(q, after)
-        received[q] = exchange(sends)
+    parts = {}
+    for q in range(chunks):
+        parts[q] = []
+        for part in range(there[q]):
+            *sends, done = left_forward(q, part, left_tokens[-1:])
+            left_tokens.append(done)
+            parts[q].append(sends)
+
+    def send_left(q):
+        received[q] = []
+        for sends in parts[q]:
+            if q == 1:
+                sends[1 + FIRST :] = gate(sends[1 + FIRST :], left_tokens[-1:])
+            if q >= 2:
+                sends[1 + EARLY :] = gate(sends[1 + EARLY :], [right_tokens[q - 2]])
+            received[q] += exchange(sends)
 
     for q in range(min(2, chunks)):
-        do_left(q)
+        send_left(q)
     for q in range(chunks):
         after = [right_tokens[q - 1]] if q else []
         *sent[q], terms, right_tokens[q] = right_both(q, received[q], terms, after)
         if q + 2 < chunks:
-            do_left(q + 2)
+            send_left(q + 2)
 
     def back_step(q):
         last = [reduced] if q == chunks - 1 else []
-        *outputs[:], back_tokens[q] = left_back(q, returned[q], last, outputs, [right_tokens[chunks - 1]])
+        for part in range(back[q]):
+            arrived = returned[q][part * ranks : (part + 1) * ranks]
+            after = [right_tokens[chunks - 1]]
+            *outputs[:], back_tokens[q] = left_back(q, part, arrived, last, outputs, after)
 
     for q in range(chunks):
-        after = []
-        if 1 <= q < chunks - 1:
-            after.append(right_tokens[chunks - 1])
-        if q >= 2:
-            after.append(back_tokens[q - 2])
-        returned[q] = exchange(sent[q][:1] + gate(sent[q][1:], after) if after else sent[q])
+        returned[q] = []
+        for part in range(back[q]):
+            sends = list(sent[q][part * ranks : (part + 1) * ranks])
+            after = []
+            if 1 <= q < chunks - 1:
+                after.append(right_tokens[chunks - 1])
+            if q >= 2:
+                after.append(back_tokens[q - 2 + part])
+            if q == 0 and chunks > 2:
+                sends[1 : 1 + EARLY] = gate(sends[1 : 1 + EARLY], [right_tokens[chunks - 2]])
+            if after:
+                sends[1:] = gate(sends[1:], after)
+            returned[q] += exchange(sends)
+            if q >= 1 and part == 0:
+                back_step(q - 1)
         if q == 0:
             (terms,) = gate([terms], returned[0][1 : 1 + EARLY])
             reduced = lax.psum_scatter(terms, "dp", scatter_dimension=0, tiled=True)
-        if q >= 1:
-            back_step(q - 1)
     back_step(chunks - 1)
     return tuple(outputs)
 

time: 421 us -> 400 us (0.950)
  waiting for transfers between devices: 192 us -> 163 us
  starting transfers between devices: 74.6 us -> 79.7 us
    ppermute x56 -> x70, waiting for transfers between devices: 192 us -> 163 us  [exchange(): lax.ppermute(sends[n], 'seq', [(r, r ^ moves[n]) for r in range(ranks)])]
    ppermute x56 -> x70, starting transfers between devices: 74.5 us -> 79.7 us  [exchange(): lax.ppermute(sends[n], 'seq', [(r, r ^ moves[n]) for r in range(ranks)])]
    pallas_call x4 -> x5, Pallas kernels: 39.6 us -> 40.5 us  [left_back(): pl.pallas_call(functools.partial(left_back_kernel, ranks, terms), out_sha...]
    pallas_call x4 -> x5, Pallas kernels: 33.2 us -> 33.9 us  [left_forward(): pl.pallas_call(functools.partial(left_forward_kernel, ranks), out_shape=[...]
  transfers between devices with their start and end apart: 57 -> 71, of which waited for: 26 -> 28; matrix products, arithmetic and copies ran while one was open for 0% -> 0% of each run, Pallas kernels for 27% -> 31%
where the time goes in v3:
time: 400 us; the launch traced here: 399 us
  waiting for transfers between devices  163 us (41%)
  Pallas kernels  135 us (34%)
  starting transfers between devices  79.7 us (20%)
  between operations  14.8 us (4%)
  local copies, waits for them, and re-layouts  5.84 us (1%)
    ppermute x70, waiting for transfers between devices, exchange(): lax.ppermute(sends[n], 'seq', [(r, r ^ moves[n]) for r in range(ranks)])  163 us
    ppermute x70, starting transfers between devices, exchange(): lax.ppermute(sends[n], 'seq', [(r, r ^ moves[n]) for r in range(ranks)])  79.7 us
    pallas_call x4, Pallas kernels, right_both(): pl.pallas_call(functools.partial(right_kernel, ranks, ins, outs), out_sha...  60.2 us
    pallas_call x5, Pallas kernels, left_back(): pl.pallas_call(functools.partial(left_back_kernel, ranks, terms), out_sha...  40.5 us
    pallas_call x5, Pallas kernels, left_forward(): pl.pallas_call(functools.partial(left_forward_kernel, ranks), out_shape=[...  33.9 us
  transfers between devices with their start and end apart: 71, of which 28 were waited for; matrix products, arithmetic and copies ran while one was open for 0% of the time, Pallas kernels for 31%

profile of v3, /device:TPU:0, one launch (start us, length us, event | category | flops | bytes accessed | tf_op | source)
XLA Modules:
  0.0 398.5 jit_solution(10611811863270424646)
XLA Ops:
  7.2 4.6 %shard_map.76 = (bf16[16,32,256]{2,1,0:T(8,128)(2,1)}, bf16[16,32,256]{2,1,0:T(8,128)(2,1)}, bf16[16,32,256]{2,1,0:T(8,128)(2,1)}, bf16[16,32,256]{2,1,0:T(8,128...) custom-call(s32[1]{0:T(128)} %bitcast.rank_ref, ...), custom_call_target="tpu_custom_call" | custom-call | flops 1024 | bytes 1024 | tf_op jit(solution)/shard_map/pallas_call | solution.py:173
  22.7 7.3 %collective-permute-done.11.refs_2_ = bf16[16,32,256]{2,1,0:T(8,128)(2,1)} collective-permute-done((bf16[16,32,256]{2,1,0:T(8,128)(2,1)}, bf16[16,32,256]{2,1,0:T(8,128)(2,1)}, u32[]{:S(2)}, u32[]{:S(2)}) %collective-permute-start.11) | collective-permute-done | bytes 262176 | tf_op jit(solution)/shard_map/ppermute | solution.py:190
  30.0 4.6 %shard_map.77 = (bf16[16,32,256]{2,1,0:T(8,128)(2,1)}, bf16[16,32,256]{2,1,0:T(8,128)(2,1)}, bf16[16,32,256]{2,1,0:T(8,128)(2,1)}, bf16[16,32,256]{2,1,0:T(8,128...) custom-call(s32[1]{0:T(128)} %bitcast.rank_ref, ...), custom_call_target="tpu_custom_call" | custom-call | flops 1024 | bytes 1024 | tf_op jit(solution)/shard_map/pallas_call | solution.py:173
  45.1 8.3 %shard_map.78 = (bf16[32,32,256]{2,1,0:T(8,128)(2,1)}, bf16[32,32,256]{2,1,0:T(8,128)(2,1)}, bf16[32,32,256]{2,1,0:T(8,128)(2,1)}, bf16[32,32,256]{2,1,0:T(8,128...) custom-call(s32[1]{0:T(128)} %bitcast.rank_ref, ...), custom_call_target="tpu_custom_call" | custom-call | flops 1024 | bytes 1024 | tf_op jit(solution)/shard_map/pallas_call | solution.py:173
  57.4 5.1 %collective-permute-done.21.refs_13_ = bf16[16,32,256]{2,1,0:T(8,128)(2,1)S(1)} collective-permute-done((bf16[16,32,256]{2,1,0:T(8,128)(2,1)}, bf16[16,32,256]{2,1,0:T(8,128)(2,1)S(1)}, u32[]{:S(2)}, u32[]{:S(2)}) %collective-permute-start.21) | collective-permute-done | bytes 262176 | tf_op jit(solution)/shard_map/ppermute | solution.py:190
  63.3 8.3 %shard_map.79 = (bf16[32,32,256]{2,1,0:T(8,128)(2,1)}, bf16[32,32,256]{2,1,0:T(8,128)(2,1)}, bf16[32,32,256]{2,1,0:T(8,128)(2,1)}, bf16[32,32,256]{2,1,0:T(8,128...) custom-call(s32[1]{0:T(128)} %bitcast.rank_ref, ...), custom_call_target="tpu_custom_call" | custom-call | flops 1024 | bytes 1024 | tf_op jit(solution)/shard_map/pallas_call | solution.py:173
  71.6 8.2 %shard_map.80 = (bf16[32,32,256]{2,1,0:T(8,128)(2,1)}, bf16[32,32,256]{2,1,0:T(8,128)(2,1)}, bf16[32,32,256]{2,1,0:T(8,128)(2,1)}, bf16[32,32,256]{2,1,0:T(8,128...) custom-call(s32[1]{0:T(128)} %bitcast.rank_ref, ...), custom_call_target="tpu_custom_call" | custom-call | flops 1024 | bytes 1024 | tf_op jit(solution)/shard_map/pallas_call | solution.py:173
  86.5 9.0 %collective-permute-done.6.refs_4_ = bf16[32,32,256]{2,1,0:T(8,128)(2,1)S(1)} collective-permute-done((bf16[32,32,256]{2,1,0:T(8,128)(2,1)}, bf16[32,32,256]{2,1,0:T(8,128)(2,1)S(1)}, u32[]{:S(2)}, u32[]{:S(2)}) %collective-permute-start.6) | collective-permute-done | bytes 524320 | tf_op jit(solution)/shard_map/ppermute | solution.py:190
  95.5 15.1 %shard_map.82 = (bf16[32,32,256]{2,1,0:T(8,128)(2,1)}, bf16[32,32,256]{2,1,0:T(8,128)(2,1)}, bf16[32,32,256]{2,1,0:T(8,128)(2,1)}, bf16[32,32,256]{2,1,0:T(8,128...) custom-call(s32[1]{0:T(128)} %bitcast.rank_ref, ...), custom_call_target="tpu_custom_call" | custom-call | flops 1024 | bytes 1024 | tf_op jit(solution)/shard_map/pallas_call | solution.py:202
  113.2 15.5 %collective-permute-done.29.refs_2_ = bf16[32,32,256]{2,1,0:T(8,128)(2,1)S(1)} collective-permute-done((bf16[32,32,256]{2,1,0:T(8,128)(2,1)}, bf16[32,32,256]{2,1,0:T(8,128)(2,1)S(1)}, u32[]{:S(2)}, u32[]{:S(2)}) %collective-permute-start.29) | collective-permute-done | bytes 524320 | tf_op jit(solution)/shard_map/ppermute | solution.py:190
  131.7 14.9 %shard_map.83 = (bf16[32,32,256]{2,1,0:T(8,128)(2,1)}, bf16[32,32,256]{2,1,0:T(8,128)(2,1)}, bf16[32,32,256]{2,1,0:T(8,128)(2,1)}, bf16[32,32,256]{2,1,0:T(8,128...) custom-call(s32[1]{0:T(128)} %bitcast.rank_ref, ...), custom_call_target="tpu_custom_call", output_to_operand_aliasing={{8}: (11, {})} | custom-call | flops 1024 | bytes 1024 | tf_op jit(solution)/shard_map/pallas_call | solution.py:202
  149.3 4.6 %collective-permute-done.32.refs_5_ = bf16[32,32,256]{2,1,0:T(8,128)(2,1)S(1)} collective-permute-done((bf16[32,32,256]{2,1,0:T(8,128)(2,1)}, bf16[32,32,256]{2,1,0:T(8,128)(2,1)S(1)}, u32[]{:S(2)}, u32[]{:S(2)}) %collective-permute-start.32) | collective-permute-done | bytes 524320 | tf_op jit(solution)/shard_map/ppermute | solution.py:190
  158.2 14.9 %shard_map.86 = (bf16[32,32,256]{2,1,0:T(8,128)(2,1)}, bf16[32,32,256]{2,1,0:T(8,128)(2,1)}, bf16[32,32,256]{2,1,0:T(8,128)(2,1)}, bf16[32,32,256]{2,1,0:T(8,128...) custom-call(s32[1]{0:T(128)} %bitcast.rank_ref, ...), custom_call_target="tpu_custom_call", output_to_operand_aliasing={{8}: (11, {})} | custom-call | flops 1024 | bytes 1024 | tf_op jit(solution)/shard_map/pallas_call | solution.py:202
  178.8 6.3 %collective-permute-done.24.refs_4_ = bf16[32,32,256]{2,1,0:T(8,128)(2,1)S(1)} collective-permute-done((bf16[32,32,256]{2,1,0:T(8,128)(2,1)}, bf16[32,32,256]{2,1,0:T(8,128)(2,1)S(1)}, u32[]{:S(2)}, u32[]{:S(2)}) %collective-permute-start.24) | collective-permute-done | bytes 524320 | tf_op jit(solution)/shard_map/ppermute | solution.py:190
  186.5 12.4 %collective-permute-done.25.refs_5_ = bf16[32,32,256]{2,1,0:T(8,128)(2,1)} collective-permute-done((bf16[32,32,256]{2,1,0:T(8,128)(2,1)}, bf16[32,32,256]{2,1,0:T(8,128)(2,1)}, u32[]{:S(2)}, u32[]{:S(2)}) %collective-permute-start.25) | collective-permute-done | bytes 524320 | tf_op jit(solution)/shard_map/ppermute | solution.py:190
  202.2 15.3 %shard_map.87 = (bf16[16,32,256]{2,1,0:T(8,128)(2,1)}, bf16[16,32,256]{2,1,0:T(8,128)(2,1)}, bf16[16,32,256]{2,1,0:T(8,128)(2,1)}, bf16[16,32,256]{2,1,0:T(8,128...) custom-call(s32[1]{0:T(128)} %bitcast.rank_ref, ...), custom_call_target="tpu_custom_call", output_to_operand_aliasing={{16}: (11, {})} | custom-call | flops 1024 | bytes 1024 | tf_op jit(solution)/shard_map/pallas_call | solution.py:202
  217.5 4.3 %collective-permute-done.36.refs_2_ = bf16[32,32,256]{2,1,0:T(8,128)(2,1)S(1)} collective-permute-done((bf16[32,32,256]{2,1,0:T(8,128)(2,1)}, bf16[32,32,256]{2,1,0:T(8,128)(2,1)S(1)}, u32[]{:S(2)}, u32[]{:S(2)}) %collective-permute-start.36) | collective-permute-done | bytes 524320 | tf_op jit(solution)/shard_map/ppermute | solution.py:190
  228.0 9.0 %collective-permute-done.38.refs_4_ = bf16[32,32,256]{2,1,0:T(8,128)(2,1)S(1)} collective-permute-done((bf16[32,32,256]{2,1,0:T(8,128)(2,1)}, bf16[32,32,256]{2,1,0:T(8,128)(2,1)S(1)}, u32[]{:S(2)}, u32[]{:S(2)}) %collective-permute-start.38) | collective-permute-done | bytes 524320 | tf_op jit(solution)/shard_map/ppermute | solution.py:190
  239.1 10.1 %collective-permute-done.39.refs_5_ = bf16[32,32,256]{2,1,0:T(8,128)(2,1)S(1)} collective-permute-done((bf16[32,32,256]{2,1,0:T(8,128)(2,1)S(1)}, bf16[32,32,256]{2,1,0:T(8,128)(2,1)S(1)}, u32[]{:S(2)}, u32[]{:S(2)}) %collective-permute-start.39) | collective-permute-done | bytes 524320 | tf_op jit(solution)/shard_map/ppermute | solution.py:190
  254.3 9.4 %shard_map.89 = (bf16[1,8192,512]{2,1,0:T(8,128)(2,1)}, bf16[1,8192,512]{2,1,0:T(8,128)(2,1)}, f32[2048,512]{1,0:T(8,128)}, f32[8,128]{1,0:T(8,128)}) custom-call(s32[1]{0:T(128)} %bitcast.rank_ref, bf16[1,8192,512]{2,1,0:T(8,128)(2,1)} %values_ref.19, bf16[1,8192,512]{2,1,0:T(8,128)(2,1)} %cotangent_ref.19, bf16[32,256,256]{2,1,0:T(8,128)(2,1)} %left_ref.19, ...), custom_call_target="tpu_custom_call" | custom-call | flops 1024 | bytes 1024 | tf_op jit(solution)/shard_map/pallas_call | solution.py:255
  265.6 6.1 %collective-permute-done.50.refs_2_ = bf16[32,32,256]{2,1,0:T(8,128)(2,1)S(1)} collective-permute-done((bf16[32,32,256]{2,1,0:T(8,128)(2,1)}, bf16[32,32,256]{2,1,0:T(8,128)(2,1)S(1)}, u32[]{:S(2)}, u32[]{:S(2)}) %collective-permute-start.50) | collective-permute-done | bytes 524320 | tf_op jit(solution)/shard_map/ppermute | solution.py:190
  273.8 8.3 %collective-permute-done.52.refs_4_ = bf16[32,32,256]{2,1,0:T(8,128)(2,1)S(1)} collective-permute-done((bf16[32,32,256]{2,1,0:T(8,128)(2,1)}, bf16[32,32,256]{2,1,0:T(8,128)(2,1)S(1)}, u32[]{:S(2)}, u32[]{:S(2)}) %collective-permute-start.52) | collective-permute-done | bytes 524320 | tf_op jit(solution)/shard_map/ppermute | solution.py:190
  284.1 10.1 %collective-permute-done.53.refs_5_ = bf16[32,32,256]{2,1,0:T(8,128)(2,1)S(1)} collective-permute-done((bf16[32,32,256]{2,1,0:T(8,128)(2,1)}, bf16[32,32,256]{2,1,0:T(8,128)(2,1)S(1)}, u32[]{:S(2)}, u32[]{:S(2)}) %collective-permute-start.53) | collective-permute-done | bytes 524320 | tf_op jit(solution)/shard_map/ppermute | solution.py:190
  298.4 6.8 %collective-permute-done.42.refs_1_ = bf16[32,32,256]{2,1,0:T(8,128)(2,1)S(1)} collective-permute-done((bf16[32,32,256]{2,1,0:T(8,128)(2,1)}, bf16[32,32,256]{2,1,0:T(8,128)(2,1)S(1)}, u32[]{:S(2)}, u32[]{:S(2)}) %collective-permute-start.42) | collective-permute-done | bytes 524320 | tf_op jit(solution)/shard_map/ppermute | solution.py:190
  306.3 10.4 %collective-permute-done.43.refs_2_ = bf16[32,32,256]{2,1,0:T(8,128)(2,1)S(1)} collective-permute-done((bf16[32,32,256]{2,1,0:T(8,128)(2,1)}, bf16[32,32,256]{2,1,0:T(8,128)(2,1)S(1)}, u32[]{:S(2)}, u32[]{:S(2)}) %collective-permute-start.43) | collective-permute-done | bytes 524320 | tf_op jit(solution)/shard_map/ppermute | solution.py:190
  316.7 9.5 %shard_map.92 = (bf16[1,8192,512]{2,1,0:T(8,128)(2,1)}, bf16[1,8192,512]{2,1,0:T(8,128)(2,1)}, f32[2048,512]{1,0:T(8,128)}, f32[8,128]{1,0:T(8,128)}) custom-call(s32[1]{0:T(128)} %bitcast.rank_ref, bf16[1,8192,512]{2,1,0:T(8,128)(2,1)} %values_ref.19, ...), custom_call_target="tpu_custom_call", output_to_operand_aliasing={{0}: (12, {}), {1}: (13, {}), {2}: (14, {})} | custom-call | flops 1024 | bytes 1024 | tf_op jit(solution)/shard_map/pallas_call | solution.py:255
  329.4 9.8 %collective-permute-done.46.refs_5_ = bf16[32,32,256]{2,1,0:T(8,128)(2,1)} collective-permute-done((bf16[32,32,256]{2,1,0:T(8,128)(2,1)}, bf16[32,32,256]{2,1,0:T(8,128)(2,1)}, u32[]{:S(2)}, u32[]{:S(2)}) %collective-permute-start.46) | collective-permute-done | bytes 524320 | tf_op jit(solution)/shard_map/ppermute | solution.py:190
  342.6 9.5 %shard_map.93 = (bf16[1,8192,512]{2,1,0:T(8,128)(2,1)}, bf16[1,8192,512]{2,1,0:T(8,128)(2,1)}, f32[2048,512]{1,0:T(8,128)}, f32[8,128]{1,0:T(8,128)}) custom-call(s32[1]{0:T(128)} %bitcast.rank_ref, bf16[1,8192,512]{2,1,0:T(8,128)(2,1)} %values_ref.19, ...), custom_call_target="tpu_custom_call", output_to_operand_aliasing={{0}: (12, {}), {1}: (13, {}), {2}: (14, {})} | custom-call | flops 1024 | bytes 1024 | tf_op jit(solution)/shard_map/pallas_call | solution.py:255
  368.3 3.9 collective-permute-done.57.refs_2_
  372.3 6.0 %shard_map.97 = (bf16[1,8192,512]{2,1,0:T(8,128)(2,1)}, bf16[1,8192,512]{2,1,0:T(8,128)(2,1)}, f32[2048,512]{1,0:T(8,128)}, f32[8,128]{1,0:T(8,128)}) custom-call(s32[1]{0:T(128)} %bitcast.rank_ref, bf16[1,8192,512]{2,1,0:T(8,128)(2,1)} %values_ref.19, ...), custom_call_target="tpu_custom_call", output_to_operand_aliasing={{0}: (13, {}), {1}: (14, {}), {2}: (15, {})} | custom-call | flops 1024 | bytes 1024 | tf_op jit(solution)/shard_map/pallas_call | solution.py:255
  378.4 5.4 %collective-permute-done.60.refs_5_ = bf16[16,32,256]{2,1,0:T(8,128)(2,1)S(1)} collective-permute-done((bf16[16,32,256]{2,1,0:T(8,128)(2,1)}, bf16[16,32,256]{2,1,0:T(8,128)(2,1)S(1)}, u32[]{:S(2)}, u32[]{:S(2)}) %collective-permute-start.60) | collective-permute-done | bytes 262176 | tf_op jit(solution)/shard_map/ppermute | solution.py:190
  385.6 6.0 %shard_map.98 = (bf16[1,8192,512]{2,1,0:T(8,128)(2,1)}, bf16[1,8192,512]{2,1,0:T(8,128)(2,1)}, f32[2048,512]{1,0:T(8,128)}, f32[8,128]{1,0:T(8,128)}) custom-call(s32[1]{0:T(128)} %bitcast.rank_ref, bf16[1,8192,512]{2,1,0:T(8,128)(2,1)} %values_ref.19, ...), custom_call_target="tpu_custom_call", output_to_operand_aliasing={{0}: (13, {}), {1}: (14, {}), {2}: (15, {})} | custom-call | flops 1024 | bytes 1024 | tf_op jit(solution)/shard_map/pallas_call | solution.py:255
  (256 shorter events, 104.6 us)
Async XLA Ops:
  7.2 365.0 %reduce-scatter.2.cloned.1.call-start = ((), (), s32[]{:S(2)}) async-start(), calls=%async_computation.1 | async-start | bytes 10485760 | tf_op jit(solution)/shard_map/reduce_scatter | solution.py:336
  53.5 28.6 %collective-permute-start.3 = (bf16[32,32,256]{2,1,0:T(8,128)(2,1)}, bf16[32,32,256]{2,1,0:T(8,128)(2,1)S(1)}, u32[]{:S(2)}, u32[]{:S(2)}) collective-permute-start(bf16[32,32,256]{2,1,0:T(8,128)(2,1)} %get-tuple-element.168), channel_id=1, source_target_pairs={{0,2},{1,3},{2,0},{3,1},{4,6},{5,7},{6,4},{7,5},{8,10},{9,11},{10,... | collective-permute-start | bytes 1572872 | tf_op jit(solution)/shard_map/ppermute | solution.py:190
  55.3 28.8 %collective-permute-start.4 = (bf16[32,32,256]{2,1,0:T(8,128)(2,1)}, bf16[32,32,256]{2,1,0:T(8,128)(2,1)S(1)}, u32[]{:S(2)}, u32[]{:S(2)}) collective-permute-start(bf16[32,32,256]{2,1,0:T(8,128)(2,1)} %get-tuple-element.169), channel_id=1, source_target_pairs={{0,4},{1,5},{2,6},{3,7},{4,0},{5,1},{6,2},{7,3},{8,12},{9,13},{10,... | collective-permute-start | bytes 1572872 | tf_op jit(solution)/shard_map/ppermute | solution.py:190
  56.8 29.6 %collective-permute-start.5 = (bf16[32,32,256]{2,1,0:T(8,128)(2,1)}, bf16[32,32,256]{2,1,0:T(8,128)(2,1)S(1)}, u32[]{:S(2)}, u32[]{:S(2)}) collective-permute-start(bf16[32,32,256]{2,1,0:T(8,128)(2,1)} %get-tuple-element.170), channel_id=1, source_target_pairs={{0,6},{1,7},{2,4},{3,5},{4,2},{5,3},{6,0},{7,1},{8,14},{9,15},{10,... | collective-permute-start | bytes 1572872 | tf_op jit(solution)/shard_map/ppermute | solution.py:190
  63.2 32.3 %collective-permute-start.6 = (bf16[32,32,256]{2,1,0:T(8,128)(2,1)}, bf16[32,32,256]{2,1,0:T(8,128)(2,1)S(1)}, u32[]{:S(2)}, u32[]{:S(2)}) collective-permute-start(bf16[32,32,256]{2,1,0:T(8,128)(2,1)} %get-tuple-element.171), channel_id=1, source_target_pairs={{0,3},{1,2},{2,1},{3,0},{4,7},{5,6},{6,5},{7,4},{8,11},{9,10},{10,... | collective-permute-start | bytes 1572872 | tf_op jit(solution)/shard_map/ppermute | solution.py:190
  79.8 30.8 %collective-permute-start.7 = (bf16[32,32,256]{2,1,0:T(8,128)(2,1)}, bf16[32,32,256]{2,1,0:T(8,128)(2,1)S(1)}, u32[]{:S(2)}, u32[]{:S(2)}) collective-permute-start(bf16[32,32,256]{2,1,0:T(8,128)(2,1)} %get-tuple-element.172), channel_id=1, source_target_pairs={{0,5},{1,4},{2,7},{3,6},{4,1},{5,0},{6,3},{7,2},{8,13},{9,12},{10,... | collective-permute-start | bytes 1572872 | tf_op jit(solution)/shard_map/ppermute | solution.py:190
  82.0 31.2 %collective-permute-start.28 = (bf16[32,32,256]{2,1,0:T(8,128)(2,1)}, bf16[32,32,256]{2,1,0:T(8,128)(2,1)S(1)}, u32[]{:S(2)}, u32[]{:S(2)}) collective-permute-start(bf16[32,32,256]{2,1,0:T(8,128)(2,1)} %get-tuple-element.202), channel_id=1, source_target_pairs={{0,2},{1,3},{2,0},{3,1},{4,6},{5,7},{6,4},{7,5},{8,10},{9,11},{10,... | collective-permute-start | bytes 1572872 | tf_op jit(solution)/shard_map/ppermute | solution.py:190
  84.1 44.6 %collective-permute-start.29 = (bf16[32,32,256]{2,1,0:T(8,128)(2,1)}, bf16[32,32,256]{2,1,0:T(8,128)(2,1)S(1)}, u32[]{:S(2)}, u32[]{:S(2)}) collective-permute-start(bf16[32,32,256]{2,1,0:T(8,128)(2,1)} %get-tuple-element.203), channel_id=1, source_target_pairs={{0,4},{1,5},{2,6},{3,7},{4,0},{5,1},{6,2},{7,3},{8,12},{9,13},{10,... | collective-permute-start | bytes 1572872 | tf_op jit(solution)/shard_map/ppermute | solution.py:190
  86.5 43.8 %collective-permute-start.8 = (bf16[32,32,256]{2,1,0:T(8,128)(2,1)}, bf16[32,32,256]{2,1,0:T(8,128)(2,1)}, u32[]{:S(2)}, u32[]{:S(2)}) collective-permute-start(bf16[32,32,256]{2,1,0:T(8,128)(2,1)} %get-tuple-element.176), channel_id=1, source_target_pairs={{0,7},{1,6},{2,5},{3,4},{4,3},{5,2},{6,1},{7,0},{8,15},{9,14},{10,... | collective-permute-start | bytes 1572872 | tf_op jit(solution)/shard_map/ppermute | solution.py:190
  95.5 36.1 %collective-permute-start.9 = (bf16[32,32,256]{2,1,0:T(8,128)(2,1)}, bf16[32,32,256]{2,1,0:T(8,128)(2,1)}, u32[]{:S(2)}, u32[]{:S(2)}) collective-permute-start(bf16[32,32,256]{2,1,0:T(8,128)(2,1)} %get-tuple-element.177), channel_id=1, source_target_pairs={{0,1},{1,0},{2,3},{3,2},{4,5},{5,4},{6,7},{7,6},{8,9},{9,8},{10,11... | collective-permute-start | bytes 1572872 | tf_op jit(solution)/shard_map/ppermute | solution.py:190
  110.7 36.0 %collective-permute-start.30 = (bf16[32,32,256]{2,1,0:T(8,128)(2,1)}, bf16[32,32,256]{2,1,0:T(8,128)(2,1)S(1)}, u32[]{:S(2)}, u32[]{:S(2)}) collective-permute-start(bf16[32,32,256]{2,1,0:T(8,128)(2,1)} %get-tuple-element.204), channel_id=1, source_target_pairs={{0,6},{1,7},{2,4},{3,5},{4,2},{5,3},{6,0},{7,1},{8,14},{9,15},{10,... | collective-permute-start | bytes 1572872 | tf_op jit(solution)/shard_map/ppermute | solution.py:190
  113.2 34.5 %collective-permute-start.31 = (bf16[32,32,256]{2,1,0:T(8,128)(2,1)}, bf16[32,32,256]{2,1,0:T(8,128)(2,1)S(1)}, u32[]{:S(2)}, u32[]{:S(2)}) collective-permute-start(bf16[32,32,256]{2,1,0:T(8,128)(2,1)} %get-tuple-element.209), channel_id=1, source_target_pairs={{0,3},{1,2},{2,1},{3,0},{4,7},{5,6},{6,5},{7,4},{8,11},{9,10},{10,... | collective-permute-start | bytes 1572872 | tf_op jit(solution)/shard_map/ppermute | solution.py:190
  130.3 27.6 %collective-permute-start.33 = (bf16[32,32,256]{2,1,0:T(8,128)(2,1)}, bf16[32,32,256]{2,1,0:T(8,128)(2,1)}, u32[]{:S(2)}, u32[]{:S(2)}) collective-permute-start(bf16[32,32,256]{2,1,0:T(8,128)(2,1)} %get-tuple-element.211), channel_id=1, source_target_pairs={{0,7},{1,6},{2,5},{3,4},{4,3},{5,2},{6,1},{7,0},{8,15},{9,14},{10,... | collective-permute-start | bytes 1572872 | tf_op jit(solution)/shard_map/ppermute | solution.py:190
  147.7 30.0 %collective-permute-start.1 = (bf16[32,32,256]{2,1,0:T(8,128)(2,1)}, bf16[32,32,256]{2,1,0:T(8,128)(2,1)S(1)}, u32[]{:S(2)}, u32[]{:S(2)}) collective-permute-start(bf16[32,32,256]{2,1,0:T(8,128)(2,1)} %get-tuple-element.161), channel_id=1, source_target_pairs={{0,4},{1,5},{2,6},{3,7},{4,0},{5,1},{6,2},{7,3},{8,12},{9,13},{10,... | collective-permute-start | bytes 1572872 | tf_op jit(solution)/shard_map/ppermute | solution.py:190
  157.9 27.2 %collective-permute-start.24 = (bf16[32,32,256]{2,1,0:T(8,128)(2,1)}, bf16[32,32,256]{2,1,0:T(8,128)(2,1)S(1)}, u32[]{:S(2)}, u32[]{:S(2)}) collective-permute-start(bf16[32,32,256]{2,1,0:T(8,128)(2,1)} %get-tuple-element.197), channel_id=1, source_target_pairs={{0,3},{1,2},{2,1},{3,0},{4,7},{5,6},{6,5},{7,4},{8,11},{9,10},{10,... | collective-permute-start | bytes 1572872 | tf_op jit(solution)/shard_map/ppermute | solution.py:190
  158.1 40.9 %collective-permute-start.25 = (bf16[32,32,256]{2,1,0:T(8,128)(2,1)}, bf16[32,32,256]{2,1,0:T(8,128)(2,1)}, u32[]{:S(2)}, u32[]{:S(2)}) collective-permute-start(bf16[32,32,256]{2,1,0:T(8,128)(2,1)} %get-tuple-element.198), channel_id=1, source_target_pairs={{0,5},{1,4},{2,7},{3,6},{4,1},{5,0},{6,3},{7,2},{8,13},{9,12},{10,... | collective-permute-start | bytes 1572872 | tf_op jit(solution)/shard_map/ppermute | solution.py:190
  173.2 29.0 %collective-permute-start.26 = (bf16[32,32,256]{2,1,0:T(8,128)(2,1)}, bf16[32,32,256]{2,1,0:T(8,128)(2,1)}, u32[]{:S(2)}, u32[]{:S(2)}) collective-permute-start(bf16[32,32,256]{2,1,0:T(8,128)(2,1)} %get-tuple-element.199), channel_id=1, source_target_pairs={{0,7},{1,6},{2,5},{3,4},{4,3},{5,2},{6,1},{7,0},{8,15},{9,14},{10,... | collective-permute-start | bytes 1572872 | tf_op jit(solution)/shard_map/ppermute | solution.py:190
  177.7 39.7 %collective-permute-start.35 = (bf16[32,32,256]{2,1,0:T(8,128)(2,1)}, bf16[32,32,256]{2,1,0:T(8,128)(2,1)S(1)}, u32[]{:S(2)}, u32[]{:S(2)}) collective-permute-start(bf16[32,32,256]{2,1,0:T(8,128)(2,1)} %get-tuple-element.237), channel_id=1, source_target_pairs={{0,2},{1,3},{2,0},{3,1},{4,6},{5,7},{6,4},{7,5},{8,10},{9,11},{10,... | collective-permute-start | bytes 1572872 | tf_op jit(solution)/shard_map/ppermute | solution.py:190
  185.1 36.7 %collective-permute-start.36 = (bf16[32,32,256]{2,1,0:T(8,128)(2,1)}, bf16[32,32,256]{2,1,0:T(8,128)(2,1)S(1)}, u32[]{:S(2)}, u32[]{:S(2)}) collective-permute-start(bf16[32,32,256]{2,1,0:T(8,128)(2,1)} %get-tuple-element.238), channel_id=1, source_target_pairs={{0,4},{1,5},{2,6},{3,7},{4,0},{5,1},{6,2},{7,3},{8,12},{9,13},{10,... | collective-permute-start | bytes 1572872 | tf_op jit(solution)/shard_map/ppermute | solution.py:190
  226.8 26.6 %collective-permute-start.41 = (bf16[32,32,256]{2,1,0:T(8,128)(2,1)}, bf16[32,32,256]{2,1,0:T(8,128)(2,1)S(1)}, u32[]{:S(2)}, u32[]{:S(2)}) collective-permute-start(bf16[32,32,256]{2,1,0:T(8,128)(2,1)} %get-tuple-element.243), channel_id=1, source_target_pairs={{0,1},{1,0},{2,3},{3,2},{4,5},{5,4},{6,7},{7,6},{8,9},{9,8},{10,11... | collective-permute-start | bytes 1572872 | tf_op jit(solution)/shard_map/ppermute | solution.py:190
  226.8 36.9 %collective-permute-start.49 = (bf16[32,32,256]{2,1,0:T(8,128)(2,1)}, bf16[32,32,256]{2,1,0:T(8,128)(2,1)S(1)}, u32[]{:S(2)}, u32[]{:S(2)}) collective-permute-start(bf16[32,32,256]{2,1,0:T(8,128)(2,1)} %get-tuple-element.260), channel_id=1, source_target_pairs={{0,2},{1,3},{2,0},{3,1},{4,6},{5,7},{6,4},{7,5},{8,10},{9,11},{10,... | collective-permute-start | bytes 1572872 | tf_op jit(solution)/shard_map/ppermute | solution.py:190
  237.1 34.7 %collective-permute-start.50 = (bf16[32,32,256]{2,1,0:T(8,128)(2,1)}, bf16[32,32,256]{2,1,0:T(8,128)(2,1)S(1)}, u32[]{:S(2)}, u32[]{:S(2)}) collective-permute-start(bf16[32,32,256]{2,1,0:T(8,128)(2,1)} %get-tuple-element.261), channel_id=1, source_target_pairs={{0,4},{1,5},{2,6},{3,7},{4,0},{5,1},{6,2},{7,3},{8,12},{9,13},{10,... | collective-permute-start | bytes 1572872 | tf_op jit(solution)/shard_map/ppermute | solution.py:190
  250.9 31.2 %collective-permute-start.52 = (bf16[32,32,256]{2,1,0:T(8,128)(2,1)}, bf16[32,32,256]{2,1,0:T(8,128)(2,1)S(1)}, u32[]{:S(2)}, u32[]{:S(2)}) collective-permute-start(bf16[32,32,256]{2,1,0:T(8,128)(2,1)} %get-tuple-element.263), channel_id=1, source_target_pairs={{0,3},{1,2},{2,1},{3,0},{4,7},{5,6},{6,5},{7,4},{8,11},{9,10},{10,... | collective-permute-start | bytes 1572872 | tf_op jit(solution)/shard_map/ppermute | solution.py:190
  254.3 39.9 %collective-permute-start.53 = (bf16[32,32,256]{2,1,0:T(8,128)(2,1)}, bf16[32,32,256]{2,1,0:T(8,128)(2,1)S(1)}, u32[]{:S(2)}, u32[]{:S(2)}) collective-permute-start(bf16[32,32,256]{2,1,0:T(8,128)(2,1)} %get-tuple-element.264), channel_id=1, source_target_pairs={{0,5},{1,4},{2,7},{3,6},{4,1},{5,0},{6,3},{7,2},{8,13},{9,12},{10,... | collective-permute-start | bytes 1572872 | tf_op jit(solution)/shard_map/ppermute | solution.py:190
  263.7 32.0 %collective-permute-start.54 = (bf16[32,32,256]{2,1,0:T(8,128)(2,1)}, bf16[32,32,256]{2,1,0:T(8,128)(2,1)S(1)}, u32[]{:S(2)}, u32[]{:S(2)}) collective-permute-start(bf16[32,32,256]{2,1,0:T(8,128)(2,1)} %get-tuple-element.265), channel_id=1, source_target_pairs={{0,7},{1,6},{2,5},{3,4},{4,3},{5,2},{6,1},{7,0},{8,15},{9,14},{10,... | collective-permute-start | bytes 1572872 | tf_op jit(solution)/shard_map/ppermute | solution.py:190
  271.8 26.7 %collective-permute-start.55 = (bf16[32,32,256]{2,1,0:T(8,128)(2,1)}, bf16[32,32,256]{2,1,0:T(8,128)(2,1)S(1)}, u32[]{:S(2)}, u32[]{:S(2)}) collective-permute-start(bf16[32,32,256]{2,1,0:T(8,128)(2,1)} %get-tuple-element.266), channel_id=1, source_target_pairs={{0,1},{1,0},{2,3},{3,2},{4,5},{5,4},{6,7},{7,6},{8,9},{9,8},{10,11... | collective-permute-start | bytes 1572872 | tf_op jit(solution)/shard_map/ppermute | solution.py:190
  272.9 32.3 %collective-permute-start.42 = (bf16[32,32,256]{2,1,0:T(8,128)(2,1)}, bf16[32,32,256]{2,1,0:T(8,128)(2,1)S(1)}, u32[]{:S(2)}, u32[]{:S(2)}) collective-permute-start(bf16[32,32,256]{2,1,0:T(8,128)(2,1)} %get-tuple-element.245), channel_id=1, source_target_pairs={{0,2},{1,3},{2,0},{3,1},{4,6},{5,7},{6,4},{7,5},{8,10},{9,11},{10,... | collective-permute-start | bytes 1572872 | tf_op jit(solution)/shard_map/ppermute | solution.py:190
  282.1 34.6 %collective-permute-start.43 = (bf16[32,32,256]{2,1,0:T(8,128)(2,1)}, bf16[32,32,256]{2,1,0:T(8,128)(2,1)S(1)}, u32[]{:S(2)}, u32[]{:S(2)}) collective-permute-start(bf16[32,32,256]{2,1,0:T(8,128)(2,1)} %get-tuple-element.246), channel_id=1, source_target_pairs={{0,4},{1,5},{2,6},{3,7},{4,0},{5,1},{6,2},{7,3},{8,12},{9,13},{10,... | collective-permute-start | bytes 1572872 | tf_op jit(solution)/shard_map/ppermute | solution.py:190
  295.0 31.3 %collective-permute-start.44 = (bf16[32,32,256]{2,1,0:T(8,128)(2,1)}, bf16[32,32,256]{2,1,0:T(8,128)(2,1)S(1)}, u32[]{:S(2)}, u32[]{:S(2)}) collective-permute-start(bf16[32,32,256]{2,1,0:T(8,128)(2,1)} %get-tuple-element.247), channel_id=1, source_target_pairs={{0,6},{1,7},{2,4},{3,5},{4,2},{5,3},{6,0},{7,1},{8,14},{9,15},{10,... | collective-permute-start | bytes 1572872 | tf_op jit(solution)/shard_map/ppermute | solution.py:190
  295.8 32.6 %collective-permute-start.45 = (bf16[32,32,256]{2,1,0:T(8,128)(2,1)}, bf16[32,32,256]{2,1,0:T(8,128)(2,1)}, u32[]{:S(2)}, u32[]{:S(2)}) collective-permute-start(bf16[32,32,256]{2,1,0:T(8,128)(2,1)} %get-tuple-element.248), channel_id=1, source_target_pairs={{0,3},{1,2},{2,1},{3,0},{4,7},{5,6},{6,5},{7,4},{8,11},{9,10},{10,... | collective-permute-start | bytes 1572872 | tf_op jit(solution)/shard_map/ppermute | solution.py:190
  298.4 40.7 %collective-permute-start.46 = (bf16[32,32,256]{2,1,0:T(8,128)(2,1)}, bf16[32,32,256]{2,1,0:T(8,128)(2,1)}, u32[]{:S(2)}, u32[]{:S(2)}) collective-permute-start(bf16[32,32,256]{2,1,0:T(8,128)(2,1)} %get-tuple-element.249), channel_id=1, source_target_pairs={{0,5},{1,4},{2,7},{3,6},{4,1},{5,0},{6,3},{7,2},{8,13},{9,12},{10,... | collective-permute-start | bytes 1572872 | tf_op jit(solution)/shard_map/ppermute | solution.py:190
  305.2 34.8 %collective-permute-start.47 = (bf16[32,32,256]{2,1,0:T(8,128)(2,1)}, bf16[32,32,256]{2,1,0:T(8,128)(2,1)}, u32[]{:S(2)}, u32[]{:S(2)}) collective-permute-start(bf16[32,32,256]{2,1,0:T(8,128)(2,1)} %get-tuple-element.250), channel_id=1, source_target_pairs={{0,7},{1,6},{2,5},{3,4},{4,3},{5,2},{6,1},{7,0},{8,15},{9,14},{10,... | collective-permute-start | bytes 1572872 | tf_op jit(solution)/shard_map/ppermute | solution.py:190
  (100 other events, 1632.3 us)
Sparse Core Ops, SparseCore 0:
  223.0 145.1 reduce-scatter.1

commit v4 on v3

--- a/solution.py
+++ b/solution.py
@@ -13,12 +13,13 @@
 COST = pl.CostEstimate(flops=1024, bytes_accessed=1024, transcendentals=0)
 FIRST = 5
 EARLY = 3
-UNROLL = 4
+UNROLL = 8
 TOKEN = (8, 128)
 
 
 def moves_of(ranks):
-    return [0] + list(range(2, ranks, 2)) + list(range(3, ranks, 2)) + [1]
+    far, near = list(range(ranks - 2, ranks)), list(range(2, ranks - 2))
+    return [0, far[0]] + near[::2] + [far[1]] + near[1::2] + [1]
 
 
 def left_forward_kernel(ranks, rank_ref, values_ref, cotangent_ref, left_ref, *refs):
@@ -143,7 +144,7 @@
     local, order, _ = left_factor.shape
     width = WIDTH
     lanes = 2 * width
-    blocks = min(4, local)
+    blocks = min(8, local // 2)
     rows = min(ROWS, local)
     chunks = channels // width
     moves = moves_of(ranks)
@@ -251,7 +252,7 @@
         earlier = list(outputs) if outputs else []
         terms = len(reduced)
         aliases = {4 + ranks + terms + n: n for n in range(len(earlier))}
-        grad_spec = pl.BlockSpec((shard * blocks // local, channels), lambda g, rank: (first + g, 0))
+        grad_spec = pl.BlockSpec((shard // steps, channels), lambda g, rank: (g, 0))
         return pl.pallas_call(
             functools.partial(left_back_kernel, ranks, terms),
             out_shape=out_shape,
@@ -314,6 +315,7 @@
             arrived = returned[q][part * ranks : (part + 1) * ranks]
             after = [right_tokens[chunks - 1]]
             *outputs[:], back_tokens[q] = left_back(q, part, arrived, last, outputs, after)
+            last = []
 
     for q in range(chunks):
         returned[q] = []

time: 400 us -> 393 us (0.983)
  waiting for transfers between devices: 163 us -> 188 us
  Pallas kernels: 135 us -> 112 us
  starting transfers between devices: 79.7 us -> 72.1 us
    ppermute x70, waiting for transfers between devices: 163 us -> 188 us  [exchange(): lax.ppermute(sends[n], 'seq', [(r, r ^ moves[n]) for r in range(ranks)])]
    ppermute x70, starting transfers between devices: 79.7 us -> 72 us  [exchange(): lax.ppermute(sends[n], 'seq', [(r, r ^ moves[n]) for r in range(ranks)])]
    pallas_call x5, Pallas kernels: 40.5 us -> 32.9 us  [left_back(): pl.pallas_call(functools.partial(left_back_kernel, ranks, terms), out_sha...]
    pallas_call x4, Pallas kernels: 60.2 us -> 52.6 us  [right_both(): pl.pallas_call(functools.partial(right_kernel, ranks, ins, outs), out_sha...]
    pallas_call x5, Pallas kernels: 33.9 us -> 26.7 us  [left_forward(): pl.pallas_call(functools.partial(left_forward_kernel, ranks), out_shape=[...]
  transfers between devices with their start and end apart: 71 -> 71, of which waited for: 28 -> 31; matrix products, arithmetic and copies ran while one was open for 0% -> 0% of each run, Pallas kernels for 31% -> 27%
where the time goes in v4:
time: 393 us
  waiting for transfers between devices  188 us (48%)
  Pallas kernels  112 us (28%)
  starting transfers between devices  72.1 us (18%)
  between operations  14.7 us (4%)
  local copies, waits for them, and re-layouts  5.85 us (1%)
    ppermute x70, waiting for transfers between devices, exchange(): lax.ppermute(sends[n], 'seq', [(r, r ^ moves[n]) for r in range(ranks)])  188 us
    ppermute x70, starting transfers between devices, exchange(): lax.ppermute(sends[n], 'seq', [(r, r ^ moves[n]) for r in range(ranks)])  72 us
    pallas_call x4, Pallas kernels, right_both(): pl.pallas_call(functools.partial(right_kernel, ranks, ins, outs), out_sha...  52.6 us
    pallas_call x5, Pallas kernels, left_back(): pl.pallas_call(functools.partial(left_back_kernel, ranks, terms), out_sha...  32.9 us
    pallas_call x5, Pallas kernels, left_forward(): pl.pallas_call(functools.partial(left_forward_kernel, ranks), out_shape=[...  26.7 us
  transfers between devices with their start and end apart: 71, of which 31 were waited for; matrix products, arithmetic and copies ran while one was open for 0% of the time, Pallas kernels for 27%

profile of v4, /device:TPU:0, one launch (start us, length us, event | category | flops | bytes accessed | tf_op | source)
XLA Modules:
  0.0 393.1 jit_solution(14445116186959292559)
XLA Ops:
  22.2 6.3 %collective-permute-done.11.refs_2_ = bf16[16,32,256]{2,1,0:T(8,128)(2,1)} collective-permute-done((bf16[16,32,256]{2,1,0:T(8,128)(2,1)}, bf16[16,32,256]{2,1,0:T(8,128)(2,1)}, u32[]{:S(2)}, u32[]{:S(2)}) %collective-permute-start.11) | collective-permute-done | bytes 262176 | tf_op jit(solution)/shard_map/ppermute | solution.py:191
  33.8 5.0 %collective-permute-done.14.refs_5_ = bf16[16,32,256]{2,1,0:T(8,128)(2,1)S(1)} collective-permute-done((bf16[16,32,256]{2,1,0:T(8,128)(2,1)}, bf16[16,32,256]{2,1,0:T(8,128)(2,1)S(1)}, u32[]{:S(2)}, u32[]{:S(2)}) %collective-permute-start.14) | collective-permute-done | bytes 262176 | tf_op jit(solution)/shard_map/ppermute | solution.py:191
  44.7 6.5 %shard_map.78 = (bf16[32,32,256]{2,1,0:T(8,128)(2,1)}, bf16[32,32,256]{2,1,0:T(8,128)(2,1)}, bf16[32,32,256]{2,1,0:T(8,128)(2,1)}, bf16[32,32,256]{2,1,0:T(8,128...) custom-call(s32[1]{0:T(128)} %bitcast.rank_ref, ...), custom_call_target="tpu_custom_call" | custom-call | flops 1024 | bytes 1024 | tf_op jit(solution)/shard_map/pallas_call | solution.py:174
  56.2 5.1 %collective-permute-done.21.refs_13_ = bf16[16,32,256]{2,1,0:T(8,128)(2,1)S(1)} collective-permute-done((bf16[16,32,256]{2,1,0:T(8,128)(2,1)}, bf16[16,32,256]{2,1,0:T(8,128)(2,1)S(1)}, u32[]{:S(2)}, u32[]{:S(2)}) %collective-permute-start.21) | collective-permute-done | bytes 262176 | tf_op jit(solution)/shard_map/ppermute | solution.py:191
  64.1 6.5 %shard_map.79 = (bf16[32,32,256]{2,1,0:T(8,128)(2,1)}, bf16[32,32,256]{2,1,0:T(8,128)(2,1)}, bf16[32,32,256]{2,1,0:T(8,128)(2,1)}, bf16[32,32,256]{2,1,0:T(8,128...) custom-call(s32[1]{0:T(128)} %bitcast.rank_ref, ...), custom_call_target="tpu_custom_call" | custom-call | flops 1024 | bytes 1024 | tf_op jit(solution)/shard_map/pallas_call | solution.py:174
  70.6 6.4 %shard_map.80 = (bf16[32,32,256]{2,1,0:T(8,128)(2,1)}, bf16[32,32,256]{2,1,0:T(8,128)(2,1)}, bf16[32,32,256]{2,1,0:T(8,128)(2,1)}, bf16[32,32,256]{2,1,0:T(8,128...) custom-call(s32[1]{0:T(128)} %bitcast.rank_ref, ...), custom_call_target="tpu_custom_call" | custom-call | flops 1024 | bytes 1024 | tf_op jit(solution)/shard_map/pallas_call | solution.py:174
  80.2 4.5 %collective-permute-done.4.refs_2_ = bf16[32,32,256]{2,1,0:T(8,128)(2,1)S(1)} collective-permute-done((bf16[32,32,256]{2,1,0:T(8,128)(2,1)}, bf16[32,32,256]{2,1,0:T(8,128)(2,1)S(1)}, u32[]{:S(2)}, u32[]{:S(2)}) %collective-permute-start.4) | collective-permute-done | bytes 524320 | tf_op jit(solution)/shard_map/ppermute | solution.py:191
  86.2 8.9 %collective-permute-done.6.refs_4_ = bf16[32,32,256]{2,1,0:T(8,128)(2,1)S(1)} collective-permute-done((bf16[32,32,256]{2,1,0:T(8,128)(2,1)}, bf16[32,32,256]{2,1,0:T(8,128)(2,1)S(1)}, u32[]{:S(2)}, u32[]{:S(2)}) %collective-permute-start.6) | collective-permute-done | bytes 524320 | tf_op jit(solution)/shard_map/ppermute | solution.py:191
  95.2 13.1 %shard_map.82 = (bf16[32,32,256]{2,1,0:T(8,128)(2,1)}, bf16[32,32,256]{2,1,0:T(8,128)(2,1)}, bf16[32,32,256]{2,1,0:T(8,128)(2,1)}, bf16[32,32,256]{2,1,0:T(8,128...) custom-call(s32[1]{0:T(128)} %bitcast.rank_ref, ...), custom_call_target="tpu_custom_call" | custom-call | flops 1024 | bytes 1024 | tf_op jit(solution)/shard_map/pallas_call | solution.py:203
  110.4 7.5 %collective-permute-done.28.refs_1_ = bf16[32,32,256]{2,1,0:T(8,128)(2,1)S(1)} collective-permute-done((bf16[32,32,256]{2,1,0:T(8,128)(2,1)}, bf16[32,32,256]{2,1,0:T(8,128)(2,1)S(1)}, u32[]{:S(2)}, u32[]{:S(2)}) %collective-permute-start.28) | collective-permute-done | bytes 524320 | tf_op jit(solution)/shard_map/ppermute | solution.py:191
  118.3 11.4 %collective-permute-done.29.refs_2_ = bf16[32,32,256]{2,1,0:T(8,128)(2,1)S(1)} collective-permute-done((bf16[32,32,256]{2,1,0:T(8,128)(2,1)}, bf16[32,32,256]{2,1,0:T(8,128)(2,1)S(1)}, u32[]{:S(2)}, u32[]{:S(2)}) %collective-permute-start.29) | collective-permute-done | bytes 524320 | tf_op jit(solution)/shard_map/ppermute | solution.py:191
  131.4 13.1 %shard_map.83 = (bf16[32,32,256]{2,1,0:T(8,128)(2,1)}, bf16[32,32,256]{2,1,0:T(8,128)(2,1)}, bf16[32,32,256]{2,1,0:T(8,128)(2,1)}, bf16[32,32,256]{2,1,0:T(8,128...) custom-call(s32[1]{0:T(128)} %bitcast.rank_ref, ...), custom_call_target="tpu_custom_call", output_to_operand_aliasing={{8}: (11, {})} | custom-call | flops 1024 | bytes 1024 | tf_op jit(solution)/shard_map/pallas_call | solution.py:203
  155.5 13.2 %shard_map.86 = (bf16[32,32,256]{2,1,0:T(8,128)(2,1)}, bf16[32,32,256]{2,1,0:T(8,128)(2,1)}, bf16[32,32,256]{2,1,0:T(8,128)(2,1)}, bf16[32,32,256]{2,1,0:T(8,128...) custom-call(s32[1]{0:T(128)} %bitcast.rank_ref, ...), custom_call_target="tpu_custom_call", output_to_operand_aliasing={{8}: (11, {})} | custom-call | flops 1024 | bytes 1024 | tf_op jit(solution)/shard_map/pallas_call | solution.py:203
  169.3 5.5 %collective-permute-done.1.refs_2_ = bf16[32,32,256]{2,1,0:T(8,128)(2,1)S(1)} collective-permute-done((bf16[32,32,256]{2,1,0:T(8,128)(2,1)}, bf16[32,32,256]{2,1,0:T(8,128)(2,1)S(1)}, u32[]{:S(2)}, u32[]{:S(2)}) %collective-permute-start.1) | collective-permute-done | bytes 524320 | tf_op jit(solution)/shard_map/ppermute | solution.py:191
  176.9 8.3 %collective-permute-done.24.refs_4_ = bf16[32,32,256]{2,1,0:T(8,128)(2,1)S(1)} collective-permute-done((bf16[32,32,256]{2,1,0:T(8,128)(2,1)}, bf16[32,32,256]{2,1,0:T(8,128)(2,1)S(1)}, u32[]{:S(2)}, u32[]{:S(2)}) %collective-permute-start.24) | collective-permute-done | bytes 524320 | tf_op jit(solution)/shard_map/ppermute | solution.py:191
  185.7 10.7 %collective-permute-done.25.refs_5_ = bf16[32,32,256]{2,1,0:T(8,128)(2,1)} collective-permute-done((bf16[32,32,256]{2,1,0:T(8,128)(2,1)}, bf16[32,32,256]{2,1,0:T(8,128)(2,1)}, u32[]{:S(2)}, u32[]{:S(2)}) %collective-permute-start.25) | collective-permute-done | bytes 524320 | tf_op jit(solution)/shard_map/ppermute | solution.py:191
  196.9 13.2 %shard_map.87 = (bf16[16,32,256]{2,1,0:T(8,128)(2,1)}, bf16[16,32,256]{2,1,0:T(8,128)(2,1)}, bf16[16,32,256]{2,1,0:T(8,128)(2,1)}, bf16[16,32,256]{2,1,0:T(8,128...) custom-call(s32[1]{0:T(128)} %bitcast.rank_ref, ...), custom_call_target="tpu_custom_call", output_to_operand_aliasing={{16}: (11, {})} | custom-call | flops 1024 | bytes 1024 | tf_op jit(solution)/shard_map/pallas_call | solution.py:203
  210.1 8.5 %collective-permute-done.36.refs_2_ = bf16[32,32,256]{2,1,0:T(8,128)(2,1)S(1)} collective-permute-done((bf16[32,32,256]{2,1,0:T(8,128)(2,1)}, bf16[32,32,256]{2,1,0:T(8,128)(2,1)S(1)}, u32[]{:S(2)}, u32[]{:S(2)}) %collective-permute-start.36) | collective-permute-done | bytes 524320 | tf_op jit(solution)/shard_map/ppermute | solution.py:191
  225.2 9.9 %collective-permute-done.38.refs_4_ = bf16[32,32,256]{2,1,0:T(8,128)(2,1)S(1)} collective-permute-done((bf16[32,32,256]{2,1,0:T(8,128)(2,1)}, bf16[32,32,256]{2,1,0:T(8,128)(2,1)S(1)}, u32[]{:S(2)}, u32[]{:S(2)}) %collective-permute-start.38) | collective-permute-done | bytes 524320 | tf_op jit(solution)/shard_map/ppermute | solution.py:191
  236.7 9.2 %collective-permute-done.39.refs_5_ = bf16[32,32,256]{2,1,0:T(8,128)(2,1)S(1)} collective-permute-done((bf16[32,32,256]{2,1,0:T(8,128)(2,1)S(1)}, bf16[32,32,256]{2,1,0:T(8,128)(2,1)S(1)}, u32[]{:S(2)}, u32[]{:S(2)}) %collective-permute-start.39) | collective-permute-done | bytes 524320 | tf_op jit(solution)/shard_map/ppermute | solution.py:191
  250.7 7.6 %shard_map.89 = (bf16[1,8192,512]{2,1,0:T(8,128)(2,1)}, bf16[1,8192,512]{2,1,0:T(8,128)(2,1)}, f32[2048,512]{1,0:T(8,128)}, f32[8,128]{1,0:T(8,128)}) custom-call(s32[1]{0:T(128)} %bitcast.rank_ref, bf16[1,8192,512]{2,1,0:T(8,128)(2,1)} %values_ref.19, bf16[1,8192,512]{2,1,0:T(8,128)(2,1)} %cotangent_ref.19, bf16[32,256,256]{2,1,0:T(8,128)(2,1)} %left_ref.19, ...), custom_call_target="tpu_custom_call" | custom-call | flops 1024 | bytes 1024 | tf_op jit(solution)/shard_map/pallas_call | solution.py:256
  258.9 10.0 %collective-permute-done.50.refs_2_ = bf16[32,32,256]{2,1,0:T(8,128)(2,1)S(1)} collective-permute-done((bf16[32,32,256]{2,1,0:T(8,128)(2,1)}, bf16[32,32,256]{2,1,0:T(8,128)(2,1)S(1)}, u32[]{:S(2)}, u32[]{:S(2)}) %collective-permute-start.50) | collective-permute-done | bytes 524320 | tf_op jit(solution)/shard_map/ppermute | solution.py:191
  271.3 8.9 %collective-permute-done.52.refs_4_ = bf16[32,32,256]{2,1,0:T(8,128)(2,1)S(1)} collective-permute-done((bf16[32,32,256]{2,1,0:T(8,128)(2,1)}, bf16[32,32,256]{2,1,0:T(8,128)(2,1)S(1)}, u32[]{:S(2)}, u32[]{:S(2)}) %collective-permute-start.52) | collective-permute-done | bytes 524320 | tf_op jit(solution)/shard_map/ppermute | solution.py:191
  281.7 9.2 %collective-permute-done.53.refs_5_ = bf16[32,32,256]{2,1,0:T(8,128)(2,1)S(1)} collective-permute-done((bf16[32,32,256]{2,1,0:T(8,128)(2,1)}, bf16[32,32,256]{2,1,0:T(8,128)(2,1)S(1)}, u32[]{:S(2)}, u32[]{:S(2)}) %collective-permute-start.53) | collective-permute-done | bytes 524320 | tf_op jit(solution)/shard_map/ppermute | solution.py:191
  294.9 7.4 %collective-permute-done.42.refs_1_ = bf16[32,32,256]{2,1,0:T(8,128)(2,1)S(1)} collective-permute-done((bf16[32,32,256]{2,1,0:T(8,128)(2,1)}, bf16[32,32,256]{2,1,0:T(8,128)(2,1)S(1)}, u32[]{:S(2)}, u32[]{:S(2)}) %collective-permute-start.42) | collective-permute-done | bytes 524320 | tf_op jit(solution)/shard_map/ppermute | solution.py:191
  303.3 10.6 %collective-permute-done.43.refs_2_ = bf16[32,32,256]{2,1,0:T(8,128)(2,1)S(1)} collective-permute-done((bf16[32,32,256]{2,1,0:T(8,128)(2,1)}, bf16[32,32,256]{2,1,0:T(8,128)(2,1)S(1)}, u32[]{:S(2)}, u32[]{:S(2)}) %collective-permute-start.43) | collective-permute-done | bytes 524320 | tf_op jit(solution)/shard_map/ppermute | solution.py:191
  314.1 7.6 %shard_map.92 = (bf16[1,8192,512]{2,1,0:T(8,128)(2,1)}, bf16[1,8192,512]{2,1,0:T(8,128)(2,1)}, f32[2048,512]{1,0:T(8,128)}, f32[8,128]{1,0:T(8,128)}) custom-call(s32[1]{0:T(128)} %bitcast.rank_ref, bf16[1,8192,512]{2,1,0:T(8,128)(2,1)} %values_ref.19, ...), custom_call_target="tpu_custom_call", output_to_operand_aliasing={{0}: (12, {}), {1}: (13, {}), {2}: (14, {})} | custom-call | flops 1024 | bytes 1024 | tf_op jit(solution)/shard_map/pallas_call | solution.py:256
  326.8 9.2 %collective-permute-done.46.refs_5_ = bf16[32,32,256]{2,1,0:T(8,128)(2,1)} collective-permute-done((bf16[32,32,256]{2,1,0:T(8,128)(2,1)}, bf16[32,32,256]{2,1,0:T(8,128)(2,1)}, u32[]{:S(2)}, u32[]{:S(2)}) %collective-permute-start.46) | collective-permute-done | bytes 524320 | tf_op jit(solution)/shard_map/ppermute | solution.py:191
  339.3 7.6 %shard_map.93 = (bf16[1,8192,512]{2,1,0:T(8,128)(2,1)}, bf16[1,8192,512]{2,1,0:T(8,128)(2,1)}, f32[2048,512]{1,0:T(8,128)}, f32[8,128]{1,0:T(8,128)}) custom-call(s32[1]{0:T(128)} %bitcast.rank_ref, bf16[1,8192,512]{2,1,0:T(8,128)(2,1)} %values_ref.19, ...), custom_call_target="tpu_custom_call", output_to_operand_aliasing={{0}: (12, {}), {1}: (13, {}), {2}: (14, {})} | custom-call | flops 1024 | bytes 1024 | tf_op jit(solution)/shard_map/pallas_call | solution.py:256
  365.3 5.0 %collective-permute-done.57.refs_2_ = bf16[16,32,256]{2,1,0:T(8,128)(2,1)S(1)} collective-permute-done((bf16[16,32,256]{2,1,0:T(8,128)(2,1)}, bf16[16,32,256]{2,1,0:T(8,128)(2,1)S(1)}, u32[]{:S(2)}, u32[]{:S(2)}) %collective-permute-start.57) | collective-permute-done | bytes 262176 | tf_op jit(solution)/shard_map/ppermute | solution.py:191
  370.4 5.7 %shard_map.97 = (bf16[1,8192,512]{2,1,0:T(8,128)(2,1)}, bf16[1,8192,512]{2,1,0:T(8,128)(2,1)}, f32[2048,512]{1,0:T(8,128)}, f32[8,128]{1,0:T(8,128)}) custom-call(s32[1]{0:T(128)} %bitcast.rank_ref, bf16[1,8192,512]{2,1,0:T(8,128)(2,1)} %values_ref.19, ...), custom_call_target="tpu_custom_call", output_to_operand_aliasing={{0}: (13, {}), {1}: (14, {}), {2}: (15, {})} | custom-call | flops 1024 | bytes 1024 | tf_op jit(solution)/shard_map/pallas_call | solution.py:256
  376.2 4.8 %collective-permute-done.60.refs_5_ = bf16[16,32,256]{2,1,0:T(8,128)(2,1)S(1)} collective-permute-done((bf16[16,32,256]{2,1,0:T(8,128)(2,1)}, bf16[16,32,256]{2,1,0:T(8,128)(2,1)S(1)}, u32[]{:S(2)}, u32[]{:S(2)}) %collective-permute-start.60) | collective-permute-done | bytes 262176 | tf_op jit(solution)/shard_map/ppermute | solution.py:191
  (256 shorter events, 112.0 us)
Async XLA Ops:
  7.2 363.1 %reduce-scatter.2.cloned.1.call-start = ((), (), s32[]{:S(2)}) async-start(), calls=%async_computation.1 | async-start | bytes 10485760 | tf_op jit(solution)/shard_map/reduce_scatter | solution.py:338
  51.3 25.9 %collective-permute-start.3 = (bf16[32,32,256]{2,1,0:T(8,128)(2,1)}, bf16[32,32,256]{2,1,0:T(8,128)(2,1)S(1)}, u32[]{:S(2)}, u32[]{:S(2)}) collective-permute-start(bf16[32,32,256]{2,1,0:T(8,128)(2,1)} %get-tuple-element.168), channel_id=1, source_target_pairs={{0,6},{1,7},{2,4},{3,5},{4,2},{5,3},{6,0},{7,1},{8,14},{9,15},{10,... | collective-permute-start | bytes 1572872 | tf_op jit(solution)/shard_map/ppermute | solution.py:191
  54.4 30.3 %collective-permute-start.4 = (bf16[32,32,256]{2,1,0:T(8,128)(2,1)}, bf16[32,32,256]{2,1,0:T(8,128)(2,1)S(1)}, u32[]{:S(2)}, u32[]{:S(2)}) collective-permute-start(bf16[32,32,256]{2,1,0:T(8,128)(2,1)} %get-tuple-element.169), channel_id=1, source_target_pairs={{0,2},{1,3},{2,0},{3,1},{4,6},{5,7},{6,4},{7,5},{8,10},{9,11},{10,... | collective-permute-start | bytes 1572872 | tf_op jit(solution)/shard_map/ppermute | solution.py:191
  55.7 30.5 %collective-permute-start.5 = (bf16[32,32,256]{2,1,0:T(8,128)(2,1)}, bf16[32,32,256]{2,1,0:T(8,128)(2,1)S(1)}, u32[]{:S(2)}, u32[]{:S(2)}) collective-permute-start(bf16[32,32,256]{2,1,0:T(8,128)(2,1)} %get-tuple-element.170), channel_id=1, source_target_pairs={{0,4},{1,5},{2,6},{3,7},{4,0},{5,1},{6,2},{7,3},{8,12},{9,13},{10,... | collective-permute-start | bytes 1572872 | tf_op jit(solution)/shard_map/ppermute | solution.py:191
  62.0 33.1 %collective-permute-start.6 = (bf16[32,32,256]{2,1,0:T(8,128)(2,1)}, bf16[32,32,256]{2,1,0:T(8,128)(2,1)S(1)}, u32[]{:S(2)}, u32[]{:S(2)}) collective-permute-start(bf16[32,32,256]{2,1,0:T(8,128)(2,1)} %get-tuple-element.171), channel_id=1, source_target_pairs={{0,7},{1,6},{2,5},{3,4},{4,3},{5,2},{6,1},{7,0},{8,15},{9,14},{10,... | collective-permute-start | bytes 1572872 | tf_op jit(solution)/shard_map/ppermute | solution.py:191
  77.0 31.3 %collective-permute-start.7 = (bf16[32,32,256]{2,1,0:T(8,128)(2,1)}, bf16[32,32,256]{2,1,0:T(8,128)(2,1)S(1)}, u32[]{:S(2)}, u32[]{:S(2)}) collective-permute-start(bf16[32,32,256]{2,1,0:T(8,128)(2,1)} %get-tuple-element.172), channel_id=1, source_target_pairs={{0,3},{1,2},{2,1},{3,0},{4,7},{5,6},{6,5},{7,4},{8,11},{9,10},{10,... | collective-permute-start | bytes 1572872 | tf_op jit(solution)/shard_map/ppermute | solution.py:191
  77.2 40.7 %collective-permute-start.28 = (bf16[32,32,256]{2,1,0:T(8,128)(2,1)}, bf16[32,32,256]{2,1,0:T(8,128)(2,1)S(1)}, u32[]{:S(2)}, u32[]{:S(2)}) collective-permute-start(bf16[32,32,256]{2,1,0:T(8,128)(2,1)} %get-tuple-element.202), channel_id=1, source_target_pairs={{0,6},{1,7},{2,4},{3,5},{4,2},{5,3},{6,0},{7,1},{8,14},{9,15},{10,... | collective-permute-start | bytes 1572872 | tf_op jit(solution)/shard_map/ppermute | solution.py:191
  84.7 45.0 %collective-permute-start.29 = (bf16[32,32,256]{2,1,0:T(8,128)(2,1)}, bf16[32,32,256]{2,1,0:T(8,128)(2,1)S(1)}, u32[]{:S(2)}, u32[]{:S(2)}) collective-permute-start(bf16[32,32,256]{2,1,0:T(8,128)(2,1)} %get-tuple-element.203), channel_id=1, source_target_pairs={{0,2},{1,3},{2,0},{3,1},{4,6},{5,7},{6,4},{7,5},{8,10},{9,11},{10,... | collective-permute-start | bytes 1572872 | tf_op jit(solution)/shard_map/ppermute | solution.py:191
  86.2 43.5 %collective-permute-start.8 = (bf16[32,32,256]{2,1,0:T(8,128)(2,1)}, bf16[32,32,256]{2,1,0:T(8,128)(2,1)}, u32[]{:S(2)}, u32[]{:S(2)}) collective-permute-start(bf16[32,32,256]{2,1,0:T(8,128)(2,1)} %get-tuple-element.176), channel_id=1, source_target_pairs={{0,5},{1,4},{2,7},{3,6},{4,1},{5,0},{6,3},{7,2},{8,13},{9,12},{10,... | collective-permute-start | bytes 1572872 | tf_op jit(solution)/shard_map/ppermute | solution.py:191
  95.1 36.3 %collective-permute-start.9 = (bf16[32,32,256]{2,1,0:T(8,128)(2,1)}, bf16[32,32,256]{2,1,0:T(8,128)(2,1)}, u32[]{:S(2)}, u32[]{:S(2)}) collective-permute-start(bf16[32,32,256]{2,1,0:T(8,128)(2,1)} %get-tuple-element.177), channel_id=1, source_target_pairs={{0,1},{1,0},{2,3},{3,2},{4,5},{5,4},{6,7},{7,6},{8,9},{9,8},{10,11... | collective-permute-start | bytes 1572872 | tf_op jit(solution)/shard_map/ppermute | solution.py:191
  108.4 36.2 %collective-permute-start.30 = (bf16[32,32,256]{2,1,0:T(8,128)(2,1)}, bf16[32,32,256]{2,1,0:T(8,128)(2,1)S(1)}, u32[]{:S(2)}, u32[]{:S(2)}) collective-permute-start(bf16[32,32,256]{2,1,0:T(8,128)(2,1)} %get-tuple-element.204), channel_id=1, source_target_pairs={{0,4},{1,5},{2,6},{3,7},{4,0},{5,1},{6,2},{7,3},{8,12},{9,13},{10,... | collective-permute-start | bytes 1572872 | tf_op jit(solution)/shard_map/ppermute | solution.py:191
  117.9 28.2 %collective-permute-start.31 = (bf16[32,32,256]{2,1,0:T(8,128)(2,1)}, bf16[32,32,256]{2,1,0:T(8,128)(2,1)S(1)}, u32[]{:S(2)}, u32[]{:S(2)}) collective-permute-start(bf16[32,32,256]{2,1,0:T(8,128)(2,1)} %get-tuple-element.209), channel_id=1, source_target_pairs={{0,7},{1,6},{2,5},{3,4},{4,3},{5,2},{6,1},{7,0},{8,15},{9,14},{10,... | collective-permute-start | bytes 1572872 | tf_op jit(solution)/shard_map/ppermute | solution.py:191
  146.1 28.6 %collective-permute-start.1 = (bf16[32,32,256]{2,1,0:T(8,128)(2,1)}, bf16[32,32,256]{2,1,0:T(8,128)(2,1)S(1)}, u32[]{:S(2)}, u32[]{:S(2)}) collective-permute-start(bf16[32,32,256]{2,1,0:T(8,128)(2,1)} %get-tuple-element.161), channel_id=1, source_target_pairs={{0,2},{1,3},{2,0},{3,1},{4,6},{5,7},{6,4},{7,5},{8,10},{9,11},{10,... | collective-permute-start | bytes 1572872 | tf_op jit(solution)/shard_map/ppermute | solution.py:191
  152.6 32.5 %collective-permute-start.24 = (bf16[32,32,256]{2,1,0:T(8,128)(2,1)}, bf16[32,32,256]{2,1,0:T(8,128)(2,1)S(1)}, u32[]{:S(2)}, u32[]{:S(2)}) collective-permute-start(bf16[32,32,256]{2,1,0:T(8,128)(2,1)} %get-tuple-element.197), channel_id=1, source_target_pairs={{0,7},{1,6},{2,5},{3,4},{4,3},{5,2},{6,1},{7,0},{8,15},{9,14},{10,... | collective-permute-start | bytes 1572872 | tf_op jit(solution)/shard_map/ppermute | solution.py:191
  155.4 40.9 %collective-permute-start.25 = (bf16[32,32,256]{2,1,0:T(8,128)(2,1)}, bf16[32,32,256]{2,1,0:T(8,128)(2,1)}, u32[]{:S(2)}, u32[]{:S(2)}) collective-permute-start(bf16[32,32,256]{2,1,0:T(8,128)(2,1)} %get-tuple-element.198), channel_id=1, source_target_pairs={{0,3},{1,2},{2,1},{3,0},{4,7},{5,6},{6,5},{7,4},{8,11},{9,10},{10,... | collective-permute-start | bytes 1572872 | tf_op jit(solution)/shard_map/ppermute | solution.py:191
  168.7 28.1 %collective-permute-start.26 = (bf16[32,32,256]{2,1,0:T(8,128)(2,1)}, bf16[32,32,256]{2,1,0:T(8,128)(2,1)}, u32[]{:S(2)}, u32[]{:S(2)}) collective-permute-start(bf16[32,32,256]{2,1,0:T(8,128)(2,1)} %get-tuple-element.199), channel_id=1, source_target_pairs={{0,5},{1,4},{2,7},{3,6},{4,1},{5,0},{6,3},{7,2},{8,13},{9,12},{10,... | collective-permute-start | bytes 1572872 | tf_op jit(solution)/shard_map/ppermute | solution.py:191
  174.8 35.3 %collective-permute-start.35 = (bf16[32,32,256]{2,1,0:T(8,128)(2,1)}, bf16[32,32,256]{2,1,0:T(8,128)(2,1)S(1)}, u32[]{:S(2)}, u32[]{:S(2)}) collective-permute-start(bf16[32,32,256]{2,1,0:T(8,128)(2,1)} %get-tuple-element.237), channel_id=1, source_target_pairs={{0,6},{1,7},{2,4},{3,5},{4,2},{5,3},{6,0},{7,1},{8,14},{9,15},{10,... | collective-permute-start | bytes 1572872 | tf_op jit(solution)/shard_map/ppermute | solution.py:191
  185.2 33.5 %collective-permute-start.36 = (bf16[32,32,256]{2,1,0:T(8,128)(2,1)}, bf16[32,32,256]{2,1,0:T(8,128)(2,1)S(1)}, u32[]{:S(2)}, u32[]{:S(2)}) collective-permute-start(bf16[32,32,256]{2,1,0:T(8,128)(2,1)} %get-tuple-element.238), channel_id=1, source_target_pairs={{0,2},{1,3},{2,0},{3,1},{4,6},{5,7},{6,4},{7,5},{8,10},{9,11},{10,... | collective-permute-start | bytes 1572872 | tf_op jit(solution)/shard_map/ppermute | solution.py:191
  223.1 26.5 %collective-permute-start.41 = (bf16[32,32,256]{2,1,0:T(8,128)(2,1)}, bf16[32,32,256]{2,1,0:T(8,128)(2,1)S(1)}, u32[]{:S(2)}, u32[]{:S(2)}) collective-permute-start(bf16[32,32,256]{2,1,0:T(8,128)(2,1)} %get-tuple-element.243), channel_id=1, source_target_pairs={{0,1},{1,0},{2,3},{3,2},{4,5},{5,4},{6,7},{7,6},{8,9},{9,8},{10,11... | collective-permute-start | bytes 1572872 | tf_op jit(solution)/shard_map/ppermute | solution.py:191
  223.2 35.1 %collective-permute-start.49 = (bf16[32,32,256]{2,1,0:T(8,128)(2,1)}, bf16[32,32,256]{2,1,0:T(8,128)(2,1)S(1)}, u32[]{:S(2)}, u32[]{:S(2)}) collective-permute-start(bf16[32,32,256]{2,1,0:T(8,128)(2,1)} %get-tuple-element.260), channel_id=1, source_target_pairs={{0,6},{1,7},{2,4},{3,5},{4,2},{5,3},{6,0},{7,1},{8,14},{9,15},{10,... | collective-permute-start | bytes 1572872 | tf_op jit(solution)/shard_map/ppermute | solution.py:191
  235.1 33.8 %collective-permute-start.50 = (bf16[32,32,256]{2,1,0:T(8,128)(2,1)}, bf16[32,32,256]{2,1,0:T(8,128)(2,1)S(1)}, u32[]{:S(2)}, u32[]{:S(2)}) collective-permute-start(bf16[32,32,256]{2,1,0:T(8,128)(2,1)} %get-tuple-element.261), channel_id=1, source_target_pairs={{0,2},{1,3},{2,0},{3,1},{4,6},{5,7},{6,4},{7,5},{8,10},{9,11},{10,... | collective-permute-start | bytes 1572872 | tf_op jit(solution)/shard_map/ppermute | solution.py:191
  247.7 32.4 %collective-permute-start.52 = (bf16[32,32,256]{2,1,0:T(8,128)(2,1)}, bf16[32,32,256]{2,1,0:T(8,128)(2,1)S(1)}, u32[]{:S(2)}, u32[]{:S(2)}) collective-permute-start(bf16[32,32,256]{2,1,0:T(8,128)(2,1)} %get-tuple-element.263), channel_id=1, source_target_pairs={{0,7},{1,6},{2,5},{3,4},{4,3},{5,2},{6,1},{7,0},{8,15},{9,14},{10,... | collective-permute-start | bytes 1572872 | tf_op jit(solution)/shard_map/ppermute | solution.py:191
  250.5 40.4 %collective-permute-start.53 = (bf16[32,32,256]{2,1,0:T(8,128)(2,1)}, bf16[32,32,256]{2,1,0:T(8,128)(2,1)S(1)}, u32[]{:S(2)}, u32[]{:S(2)}) collective-permute-start(bf16[32,32,256]{2,1,0:T(8,128)(2,1)} %get-tuple-element.264), channel_id=1, source_target_pairs={{0,3},{1,2},{2,1},{3,0},{4,7},{5,6},{6,5},{7,4},{8,11},{9,10},{10,... | collective-permute-start | bytes 1572872 | tf_op jit(solution)/shard_map/ppermute | solution.py:191
  258.3 34.5 %collective-permute-start.54 = (bf16[32,32,256]{2,1,0:T(8,128)(2,1)}, bf16[32,32,256]{2,1,0:T(8,128)(2,1)S(1)}, u32[]{:S(2)}, u32[]{:S(2)}) collective-permute-start(bf16[32,32,256]{2,1,0:T(8,128)(2,1)} %get-tuple-element.265), channel_id=1, source_target_pairs={{0,5},{1,4},{2,7},{3,6},{4,1},{5,0},{6,3},{7,2},{8,13},{9,12},{10,... | collective-permute-start | bytes 1572872 | tf_op jit(solution)/shard_map/ppermute | solution.py:191
  268.9 25.8 %collective-permute-start.55 = (bf16[32,32,256]{2,1,0:T(8,128)(2,1)}, bf16[32,32,256]{2,1,0:T(8,128)(2,1)S(1)}, u32[]{:S(2)}, u32[]{:S(2)}) collective-permute-start(bf16[32,32,256]{2,1,0:T(8,128)(2,1)} %get-tuple-element.266), channel_id=1, source_target_pairs={{0,1},{1,0},{2,3},{3,2},{4,5},{5,4},{6,7},{7,6},{8,9},{9,8},{10,11... | collective-permute-start | bytes 1572872 | tf_op jit(solution)/shard_map/ppermute | solution.py:191
  268.9 33.4 %collective-permute-start.42 = (bf16[32,32,256]{2,1,0:T(8,128)(2,1)}, bf16[32,32,256]{2,1,0:T(8,128)(2,1)S(1)}, u32[]{:S(2)}, u32[]{:S(2)}) collective-permute-start(bf16[32,32,256]{2,1,0:T(8,128)(2,1)} %get-tuple-element.245), channel_id=1, source_target_pairs={{0,6},{1,7},{2,4},{3,5},{4,2},{5,3},{6,0},{7,1},{8,14},{9,15},{10,... | collective-permute-start | bytes 1572872 | tf_op jit(solution)/shard_map/ppermute | solution.py:191
  280.2 33.8 %collective-permute-start.43 = (bf16[32,32,256]{2,1,0:T(8,128)(2,1)}, bf16[32,32,256]{2,1,0:T(8,128)(2,1)S(1)}, u32[]{:S(2)}, u32[]{:S(2)}) collective-permute-start(bf16[32,32,256]{2,1,0:T(8,128)(2,1)} %get-tuple-element.246), channel_id=1, source_target_pairs={{0,2},{1,3},{2,0},{3,1},{4,6},{5,7},{6,4},{7,5},{8,10},{9,11},{10,... | collective-permute-start | bytes 1572872 | tf_op jit(solution)/shard_map/ppermute | solution.py:191
  291.7 30.1 %collective-permute-start.44 = (bf16[32,32,256]{2,1,0:T(8,128)(2,1)}, bf16[32,32,256]{2,1,0:T(8,128)(2,1)S(1)}, u32[]{:S(2)}, u32[]{:S(2)}) collective-permute-start(bf16[32,32,256]{2,1,0:T(8,128)(2,1)} %get-tuple-element.247), channel_id=1, source_target_pairs={{0,4},{1,5},{2,6},{3,7},{4,0},{5,1},{6,2},{7,3},{8,12},{9,13},{10,... | collective-permute-start | bytes 1572872 | tf_op jit(solution)/shard_map/ppermute | solution.py:191
  292.8 32.5 %collective-permute-start.45 = (bf16[32,32,256]{2,1,0:T(8,128)(2,1)}, bf16[32,32,256]{2,1,0:T(8,128)(2,1)}, u32[]{:S(2)}, u32[]{:S(2)}) collective-permute-start(bf16[32,32,256]{2,1,0:T(8,128)(2,1)} %get-tuple-element.248), channel_id=1, source_target_pairs={{0,7},{1,6},{2,5},{3,4},{4,3},{5,2},{6,1},{7,0},{8,15},{9,14},{10,... | collective-permute-start | bytes 1572872 | tf_op jit(solution)/shard_map/ppermute | solution.py:191
  294.7 41.3 %collective-permute-start.46 = (bf16[32,32,256]{2,1,0:T(8,128)(2,1)}, bf16[32,32,256]{2,1,0:T(8,128)(2,1)}, u32[]{:S(2)}, u32[]{:S(2)}) collective-permute-start(bf16[32,32,256]{2,1,0:T(8,128)(2,1)} %get-tuple-element.249), channel_id=1, source_target_pairs={{0,3},{1,2},{2,1},{3,0},{4,7},{5,6},{6,5},{7,4},{8,11},{9,10},{10,... | collective-permute-start | bytes 1572872 | tf_op jit(solution)/shard_map/ppermute | solution.py:191
  302.3 34.8 %collective-permute-start.47 = (bf16[32,32,256]{2,1,0:T(8,128)(2,1)}, bf16[32,32,256]{2,1,0:T(8,128)(2,1)}, u32[]{:S(2)}, u32[]{:S(2)}) collective-permute-start(bf16[32,32,256]{2,1,0:T(8,128)(2,1)} %get-tuple-element.250), channel_id=1, source_target_pairs={{0,5},{1,4},{2,7},{3,6},{4,1},{5,0},{6,3},{7,2},{8,13},{9,12},{10,... | collective-permute-start | bytes 1572872 | tf_op jit(solution)/shard_map/ppermute | solution.py:191
  321.8 25.1 %collective-permute-start.63 = (bf16[16,32,256]{2,1,0:T(8,128)(2,1)}, bf16[16,32,256]{2,1,0:T(8,128)(2,1)S(1)}, u32[]{:S(2)}, u32[]{:S(2)}) collective-permute-start(bf16[16,32,256]{2,1,0:T(8,128)(2,1)} %get-tuple-element.290), channel_id=1, source_target_pairs={{0,6},{1,7},{2,4},{3,5},{4,2},{5,3},{6,0},{7,1},{8,14},{9,15},{10,... | collective-permute-start | bytes 786440 | tf_op jit(solution)/shard_map/ppermute | solution.py:191
  (100 other events, 1597.6 us)
Sparse Core Ops, SparseCore 0:
  219.8 145.3 reduce-scatter.1

commit v5 on v4

--- a/solution.py
+++ b/solution.py
@@ -226,7 +226,7 @@
             cost_estimate=COST,
         )(rank, kernel, right_factor, *arrived, *held, *after)
 
-    def gate(held, after):
+    def gate(held, after, limit=VMEM_LIMIT):
         return list(
             pl.pallas_call(
                 gate_kernel,
@@ -234,7 +234,7 @@
                 in_specs=unread(held) + unread(after),
                 out_specs=unread(held),
                 input_output_aliases={n: n for n in range(len(held))},
-                compiler_params=params,
+                compiler_params=pltpu.CompilerParams(vmem_limit_bytes=limit),
                 cost_estimate=COST,
             )(*held, *after)
         )
@@ -276,7 +276,7 @@
                 ],
             ),
             input_output_aliases=aliases,
-            compiler_params=params,
+            compiler_params=pltpu.CompilerParams(vmem_limit_bytes=48 * 1024 * 1024),
             cost_estimate=COST,
         )(rank, values, cotangent, left_factor, *arrived, *reduced, *earlier, *after)
 
@@ -334,7 +334,7 @@
             if q >= 1 and part == 0:
                 back_step(q - 1)
         if q == 0:
-            (terms,) = gate([terms], returned[0][1 : 1 + EARLY])
+            (terms,) = gate([terms], returned[0][1 : 1 + EARLY], 1 * 1024 * 1024)
             reduced = lax.psum_scatter(terms, "dp", scatter_dimension=0, tiled=True)
     back_step(chunks - 1)
     return tuple(outputs)

time: 393 us -> 399 us (1.015)
  local copies, waits for them, and re-layouts: 5.85 us -> 20.1 us
    unnamed x122 -> x98, local copies, waits for them, and re-layouts: 5.85 us -> 20.1 us
  transfers between devices with their start and end apart: 71 -> 71, of which waited for: 31 -> 31; matrix products, arithmetic and copies ran while one was open for 0% -> 0% of each run, Pallas kernels for 27% -> 25%
where the time goes in v5:
time: 399 us
  waiting for transfers between devices  185 us (46%)
  Pallas kernels  109 us (27%)
  starting transfers between devices  70.3 us (18%)
  local copies, waits for them, and re-layouts  20.1 us (5%)
  between operations  14.5 us (4%)
    ppermute x70, waiting for transfers between devices, exchange(): lax.ppermute(sends[n], 'seq', [(r, r ^ moves[n]) for r in range(ranks)])  185 us
    ppermute x70, starting transfers between devices, exchange(): lax.ppermute(sends[n], 'seq', [(r, r ^ moves[n]) for r in range(ranks)])  70.3 us
    pallas_call x4, Pallas kernels, right_both(): pl.pallas_call(functools.partial(right_kernel, ranks, ins, outs), out_sha...  52.2 us
    pallas_call x5, Pallas kernels, left_back(): pl.pallas_call(functools.partial(left_back_kernel, ranks, terms), out_sha...  29.8 us
    pallas_call x5, Pallas kernels, left_forward(): pl.pallas_call(functools.partial(left_forward_kernel, ranks), out_shape=[...  26.7 us
    unnamed x98, local copies, waits for them, and re-layouts  20.1 us
  transfers between devices with their start and end apart: 71, of which 31 were waited for; matrix products, arithmetic and copies ran while one was open for 0% of the time, Pallas kernels for 25%

profile of v5, /device:TPU:0, one launch (start us, length us, event | category | flops | bytes accessed | tf_op | source)
XLA Modules:
  0.0 398.7 jit_solution(7289060176863080834)
XLA Ops:
  22.2 6.3 %collective-permute-done.11.refs_2_ = bf16[16,32,256]{2,1,0:T(8,128)(2,1)} collective-permute-done((bf16[16,32,256]{2,1,0:T(8,128)(2,1)}, bf16[16,32,256]{2,1,0:T(8,128)(2,1)}, u32[]{:S(2)}, u32[]{:S(2)}) %collective-permute-start.11) | collective-permute-done | bytes 262176 | tf_op jit(solution)/shard_map/ppermute | solution.py:191
  33.8 5.0 %collective-permute-done.14.refs_5_ = bf16[16,32,256]{2,1,0:T(8,128)(2,1)S(1)} collective-permute-done((bf16[16,32,256]{2,1,0:T(8,128)(2,1)}, bf16[16,32,256]{2,1,0:T(8,128)(2,1)S(1)}, u32[]{:S(2)}, u32[]{:S(2)}) %collective-permute-start.14) | collective-permute-done | bytes 262176 | tf_op jit(solution)/shard_map/ppermute | solution.py:191
  44.7 6.5 %shard_map.78 = (bf16[32,32,256]{2,1,0:T(8,128)(2,1)}, bf16[32,32,256]{2,1,0:T(8,128)(2,1)}, bf16[32,32,256]{2,1,0:T(8,128)(2,1)}, bf16[32,32,256]{2,1,0:T(8,128...) custom-call(s32[1]{0:T(128)} %bitcast.rank_ref, ...), custom_call_target="tpu_custom_call" | custom-call | flops 1024 | bytes 1024 | tf_op jit(solution)/shard_map/pallas_call | solution.py:174
  56.2 5.1 %collective-permute-done.21.refs_13_ = bf16[16,32,256]{2,1,0:T(8,128)(2,1)S(1)} collective-permute-done((bf16[16,32,256]{2,1,0:T(8,128)(2,1)}, bf16[16,32,256]{2,1,0:T(8,128)(2,1)S(1)}, u32[]{:S(2)}, u32[]{:S(2)}) %collective-permute-start.21) | collective-permute-done | bytes 262176 | tf_op jit(solution)/shard_map/ppermute | solution.py:191
  64.1 6.5 %shard_map.79 = (bf16[32,32,256]{2,1,0:T(8,128)(2,1)}, bf16[32,32,256]{2,1,0:T(8,128)(2,1)}, bf16[32,32,256]{2,1,0:T(8,128)(2,1)}, bf16[32,32,256]{2,1,0:T(8,128...) custom-call(s32[1]{0:T(128)} %bitcast.rank_ref, ...), custom_call_target="tpu_custom_call" | custom-call | flops 1024 | bytes 1024 | tf_op jit(solution)/shard_map/pallas_call | solution.py:174
  70.6 6.5 %shard_map.80 = (bf16[32,32,256]{2,1,0:T(8,128)(2,1)}, bf16[32,32,256]{2,1,0:T(8,128)(2,1)}, bf16[32,32,256]{2,1,0:T(8,128)(2,1)}, bf16[32,32,256]{2,1,0:T(8,128...) custom-call(s32[1]{0:T(128)} %bitcast.rank_ref, ...), custom_call_target="tpu_custom_call" | custom-call | flops 1024 | bytes 1024 | tf_op jit(solution)/shard_map/pallas_call | solution.py:174
  80.3 4.4 %collective-permute-done.4.refs_2_ = bf16[32,32,256]{2,1,0:T(8,128)(2,1)S(1)} collective-permute-done((bf16[32,32,256]{2,1,0:T(8,128)(2,1)}, bf16[32,32,256]{2,1,0:T(8,128)(2,1)S(1)}, u32[]{:S(2)}, u32[]{:S(2)}) %collective-permute-start.4) | collective-permute-done | bytes 524320 | tf_op jit(solution)/shard_map/ppermute | solution.py:191
  86.2 8.9 %collective-permute-done.6.refs_4_ = bf16[32,32,256]{2,1,0:T(8,128)(2,1)S(1)} collective-permute-done((bf16[32,32,256]{2,1,0:T(8,128)(2,1)}, bf16[32,32,256]{2,1,0:T(8,128)(2,1)S(1)}, u32[]{:S(2)}, u32[]{:S(2)}) %collective-permute-start.6) | collective-permute-done | bytes 524320 | tf_op jit(solution)/shard_map/ppermute | solution.py:191
  95.2 13.0 %shard_map.82 = (bf16[32,32,256]{2,1,0:T(8,128)(2,1)}, bf16[32,32,256]{2,1,0:T(8,128)(2,1)}, bf16[32,32,256]{2,1,0:T(8,128)(2,1)}, bf16[32,32,256]{2,1,0:T(8,128...) custom-call(s32[1]{0:T(128)} %bitcast.rank_ref, ...), custom_call_target="tpu_custom_call" | custom-call | flops 1024 | bytes 1024 | tf_op jit(solution)/shard_map/pallas_call | solution.py:203
  110.3 7.6 %collective-permute-done.28.refs_1_ = bf16[32,32,256]{2,1,0:T(8,128)(2,1)S(1)} collective-permute-done((bf16[32,32,256]{2,1,0:T(8,128)(2,1)}, bf16[32,32,256]{2,1,0:T(8,128)(2,1)S(1)}, u32[]{:S(2)}, u32[]{:S(2)}) %collective-permute-start.28) | collective-permute-done | bytes 524320 | tf_op jit(solution)/shard_map/ppermute | solution.py:191
  118.3 11.4 %collective-permute-done.29.refs_2_ = bf16[32,32,256]{2,1,0:T(8,128)(2,1)S(1)} collective-permute-done((bf16[32,32,256]{2,1,0:T(8,128)(2,1)}, bf16[32,32,256]{2,1,0:T(8,128)(2,1)S(1)}, u32[]{:S(2)}, u32[]{:S(2)}) %collective-permute-start.29) | collective-permute-done | bytes 524320 | tf_op jit(solution)/shard_map/ppermute | solution.py:191
  131.4 13.0 %shard_map.83 = (bf16[32,32,256]{2,1,0:T(8,128)(2,1)}, bf16[32,32,256]{2,1,0:T(8,128)(2,1)}, bf16[32,32,256]{2,1,0:T(8,128)(2,1)}, bf16[32,32,256]{2,1,0:T(8,128...) custom-call(s32[1]{0:T(128)} %bitcast.rank_ref, ...), custom_call_target="tpu_custom_call", output_to_operand_aliasing={{8}: (11, {})} | custom-call | flops 1024 | bytes 1024 | tf_op jit(solution)/shard_map/pallas_call | solution.py:203
  154.8 13.1 %shard_map.86 = (bf16[32,32,256]{2,1,0:T(8,128)(2,1)}, bf16[32,32,256]{2,1,0:T(8,128)(2,1)}, bf16[32,32,256]{2,1,0:T(8,128)(2,1)}, bf16[32,32,256]{2,1,0:T(8,128...) custom-call(s32[1]{0:T(128)} %bitcast.rank_ref, ...), custom_call_target="tpu_custom_call", output_to_operand_aliasing={{8}: (11, {})} | custom-call | flops 1024 | bytes 1024 | tf_op jit(solution)/shard_map/pallas_call | solution.py:203
  168.4 6.3 %collective-permute-done.1.refs_2_ = bf16[32,32,256]{2,1,0:T(8,128)(2,1)S(1)} collective-permute-done((bf16[32,32,256]{2,1,0:T(8,128)(2,1)}, bf16[32,32,256]{2,1,0:T(8,128)(2,1)S(1)}, u32[]{:S(2)}, u32[]{:S(2)}) %collective-permute-start.1) | collective-permute-done | bytes 524320 | tf_op jit(solution)/shard_map/ppermute | solution.py:191
  176.9 8.3 %collective-permute-done.24.refs_4_ = bf16[32,32,256]{2,1,0:T(8,128)(2,1)S(1)} collective-permute-done((bf16[32,32,256]{2,1,0:T(8,128)(2,1)}, bf16[32,32,256]{2,1,0:T(8,128)(2,1)S(1)}, u32[]{:S(2)}, u32[]{:S(2)}) %collective-permute-start.24) | collective-permute-done | bytes 524320 | tf_op jit(solution)/shard_map/ppermute | solution.py:191
  185.7 10.7 %collective-permute-done.25.refs_5_ = bf16[32,32,256]{2,1,0:T(8,128)(2,1)S(1)} collective-permute-done((bf16[32,32,256]{2,1,0:T(8,128)(2,1)}, bf16[32,32,256]{2,1,0:T(8,128)(2,1)S(1)}, u32[]{:S(2)}, u32[]{:S(2)}) %collective-permute-start.25) | collective-permute-done | bytes 524320 | tf_op jit(solution)/shard_map/ppermute | solution.py:191
  197.7 13.1 %shard_map.87 = (bf16[16,32,256]{2,1,0:T(8,128)(2,1)}, bf16[16,32,256]{2,1,0:T(8,128)(2,1)}, bf16[16,32,256]{2,1,0:T(8,128)(2,1)}, bf16[16,32,256]{2,1,0:T(8,128...) custom-call(s32[1]{0:T(128)} %bitcast.rank_ref, ...), custom_call_target="tpu_custom_call", output_to_operand_aliasing={{16}: (11, {})} | custom-call | flops 1024 | bytes 1024 | tf_op jit(solution)/shard_map/pallas_call | solution.py:203
  210.8 7.8 %collective-permute-done.36.refs_2_ = bf16[32,32,256]{2,1,0:T(8,128)(2,1)S(1)} collective-permute-done((bf16[32,32,256]{2,1,0:T(8,128)(2,1)}, bf16[32,32,256]{2,1,0:T(8,128)(2,1)S(1)}, u32[]{:S(2)}, u32[]{:S(2)}) %collective-permute-start.36) | collective-permute-done | bytes 524320 | tf_op jit(solution)/shard_map/ppermute | solution.py:191
  232.0 9.6 %collective-permute-done.38.refs_4_ = bf16[32,32,256]{2,1,0:T(8,128)(2,1)S(1)} collective-permute-done((bf16[32,32,256]{2,1,0:T(8,128)(2,1)S(1)}, bf16[32,32,256]{2,1,0:T(8,128)(2,1)S(1)}, u32[]{:S(2)}, u32[]{:S(2)}) %collective-permute-start.38) | collective-permute-done | bytes 524320 | tf_op jit(solution)/shard_map/ppermute | solution.py:191
  243.8 8.7 %collective-permute-done.39.refs_5_ = bf16[32,32,256]{2,1,0:T(8,128)(2,1)S(1)} collective-permute-done((bf16[32,32,256]{2,1,0:T(8,128)(2,1)}, bf16[32,32,256]{2,1,0:T(8,128)(2,1)S(1)}, u32[]{:S(2)}, u32[]{:S(2)}) %collective-permute-start.39) | collective-permute-done | bytes 524320 | tf_op jit(solution)/shard_map/ppermute | solution.py:191
  259.6 6.8 %shard_map.89 = (bf16[1,8192,512]{2,1,0:T(8,128)(2,1)}, bf16[1,8192,512]{2,1,0:T(8,128)(2,1)}, f32[2048,512]{1,0:T(8,128)}, f32[8,128]{1,0:T(8,128)S(1)}) custom-call(s32[1]{0:T(128)} %bitcast.rank_ref, bf16[1,8192,512]{2,1,0:T(8,128)(2,1)} %values_ref.19, bf16[1,8192,512]{2,1,0:T(8,128)(2,1)} %cotangent_ref.19, bf16[32,256,256]{2,1,0:T(8,128)(2,1)} %left_ref.19, ...), custom_call_target="tpu_custom_call" | custom-call | flops 1024 | bytes 1024 | tf_op jit(solution)/shard_map/pallas_call | solution.py:256
  267.5 8.1 %collective-permute-done.50.refs_2_ = bf16[32,32,256]{2,1,0:T(8,128)(2,1)S(1)} collective-permute-done((bf16[32,32,256]{2,1,0:T(8,128)(2,1)}, bf16[32,32,256]{2,1,0:T(8,128)(2,1)S(1)}, u32[]{:S(2)}, u32[]{:S(2)}) %collective-permute-start.50) | collective-permute-done | bytes 524320 | tf_op jit(solution)/shard_map/ppermute | solution.py:191
  278.7 8.1 %collective-permute-done.52.refs_4_ = bf16[32,32,256]{2,1,0:T(8,128)(2,1)} collective-permute-done((bf16[32,32,256]{2,1,0:T(8,128)(2,1)}, bf16[32,32,256]{2,1,0:T(8,128)(2,1)}, u32[]{:S(2)}, u32[]{:S(2)}) %collective-permute-start.52) | collective-permute-done | bytes 524320 | tf_op jit(solution)/shard_map/ppermute | solution.py:191
  288.1 9.5 %collective-permute-done.53.refs_5_ = bf16[32,32,256]{2,1,0:T(8,128)(2,1)} collective-permute-done((bf16[32,32,256]{2,1,0:T(8,128)(2,1)}, bf16[32,32,256]{2,1,0:T(8,128)(2,1)}, u32[]{:S(2)}, u32[]{:S(2)}) %collective-permute-start.53) | collective-permute-done | bytes 524320 | tf_op jit(solution)/shard_map/ppermute | solution.py:191
  300.9 8.3 %collective-permute-done.42.refs_1_ = bf16[32,32,256]{2,1,0:T(8,128)(2,1)S(1)} collective-permute-done((bf16[32,32,256]{2,1,0:T(8,128)(2,1)}, bf16[32,32,256]{2,1,0:T(8,128)(2,1)S(1)}, u32[]{:S(2)}, u32[]{:S(2)}) %collective-permute-start.42) | collective-permute-done | bytes 524320 | tf_op jit(solution)/shard_map/ppermute | solution.py:191
  310.0 10.6 %collective-permute-done.43.refs_2_ = bf16[32,32,256]{2,1,0:T(8,128)(2,1)S(1)} collective-permute-done((bf16[32,32,256]{2,1,0:T(8,128)(2,1)}, bf16[32,32,256]{2,1,0:T(8,128)(2,1)S(1)}, u32[]{:S(2)}, u32[]{:S(2)}) %collective-permute-start.43) | collective-permute-done | bytes 524320 | tf_op jit(solution)/shard_map/ppermute | solution.py:191
  321.6 6.9 %shard_map.92 = (bf16[1,8192,512]{2,1,0:T(8,128)(2,1)}, bf16[1,8192,512]{2,1,0:T(8,128)(2,1)}, f32[2048,512]{1,0:T(8,128)}, f32[8,128]{1,0:T(8,128)S(1)}) custom-call(s32[1]{0:T(128)} %bitcast.rank_ref, bf16[1,8192,512]{2,1,0:T(8,128)(2,1)} %values_ref.19, ...), custom_call_target="tpu_custom_call", output_to_operand_aliasing={{0}: (12, {}), {1}: (13, {}), {2}: (14, {})} | custom-call | flops 1024 | bytes 1024 | tf_op jit(solution)/shard_map/pallas_call | solution.py:256
  333.2 9.5 %collective-permute-done.46.refs_5_ = bf16[32,32,256]{2,1,0:T(8,128)(2,1)} collective-permute-done((bf16[32,32,256]{2,1,0:T(8,128)(2,1)}, bf16[32,32,256]{2,1,0:T(8,128)(2,1)}, u32[]{:S(2)}, u32[]{:S(2)}) %collective-permute-start.46) | collective-permute-done | bytes 524320 | tf_op jit(solution)/shard_map/ppermute | solution.py:191
  345.9 7.3 %shard_map.93 = (bf16[1,8192,512]{2,1,0:T(8,128)(2,1)}, bf16[1,8192,512]{2,1,0:T(8,128)(2,1)}, f32[2048,512]{1,0:T(8,128)}, f32[8,128]{1,0:T(8,128)S(1)}) custom-call(s32[1]{0:T(128)} %bitcast.rank_ref, bf16[1,8192,512]{2,1,0:T(8,128)(2,1)} %values_ref.19, ...), custom_call_target="tpu_custom_call", output_to_operand_aliasing={{0}: (12, {}), {1}: (13, {}), {2}: (14, {})} | custom-call | flops 1024 | bytes 1024 | tf_op jit(solution)/shard_map/pallas_call | solution.py:256
  371.9 5.0 %collective-permute-done.57.refs_2_ = bf16[16,32,256]{2,1,0:T(8,128)(2,1)S(1)} collective-permute-done((bf16[16,32,256]{2,1,0:T(8,128)(2,1)}, bf16[16,32,256]{2,1,0:T(8,128)(2,1)S(1)}, u32[]{:S(2)}, u32[]{:S(2)}) %collective-permute-start.57) | collective-permute-done | bytes 262176 | tf_op jit(solution)/shard_map/ppermute | solution.py:191
  378.5 4.8 %shard_map.97 = (bf16[1,8192,512]{2,1,0:T(8,128)(2,1)}, bf16[1,8192,512]{2,1,0:T(8,128)(2,1)}, f32[2048,512]{1,0:T(8,128)}, f32[8,128]{1,0:T(8,128)}) custom-call(s32[1]{0:T(128)} %bitcast.rank_ref, bf16[1,8192,512]{2,1,0:T(8,128)(2,1)} %values_ref.19, ...), custom_call_target="tpu_custom_call", output_to_operand_aliasing={{0}: (13, {}), {1}: (14, {}), {2}: (15, {})} | custom-call | flops 1024 | bytes 1024 | tf_op jit(solution)/shard_map/pallas_call | solution.py:256
  383.4 4.4 %collective-permute-done.60.refs_5_ = bf16[16,32,256]{2,1,0:T(8,128)(2,1)} collective-permute-done((bf16[16,32,256]{2,1,0:T(8,128)(2,1)}, bf16[16,32,256]{2,1,0:T(8,128)(2,1)}, u32[]{:S(2)}, u32[]{:S(2)}) %collective-permute-start.60) | collective-permute-done | bytes 262176 | tf_op jit(solution)/shard_map/ppermute | solution.py:191
  (232 shorter events, 123.3 us)
Async XLA Ops:
  7.2 369.8 %reduce-scatter.2.cloned.1.call-start = ((), (), s32[]{:S(2)}) async-start(), calls=%async_computation.1 | async-start | bytes 10485760 | tf_op jit(solution)/shard_map/reduce_scatter | solution.py:338
  51.3 26.0 %collective-permute-start.3 = (bf16[32,32,256]{2,1,0:T(8,128)(2,1)}, bf16[32,32,256]{2,1,0:T(8,128)(2,1)S(1)}, u32[]{:S(2)}, u32[]{:S(2)}) collective-permute-start(bf16[32,32,256]{2,1,0:T(8,128)(2,1)} %get-tuple-element.168), channel_id=1, source_target_pairs={{0,6},{1,7},{2,4},{3,5},{4,2},{5,3},{6,0},{7,1},{8,14},{9,15},{10,... | collective-permute-start | bytes 1572872 | tf_op jit(solution)/shard_map/ppermute | solution.py:191
  54.4 30.3 %collective-permute-start.4 = (bf16[32,32,256]{2,1,0:T(8,128)(2,1)}, bf16[32,32,256]{2,1,0:T(8,128)(2,1)S(1)}, u32[]{:S(2)}, u32[]{:S(2)}) collective-permute-start(bf16[32,32,256]{2,1,0:T(8,128)(2,1)} %get-tuple-element.169), channel_id=1, source_target_pairs={{0,2},{1,3},{2,0},{3,1},{4,6},{5,7},{6,4},{7,5},{8,10},{9,11},{10,... | collective-permute-start | bytes 1572872 | tf_op jit(solution)/shard_map/ppermute | solution.py:191
  55.7 30.5 %collective-permute-start.5 = (bf16[32,32,256]{2,1,0:T(8,128)(2,1)}, bf16[32,32,256]{2,1,0:T(8,128)(2,1)S(1)}, u32[]{:S(2)}, u32[]{:S(2)}) collective-permute-start(bf16[32,32,256]{2,1,0:T(8,128)(2,1)} %get-tuple-element.170), channel_id=1, source_target_pairs={{0,4},{1,5},{2,6},{3,7},{4,0},{5,1},{6,2},{7,3},{8,12},{9,13},{10,... | collective-permute-start | bytes 1572872 | tf_op jit(solution)/shard_map/ppermute | solution.py:191
  62.0 33.1 %collective-permute-start.6 = (bf16[32,32,256]{2,1,0:T(8,128)(2,1)}, bf16[32,32,256]{2,1,0:T(8,128)(2,1)S(1)}, u32[]{:S(2)}, u32[]{:S(2)}) collective-permute-start(bf16[32,32,256]{2,1,0:T(8,128)(2,1)} %get-tuple-element.171), channel_id=1, source_target_pairs={{0,7},{1,6},{2,5},{3,4},{4,3},{5,2},{6,1},{7,0},{8,15},{9,14},{10,... | collective-permute-start | bytes 1572872 | tf_op jit(solution)/shard_map/ppermute | solution.py:191
  77.1 31.2 %collective-permute-start.7 = (bf16[32,32,256]{2,1,0:T(8,128)(2,1)}, bf16[32,32,256]{2,1,0:T(8,128)(2,1)S(1)}, u32[]{:S(2)}, u32[]{:S(2)}) collective-permute-start(bf16[32,32,256]{2,1,0:T(8,128)(2,1)} %get-tuple-element.172), channel_id=1, source_target_pairs={{0,3},{1,2},{2,1},{3,0},{4,7},{5,6},{6,5},{7,4},{8,11},{9,10},{10,... | collective-permute-start | bytes 1572872 | tf_op jit(solution)/shard_map/ppermute | solution.py:191
  77.3 40.6 %collective-permute-start.28 = (bf16[32,32,256]{2,1,0:T(8,128)(2,1)}, bf16[32,32,256]{2,1,0:T(8,128)(2,1)S(1)}, u32[]{:S(2)}, u32[]{:S(2)}) collective-permute-start(bf16[32,32,256]{2,1,0:T(8,128)(2,1)} %get-tuple-element.202), channel_id=1, source_target_pairs={{0,6},{1,7},{2,4},{3,5},{4,2},{5,3},{6,0},{7,1},{8,14},{9,15},{10,... | collective-permute-start | bytes 1572872 | tf_op jit(solution)/shard_map/ppermute | solution.py:191
  84.7 45.0 %collective-permute-start.29 = (bf16[32,32,256]{2,1,0:T(8,128)(2,1)}, bf16[32,32,256]{2,1,0:T(8,128)(2,1)S(1)}, u32[]{:S(2)}, u32[]{:S(2)}) collective-permute-start(bf16[32,32,256]{2,1,0:T(8,128)(2,1)} %get-tuple-element.203), channel_id=1, source_target_pairs={{0,2},{1,3},{2,0},{3,1},{4,6},{5,7},{6,4},{7,5},{8,10},{9,11},{10,... | collective-permute-start | bytes 1572872 | tf_op jit(solution)/shard_map/ppermute | solution.py:191
  86.2 43.5 %collective-permute-start.8 = (bf16[32,32,256]{2,1,0:T(8,128)(2,1)}, bf16[32,32,256]{2,1,0:T(8,128)(2,1)}, u32[]{:S(2)}, u32[]{:S(2)}) collective-permute-start(bf16[32,32,256]{2,1,0:T(8,128)(2,1)} %get-tuple-element.176), channel_id=1, source_target_pairs={{0,5},{1,4},{2,7},{3,6},{4,1},{5,0},{6,3},{7,2},{8,13},{9,12},{10,... | collective-permute-start | bytes 1572872 | tf_op jit(solution)/shard_map/ppermute | solution.py:191
  95.1 36.3 %collective-permute-start.9 = (bf16[32,32,256]{2,1,0:T(8,128)(2,1)}, bf16[32,32,256]{2,1,0:T(8,128)(2,1)}, u32[]{:S(2)}, u32[]{:S(2)}) collective-permute-start(bf16[32,32,256]{2,1,0:T(8,128)(2,1)} %get-tuple-element.177), channel_id=1, source_target_pairs={{0,1},{1,0},{2,3},{3,2},{4,5},{5,4},{6,7},{7,6},{8,9},{9,8},{10,11... | collective-permute-start | bytes 1572872 | tf_op jit(solution)/shard_map/ppermute | solution.py:191
  108.3 36.2 %collective-permute-start.30 = (bf16[32,32,256]{2,1,0:T(8,128)(2,1)}, bf16[32,32,256]{2,1,0:T(8,128)(2,1)S(1)}, u32[]{:S(2)}, u32[]{:S(2)}) collective-permute-start(bf16[32,32,256]{2,1,0:T(8,128)(2,1)} %get-tuple-element.204), channel_id=1, source_target_pairs={{0,4},{1,5},{2,6},{3,7},{4,0},{5,1},{6,2},{7,3},{8,12},{9,13},{10,... | collective-permute-start | bytes 1572872 | tf_op jit(solution)/shard_map/ppermute | solution.py:191
  117.9 28.2 %collective-permute-start.31 = (bf16[32,32,256]{2,1,0:T(8,128)(2,1)}, bf16[32,32,256]{2,1,0:T(8,128)(2,1)S(1)}, u32[]{:S(2)}, u32[]{:S(2)}) collective-permute-start(bf16[32,32,256]{2,1,0:T(8,128)(2,1)} %get-tuple-element.209), channel_id=1, source_target_pairs={{0,7},{1,6},{2,5},{3,4},{4,3},{5,2},{6,1},{7,0},{8,15},{9,14},{10,... | collective-permute-start | bytes 1572872 | tf_op jit(solution)/shard_map/ppermute | solution.py:191
  146.8 27.9 %collective-permute-start.1 = (bf16[32,32,256]{2,1,0:T(8,128)(2,1)}, bf16[32,32,256]{2,1,0:T(8,128)(2,1)S(1)}, u32[]{:S(2)}, u32[]{:S(2)}) collective-permute-start(bf16[32,32,256]{2,1,0:T(8,128)(2,1)} %get-tuple-element.161), channel_id=1, source_target_pairs={{0,2},{1,3},{2,0},{3,1},{4,6},{5,7},{6,4},{7,5},{8,10},{9,11},{10,... | collective-permute-start | bytes 1572872 | tf_op jit(solution)/shard_map/ppermute | solution.py:191
  151.8 33.3 %collective-permute-start.24 = (bf16[32,32,256]{2,1,0:T(8,128)(2,1)}, bf16[32,32,256]{2,1,0:T(8,128)(2,1)S(1)}, u32[]{:S(2)}, u32[]{:S(2)}) collective-permute-start(bf16[32,32,256]{2,1,0:T(8,128)(2,1)} %get-tuple-element.197), channel_id=1, source_target_pairs={{0,7},{1,6},{2,5},{3,4},{4,3},{5,2},{6,1},{7,0},{8,15},{9,14},{10,... | collective-permute-start | bytes 1572872 | tf_op jit(solution)/shard_map/ppermute | solution.py:191
  154.7 41.7 %collective-permute-start.25 = (bf16[32,32,256]{2,1,0:T(8,128)(2,1)}, bf16[32,32,256]{2,1,0:T(8,128)(2,1)S(1)}, u32[]{:S(2)}, u32[]{:S(2)}) collective-permute-start(bf16[32,32,256]{2,1,0:T(8,128)(2,1)} %get-tuple-element.198), channel_id=1, source_target_pairs={{0,3},{1,2},{2,1},{3,0},{4,7},{5,6},{6,5},{7,4},{8,11},{9,10},{10,... | collective-permute-start | bytes 1572872 | tf_op jit(solution)/shard_map/ppermute | solution.py:191
  167.9 29.7 %collective-permute-start.26 = (bf16[32,32,256]{2,1,0:T(8,128)(2,1)}, bf16[32,32,256]{2,1,0:T(8,128)(2,1)}, u32[]{:S(2)}, u32[]{:S(2)}) collective-permute-start(bf16[32,32,256]{2,1,0:T(8,128)(2,1)} %get-tuple-element.199), channel_id=1, source_target_pairs={{0,5},{1,4},{2,7},{3,6},{4,1},{5,0},{6,3},{7,2},{8,13},{9,12},{10,... | collective-permute-start | bytes 1572872 | tf_op jit(solution)/shard_map/ppermute | solution.py:191
  174.8 36.0 %collective-permute-start.35 = (bf16[32,32,256]{2,1,0:T(8,128)(2,1)}, bf16[32,32,256]{2,1,0:T(8,128)(2,1)S(1)}, u32[]{:S(2)}, u32[]{:S(2)}) collective-permute-start(bf16[32,32,256]{2,1,0:T(8,128)(2,1)} %get-tuple-element.237), channel_id=1, source_target_pairs={{0,6},{1,7},{2,4},{3,5},{4,2},{5,3},{6,0},{7,1},{8,14},{9,15},{10,... | collective-permute-start | bytes 1572872 | tf_op jit(solution)/shard_map/ppermute | solution.py:191
  185.2 33.5 %collective-permute-start.36 = (bf16[32,32,256]{2,1,0:T(8,128)(2,1)}, bf16[32,32,256]{2,1,0:T(8,128)(2,1)S(1)}, u32[]{:S(2)}, u32[]{:S(2)}) collective-permute-start(bf16[32,32,256]{2,1,0:T(8,128)(2,1)} %get-tuple-element.238), channel_id=1, source_target_pairs={{0,2},{1,3},{2,0},{3,1},{4,6},{5,7},{6,4},{7,5},{8,10},{9,11},{10,... | collective-permute-start | bytes 1572872 | tf_op jit(solution)/shard_map/ppermute | solution.py:191
  229.0 25.1 %collective-permute-start.40 = (bf16[32,32,256]{2,1,0:T(8,128)(2,1)}, bf16[32,32,256]{2,1,0:T(8,128)(2,1)}, u32[]{:S(2)}, u32[]{:S(2)}) collective-permute-start(bf16[32,32,256]{2,1,0:T(8,128)(2,1)} %get-tuple-element.242), channel_id=1, source_target_pairs={{0,5},{1,4},{2,7},{3,6},{4,1},{5,0},{6,3},{7,2},{8,13},{9,12},{10,... | collective-permute-start | bytes 1572872 | tf_op jit(solution)/shard_map/ppermute | solution.py:191
  229.1 27.2 %collective-permute-start.41 = (bf16[32,32,256]{2,1,0:T(8,128)(2,1)}, bf16[32,32,256]{2,1,0:T(8,128)(2,1)}, u32[]{:S(2)}, u32[]{:S(2)}) collective-permute-start(bf16[32,32,256]{2,1,0:T(8,128)(2,1)} %get-tuple-element.243), channel_id=1, source_target_pairs={{0,1},{1,0},{2,3},{3,2},{4,5},{5,4},{6,7},{7,6},{8,9},{9,8},{10,11... | collective-permute-start | bytes 1572872 | tf_op jit(solution)/shard_map/ppermute | solution.py:191
  229.7 37.3 %collective-permute-start.49 = (bf16[32,32,256]{2,1,0:T(8,128)(2,1)}, bf16[32,32,256]{2,1,0:T(8,128)(2,1)S(1)}, u32[]{:S(2)}, u32[]{:S(2)}) collective-permute-start(bf16[32,32,256]{2,1,0:T(8,128)(2,1)} %get-tuple-element.260), channel_id=1, source_target_pairs={{0,6},{1,7},{2,4},{3,5},{4,2},{5,3},{6,0},{7,1},{8,14},{9,15},{10,... | collective-permute-start | bytes 1572872 | tf_op jit(solution)/shard_map/ppermute | solution.py:191
  242.4 33.1 %collective-permute-start.50 = (bf16[32,32,256]{2,1,0:T(8,128)(2,1)}, bf16[32,32,256]{2,1,0:T(8,128)(2,1)S(1)}, u32[]{:S(2)}, u32[]{:S(2)}) collective-permute-start(bf16[32,32,256]{2,1,0:T(8,128)(2,1)} %get-tuple-element.261), channel_id=1, source_target_pairs={{0,2},{1,3},{2,0},{3,1},{4,6},{5,7},{6,4},{7,5},{8,10},{9,11},{10,... | collective-permute-start | bytes 1572872 | tf_op jit(solution)/shard_map/ppermute | solution.py:191
  254.2 32.6 %collective-permute-start.52 = (bf16[32,32,256]{2,1,0:T(8,128)(2,1)}, bf16[32,32,256]{2,1,0:T(8,128)(2,1)}, u32[]{:S(2)}, u32[]{:S(2)}) collective-permute-start(bf16[32,32,256]{2,1,0:T(8,128)(2,1)} %get-tuple-element.263), channel_id=1, source_target_pairs={{0,7},{1,6},{2,5},{3,4},{4,3},{5,2},{6,1},{7,0},{8,15},{9,14},{10,... | collective-permute-start | bytes 1572872 | tf_op jit(solution)/shard_map/ppermute | solution.py:191
  256.3 41.3 %collective-permute-start.53 = (bf16[32,32,256]{2,1,0:T(8,128)(2,1)}, bf16[32,32,256]{2,1,0:T(8,128)(2,1)}, u32[]{:S(2)}, u32[]{:S(2)}) collective-permute-start(bf16[32,32,256]{2,1,0:T(8,128)(2,1)} %get-tuple-element.264), channel_id=1, source_target_pairs={{0,3},{1,2},{2,1},{3,0},{4,7},{5,6},{6,5},{7,4},{8,11},{9,10},{10,... | collective-permute-start | bytes 1572872 | tf_op jit(solution)/shard_map/ppermute | solution.py:191
  267.1 31.4 %collective-permute-start.54 = (bf16[32,32,256]{2,1,0:T(8,128)(2,1)}, bf16[32,32,256]{2,1,0:T(8,128)(2,1)S(1)}, u32[]{:S(2)}, u32[]{:S(2)}) collective-permute-start(bf16[32,32,256]{2,1,0:T(8,128)(2,1)} %get-tuple-element.265), channel_id=1, source_target_pairs={{0,5},{1,4},{2,7},{3,6},{4,1},{5,0},{6,3},{7,2},{8,13},{9,12},{10,... | collective-permute-start | bytes 1572872 | tf_op jit(solution)/shard_map/ppermute | solution.py:191
  275.5 25.0 %collective-permute-start.55 = (bf16[32,32,256]{2,1,0:T(8,128)(2,1)}, bf16[32,32,256]{2,1,0:T(8,128)(2,1)S(1)}, u32[]{:S(2)}, u32[]{:S(2)}) collective-permute-start(bf16[32,32,256]{2,1,0:T(8,128)(2,1)} %get-tuple-element.266), channel_id=1, source_target_pairs={{0,1},{1,0},{2,3},{3,2},{4,5},{5,4},{6,7},{7,6},{8,9},{9,8},{10,11... | collective-permute-start | bytes 1572872 | tf_op jit(solution)/shard_map/ppermute | solution.py:191
  276.3 32.8 %collective-permute-start.42 = (bf16[32,32,256]{2,1,0:T(8,128)(2,1)}, bf16[32,32,256]{2,1,0:T(8,128)(2,1)S(1)}, u32[]{:S(2)}, u32[]{:S(2)}) collective-permute-start(bf16[32,32,256]{2,1,0:T(8,128)(2,1)} %get-tuple-element.245), channel_id=1, source_target_pairs={{0,6},{1,7},{2,4},{3,5},{4,2},{5,3},{6,0},{7,1},{8,14},{9,15},{10,... | collective-permute-start | bytes 1572872 | tf_op jit(solution)/shard_map/ppermute | solution.py:191
  286.7 33.8 %collective-permute-start.43 = (bf16[32,32,256]{2,1,0:T(8,128)(2,1)}, bf16[32,32,256]{2,1,0:T(8,128)(2,1)S(1)}, u32[]{:S(2)}, u32[]{:S(2)}) collective-permute-start(bf16[32,32,256]{2,1,0:T(8,128)(2,1)} %get-tuple-element.246), channel_id=1, source_target_pairs={{0,2},{1,3},{2,0},{3,1},{4,6},{5,7},{6,4},{7,5},{8,10},{9,11},{10,... | collective-permute-start | bytes 1572872 | tf_op jit(solution)/shard_map/ppermute | solution.py:191
  297.6 31.5 %collective-permute-start.44 = (bf16[32,32,256]{2,1,0:T(8,128)(2,1)}, bf16[32,32,256]{2,1,0:T(8,128)(2,1)}, u32[]{:S(2)}, u32[]{:S(2)}) collective-permute-start(bf16[32,32,256]{2,1,0:T(8,128)(2,1)} %get-tuple-element.247), channel_id=1, source_target_pairs={{0,4},{1,5},{2,6},{3,7},{4,0},{5,1},{6,2},{7,3},{8,12},{9,13},{10,... | collective-permute-start | bytes 1572872 | tf_op jit(solution)/shard_map/ppermute | solution.py:191
  298.5 33.3 %collective-permute-start.45 = (bf16[32,32,256]{2,1,0:T(8,128)(2,1)}, bf16[32,32,256]{2,1,0:T(8,128)(2,1)}, u32[]{:S(2)}, u32[]{:S(2)}) collective-permute-start(bf16[32,32,256]{2,1,0:T(8,128)(2,1)} %get-tuple-element.248), channel_id=1, source_target_pairs={{0,7},{1,6},{2,5},{3,4},{4,3},{5,2},{6,1},{7,0},{8,15},{9,14},{10,... | collective-permute-start | bytes 1572872 | tf_op jit(solution)/shard_map/ppermute | solution.py:191
  300.5 42.1 %collective-permute-start.46 = (bf16[32,32,256]{2,1,0:T(8,128)(2,1)}, bf16[32,32,256]{2,1,0:T(8,128)(2,1)}, u32[]{:S(2)}, u32[]{:S(2)}) collective-permute-start(bf16[32,32,256]{2,1,0:T(8,128)(2,1)} %get-tuple-element.249), channel_id=1, source_target_pairs={{0,3},{1,2},{2,1},{3,0},{4,7},{5,6},{6,5},{7,4},{8,11},{9,10},{10,... | collective-permute-start | bytes 1572872 | tf_op jit(solution)/shard_map/ppermute | solution.py:191
  309.1 34.4 %collective-permute-start.47 = (bf16[32,32,256]{2,1,0:T(8,128)(2,1)}, bf16[32,32,256]{2,1,0:T(8,128)(2,1)}, u32[]{:S(2)}, u32[]{:S(2)}) collective-permute-start(bf16[32,32,256]{2,1,0:T(8,128)(2,1)} %get-tuple-element.250), channel_id=1, source_target_pairs={{0,5},{1,4},{2,7},{3,6},{4,1},{5,0},{6,3},{7,2},{8,13},{9,12},{10,... | collective-permute-start | bytes 1572872 | tf_op jit(solution)/shard_map/ppermute | solution.py:191
  (88 other events, 1372.1 us)
Sparse Core Ops, SparseCore 0:
  225.5 145.5 reduce-scatter.1

commit v6 on v4

--- a/solution.py
+++ b/solution.py
@@ -276,7 +276,7 @@
                 ],
             ),
             input_output_aliases=aliases,
-            compiler_params=params,
+            compiler_params=pltpu.CompilerParams(vmem_limit_bytes=40 * 1024 * 1024),
             cost_estimate=COST,
         )(rank, values, cotangent, left_factor, *arrived, *reduced, *earlier, *after)
 

time: 393 us -> 393 us (level)
  local copies, waits for them, and re-layouts: 5.85 us -> 23.2 us
  waiting for transfers between devices: 188 us -> 177 us
  Pallas kernels: 112 us -> 105 us
    unnamed x122 -> x112, local copies, waits for them, and re-layouts: 5.85 us -> 23.2 us
    ppermute x70, waiting for transfers between devices: 188 us -> 177 us  [exchange(): lax.ppermute(sends[n], 'seq', [(r, r ^ moves[n]) for r in range(ranks)])]
    pallas_call x5, Pallas kernels: 32.9 us -> 25.9 us  [left_back(): pl.pallas_call(functools.partial(left_back_kernel, ranks, terms), out_sha...]
  transfers between devices with their start and end apart: 71 -> 71, of which waited for: 31 -> 29; matrix products, arithmetic and copies ran while one was open for 0% -> 0% of each run, Pallas kernels for 27% -> 25%
where the time goes in v6:
time: 393 us; the launch traced here: 392 us
  waiting for transfers between devices  177 us (45%)
  Pallas kernels  105 us (27%)
  starting transfers between devices  72 us (18%)
  local copies, waits for them, and re-layouts  23.2 us (6%)
  between operations  14.5 us (4%)
    ppermute x70, waiting for transfers between devices, exchange(): lax.ppermute(sends[n], 'seq', [(r, r ^ moves[n]) for r in range(ranks)])  177 us
    ppermute x70, starting transfers between devices, exchange(): lax.ppermute(sends[n], 'seq', [(r, r ^ moves[n]) for r in range(ranks)])  71.9 us
    pallas_call x4, Pallas kernels, right_both(): pl.pallas_call(functools.partial(right_kernel, ranks, ins, outs), out_sha...  52.6 us
    pallas_call x5, Pallas kernels, left_forward(): pl.pallas_call(functools.partial(left_forward_kernel, ranks), out_shape=[...  26.7 us
    pallas_call x5, Pallas kernels, left_back(): pl.pallas_call(functools.partial(left_back_kernel, ranks, terms), out_sha...  25.9 us
    unnamed x112, local copies, waits for them, and re-layouts  23.2 us
  transfers between devices with their start and end apart: 71, of which 29 were waited for; matrix products, arithmetic and copies ran while one was open for 0% of the time, Pallas kernels for 25%

profile of v6, /device:TPU:0, one launch (start us, length us, event | category | flops | bytes accessed | tf_op | source)
XLA Modules:
  0.0 392.2 jit_solution(1135644426324422347)
XLA Ops:
  10.8 3.9 %collective-permute-start.10 = (bf16[16,32,256]{2,1,0:T(8,128)(2,1)}, bf16[16,32,256]{2,1,0:T(8,128)(2,1)S(1)}, u32[]{:S(2)}, u32[]{:S(2)}) collective-permute-start(bf16[16,32,256]{2,1,0:T(8,128)(2,1)} %get-tuple-element.179), channel_id=1, source_target_pairs={{0,6},{1,7},{2,4},{3,5},{4,2},{5,3},{6,0},{7,1},{8,14},{9,15},{10,... | collective-permute-start | bytes 786440 | tf_op jit(solution)/shard_map/ppermute | solution.py:191
  22.2 6.3 %collective-permute-done.11.refs_2_ = bf16[16,32,256]{2,1,0:T(8,128)(2,1)} collective-permute-done((bf16[16,32,256]{2,1,0:T(8,128)(2,1)}, bf16[16,32,256]{2,1,0:T(8,128)(2,1)}, u32[]{:S(2)}, u32[]{:S(2)}) %collective-permute-start.11) | collective-permute-done | bytes 262176 | tf_op jit(solution)/shard_map/ppermute | solution.py:191
  33.8 5.0 %collective-permute-done.14.refs_5_ = bf16[16,32,256]{2,1,0:T(8,128)(2,1)S(1)} collective-permute-done((bf16[16,32,256]{2,1,0:T(8,128)(2,1)}, bf16[16,32,256]{2,1,0:T(8,128)(2,1)S(1)}, u32[]{:S(2)}, u32[]{:S(2)}) %collective-permute-start.14) | collective-permute-done | bytes 262176 | tf_op jit(solution)/shard_map/ppermute | solution.py:191
  44.7 6.5 %shard_map.78 = (bf16[32,32,256]{2,1,0:T(8,128)(2,1)}, bf16[32,32,256]{2,1,0:T(8,128)(2,1)}, bf16[32,32,256]{2,1,0:T(8,128)(2,1)}, bf16[32,32,256]{2,1,0:T(8,128...) custom-call(s32[1]{0:T(128)} %bitcast.rank_ref, ...), custom_call_target="tpu_custom_call" | custom-call | flops 1024 | bytes 1024 | tf_op jit(solution)/shard_map/pallas_call | solution.py:174
  56.2 5.1 %collective-permute-done.21.refs_13_ = bf16[16,32,256]{2,1,0:T(8,128)(2,1)S(1)} collective-permute-done((bf16[16,32,256]{2,1,0:T(8,128)(2,1)}, bf16[16,32,256]{2,1,0:T(8,128)(2,1)S(1)}, u32[]{:S(2)}, u32[]{:S(2)}) %collective-permute-start.21) | collective-permute-done | bytes 262176 | tf_op jit(solution)/shard_map/ppermute | solution.py:191
  64.1 6.5 %shard_map.79 = (bf16[32,32,256]{2,1,0:T(8,128)(2,1)}, bf16[32,32,256]{2,1,0:T(8,128)(2,1)}, bf16[32,32,256]{2,1,0:T(8,128)(2,1)}, bf16[32,32,256]{2,1,0:T(8,128...) custom-call(s32[1]{0:T(128)} %bitcast.rank_ref, ...), custom_call_target="tpu_custom_call" | custom-call | flops 1024 | bytes 1024 | tf_op jit(solution)/shard_map/pallas_call | solution.py:174
  70.6 6.5 %shard_map.80 = (bf16[32,32,256]{2,1,0:T(8,128)(2,1)}, bf16[32,32,256]{2,1,0:T(8,128)(2,1)}, bf16[32,32,256]{2,1,0:T(8,128)(2,1)}, bf16[32,32,256]{2,1,0:T(8,128...) custom-call(s32[1]{0:T(128)} %bitcast.rank_ref, ...), custom_call_target="tpu_custom_call" | custom-call | flops 1024 | bytes 1024 | tf_op jit(solution)/shard_map/pallas_call | solution.py:174
  80.3 4.4 %collective-permute-done.4.refs_2_ = bf16[32,32,256]{2,1,0:T(8,128)(2,1)S(1)} collective-permute-done((bf16[32,32,256]{2,1,0:T(8,128)(2,1)}, bf16[32,32,256]{2,1,0:T(8,128)(2,1)S(1)}, u32[]{:S(2)}, u32[]{:S(2)}) %collective-permute-start.4) | collective-permute-done | bytes 524320 | tf_op jit(solution)/shard_map/ppermute | solution.py:191
  86.2 8.9 %collective-permute-done.6.refs_4_ = bf16[32,32,256]{2,1,0:T(8,128)(2,1)S(1)} collective-permute-done((bf16[32,32,256]{2,1,0:T(8,128)(2,1)}, bf16[32,32,256]{2,1,0:T(8,128)(2,1)S(1)}, u32[]{:S(2)}, u32[]{:S(2)}) %collective-permute-start.6) | collective-permute-done | bytes 524320 | tf_op jit(solution)/shard_map/ppermute | solution.py:191
  95.2 13.1 %shard_map.82 = (bf16[32,32,256]{2,1,0:T(8,128)(2,1)}, bf16[32,32,256]{2,1,0:T(8,128)(2,1)}, bf16[32,32,256]{2,1,0:T(8,128)(2,1)}, bf16[32,32,256]{2,1,0:T(8,128...) custom-call(s32[1]{0:T(128)} %bitcast.rank_ref, ...), custom_call_target="tpu_custom_call" | custom-call | flops 1024 | bytes 1024 | tf_op jit(solution)/shard_map/pallas_call | solution.py:203
  110.4 7.5 %collective-permute-done.28.refs_1_ = bf16[32,32,256]{2,1,0:T(8,128)(2,1)S(1)} collective-permute-done((bf16[32,32,256]{2,1,0:T(8,128)(2,1)}, bf16[32,32,256]{2,1,0:T(8,128)(2,1)S(1)}, u32[]{:S(2)}, u32[]{:S(2)}) %collective-permute-start.28) | collective-permute-done | bytes 524320 | tf_op jit(solution)/shard_map/ppermute | solution.py:191
  118.3 11.4 %collective-permute-done.29.refs_2_ = bf16[32,32,256]{2,1,0:T(8,128)(2,1)S(1)} collective-permute-done((bf16[32,32,256]{2,1,0:T(8,128)(2,1)}, bf16[32,32,256]{2,1,0:T(8,128)(2,1)S(1)}, u32[]{:S(2)}, u32[]{:S(2)}) %collective-permute-start.29) | collective-permute-done | bytes 524320 | tf_op jit(solution)/shard_map/ppermute | solution.py:191
  131.4 13.1 %shard_map.83 = (bf16[32,32,256]{2,1,0:T(8,128)(2,1)}, bf16[32,32,256]{2,1,0:T(8,128)(2,1)}, bf16[32,32,256]{2,1,0:T(8,128)(2,1)}, bf16[32,32,256]{2,1,0:T(8,128...) custom-call(s32[1]{0:T(128)} %bitcast.rank_ref, ...), custom_call_target="tpu_custom_call", output_to_operand_aliasing={{8}: (11, {})} | custom-call | flops 1024 | bytes 1024 | tf_op jit(solution)/shard_map/pallas_call | solution.py:203
  154.7 13.2 %shard_map.86 = (bf16[32,32,256]{2,1,0:T(8,128)(2,1)}, bf16[32,32,256]{2,1,0:T(8,128)(2,1)}, bf16[32,32,256]{2,1,0:T(8,128)(2,1)}, bf16[32,32,256]{2,1,0:T(8,128...) custom-call(s32[1]{0:T(128)} %bitcast.rank_ref, ...), custom_call_target="tpu_custom_call", output_to_operand_aliasing={{8}: (11, {})} | custom-call | flops 1024 | bytes 1024 | tf_op jit(solution)/shard_map/pallas_call | solution.py:203
  168.5 6.2 %collective-permute-done.1.refs_2_ = bf16[32,32,256]{2,1,0:T(8,128)(2,1)S(1)} collective-permute-done((bf16[32,32,256]{2,1,0:T(8,128)(2,1)}, bf16[32,32,256]{2,1,0:T(8,128)(2,1)S(1)}, u32[]{:S(2)}, u32[]{:S(2)}) %collective-permute-start.1) | collective-permute-done | bytes 524320 | tf_op jit(solution)/shard_map/ppermute | solution.py:191
  176.9 8.3 %collective-permute-done.24.refs_4_ = bf16[32,32,256]{2,1,0:T(8,128)(2,1)S(1)} collective-permute-done((bf16[32,32,256]{2,1,0:T(8,128)(2,1)}, bf16[32,32,256]{2,1,0:T(8,128)(2,1)S(1)}, u32[]{:S(2)}, u32[]{:S(2)}) %collective-permute-start.24) | collective-permute-done | bytes 524320 | tf_op jit(solution)/shard_map/ppermute | solution.py:191
  185.7 10.7 %collective-permute-done.25.refs_5_ = bf16[32,32,256]{2,1,0:T(8,128)(2,1)S(1)} collective-permute-done((bf16[32,32,256]{2,1,0:T(8,128)(2,1)}, bf16[32,32,256]{2,1,0:T(8,128)(2,1)S(1)}, u32[]{:S(2)}, u32[]{:S(2)}) %collective-permute-start.25) | collective-permute-done | bytes 524320 | tf_op jit(solution)/shard_map/ppermute | solution.py:191
  197.7 13.2 %shard_map.87 = (bf16[16,32,256]{2,1,0:T(8,128)(2,1)}, bf16[16,32,256]{2,1,0:T(8,128)(2,1)}, bf16[16,32,256]{2,1,0:T(8,128)(2,1)}, bf16[16,32,256]{2,1,0:T(8,128...) custom-call(s32[1]{0:T(128)} %bitcast.rank_ref, ...), custom_call_target="tpu_custom_call", output_to_operand_aliasing={{16}: (11, {})} | custom-call | flops 1024 | bytes 1024 | tf_op jit(solution)/shard_map/pallas_call | solution.py:203
  210.9 7.7 %collective-permute-done.36.refs_2_ = bf16[32,32,256]{2,1,0:T(8,128)(2,1)S(1)} collective-permute-done((bf16[32,32,256]{2,1,0:T(8,128)(2,1)}, bf16[32,32,256]{2,1,0:T(8,128)(2,1)S(1)}, u32[]{:S(2)}, u32[]{:S(2)}) %collective-permute-start.36) | collective-permute-done | bytes 524320 | tf_op jit(solution)/shard_map/ppermute | solution.py:191
  226.1 9.7 %collective-permute-done.38.refs_4_ = bf16[32,32,256]{2,1,0:T(8,128)(2,1)S(1)} collective-permute-done((bf16[32,32,256]{2,1,0:T(8,128)(2,1)S(1)}, bf16[32,32,256]{2,1,0:T(8,128)(2,1)S(1)}, u32[]{:S(2)}, u32[]{:S(2)}) %collective-permute-start.38) | collective-permute-done | bytes 524320 | tf_op jit(solution)/shard_map/ppermute | solution.py:191
  238.2 8.4 %collective-permute-done.39.refs_5_ = bf16[32,32,256]{2,1,0:T(8,128)(2,1)S(1)} collective-permute-done((bf16[32,32,256]{2,1,0:T(8,128)(2,1)}, bf16[32,32,256]{2,1,0:T(8,128)(2,1)S(1)}, u32[]{:S(2)}, u32[]{:S(2)}) %collective-permute-start.39) | collective-permute-done | bytes 524320 | tf_op jit(solution)/shard_map/ppermute | solution.py:191
  255.9 6.0 %shard_map.89 = (bf16[1,8192,512]{2,1,0:T(8,128)(2,1)}, bf16[1,8192,512]{2,1,0:T(8,128)(2,1)}, f32[2048,512]{1,0:T(8,128)}, f32[8,128]{1,0:T(8,128)S(1)}) custom-call(s32[1]{0:T(128)} %bitcast.rank_ref, bf16[1,8192,512]{2,1,0:T(8,128)(2,1)} %values_ref.19, bf16[1,8192,512]{2,1,0:T(8,128)(2,1)} %cotangent_ref.19, bf16[32,256,256]{2,1,0:T(8,128)(2,1)S(1)} %copy-done, ...), custom_call_target="tpu_custom_call" | custom-call | flops 1024 | bytes 1024 | tf_op jit(solution)/shard_map/pallas_call | solution.py:256
  263.1 6.5 %collective-permute-done.50.refs_2_ = bf16[32,32,256]{2,1,0:T(8,128)(2,1)S(1)} collective-permute-done((bf16[32,32,256]{2,1,0:T(8,128)(2,1)}, bf16[32,32,256]{2,1,0:T(8,128)(2,1)S(1)}, u32[]{:S(2)}, u32[]{:S(2)}) %collective-permute-start.50) | collective-permute-done | bytes 524320 | tf_op jit(solution)/shard_map/ppermute | solution.py:191
  272.8 8.1 %collective-permute-done.52.refs_4_ = bf16[32,32,256]{2,1,0:T(8,128)(2,1)} collective-permute-done((bf16[32,32,256]{2,1,0:T(8,128)(2,1)}, bf16[32,32,256]{2,1,0:T(8,128)(2,1)}, u32[]{:S(2)}, u32[]{:S(2)}) %collective-permute-start.52) | collective-permute-done | bytes 524320 | tf_op jit(solution)/shard_map/ppermute | solution.py:191
  282.5 9.2 %collective-permute-done.53.refs_5_ = bf16[32,32,256]{2,1,0:T(8,128)(2,1)} collective-permute-done((bf16[32,32,256]{2,1,0:T(8,128)(2,1)}, bf16[32,32,256]{2,1,0:T(8,128)(2,1)}, u32[]{:S(2)}, u32[]{:S(2)}) %collective-permute-start.53) | collective-permute-done | bytes 524320 | tf_op jit(solution)/shard_map/ppermute | solution.py:191
  294.9 8.1 %collective-permute-done.42.refs_1_ = bf16[32,32,256]{2,1,0:T(8,128)(2,1)S(1)} collective-permute-done((bf16[32,32,256]{2,1,0:T(8,128)(2,1)}, bf16[32,32,256]{2,1,0:T(8,128)(2,1)S(1)}, u32[]{:S(2)}, u32[]{:S(2)}) %collective-permute-start.42) | collective-permute-done | bytes 524320 | tf_op jit(solution)/shard_map/ppermute | solution.py:191
  304.0 10.6 %collective-permute-done.43.refs_2_ = bf16[32,32,256]{2,1,0:T(8,128)(2,1)S(1)} collective-permute-done((bf16[32,32,256]{2,1,0:T(8,128)(2,1)}, bf16[32,32,256]{2,1,0:T(8,128)(2,1)S(1)}, u32[]{:S(2)}, u32[]{:S(2)}) %collective-permute-start.43) | collective-permute-done | bytes 524320 | tf_op jit(solution)/shard_map/ppermute | solution.py:191
  317.9 6.0 %shard_map.92 = (bf16[1,8192,512]{2,1,0:T(8,128)(2,1)}, bf16[1,8192,512]{2,1,0:T(8,128)(2,1)}, f32[2048,512]{1,0:T(8,128)}, f32[8,128]{1,0:T(8,128)S(1)}) custom-call(s32[1]{0:T(128)} %bitcast.rank_ref, bf16[1,8192,512]{2,1,0:T(8,128)(2,1)} %values_ref.19, ...), custom_call_target="tpu_custom_call", output_to_operand_aliasing={{0}: (12, {}), {1}: (13, {}), {2}: (14, {})} | custom-call | flops 1024 | bytes 1024 | tf_op jit(solution)/shard_map/pallas_call | solution.py:256
  327.5 9.2 %collective-permute-done.46.refs_5_ = bf16[32,32,256]{2,1,0:T(8,128)(2,1)} collective-permute-done((bf16[32,32,256]{2,1,0:T(8,128)(2,1)}, bf16[32,32,256]{2,1,0:T(8,128)(2,1)}, u32[]{:S(2)}, u32[]{:S(2)}) %collective-permute-start.46) | collective-permute-done | bytes 524320 | tf_op jit(solution)/shard_map/ppermute | solution.py:191
  342.2 6.1 %shard_map.93 = (bf16[1,8192,512]{2,1,0:T(8,128)(2,1)}, bf16[1,8192,512]{2,1,0:T(8,128)(2,1)}, f32[2048,512]{1,0:T(8,128)}, f32[8,128]{1,0:T(8,128)S(1)}) custom-call(s32[1]{0:T(128)} %bitcast.rank_ref, bf16[1,8192,512]{2,1,0:T(8,128)(2,1)} %values_ref.19, ...), custom_call_target="tpu_custom_call", output_to_operand_aliasing={{0}: (12, {}), {1}: (13, {}), {2}: (14, {})} | custom-call | flops 1024 | bytes 1024 | tf_op jit(solution)/shard_map/pallas_call | solution.py:256
  366.0 5.0 %collective-permute-done.57.refs_2_ = bf16[16,32,256]{2,1,0:T(8,128)(2,1)S(1)} collective-permute-done((bf16[16,32,256]{2,1,0:T(8,128)(2,1)}, bf16[16,32,256]{2,1,0:T(8,128)(2,1)S(1)}, u32[]{:S(2)}, u32[]{:S(2)}) %collective-permute-start.57) | collective-permute-done | bytes 262176 | tf_op jit(solution)/shard_map/ppermute | solution.py:191
  374.8 4.5 %shard_map.97 = (bf16[1,8192,512]{2,1,0:T(8,128)(2,1)}, bf16[1,8192,512]{2,1,0:T(8,128)(2,1)}, f32[2048,512]{1,0:T(8,128)}, f32[8,128]{1,0:T(8,128)}) custom-call(s32[1]{0:T(128)} %bitcast.rank_ref, bf16[1,8192,512]{2,1,0:T(8,128)(2,1)} %values_ref.19, ...), custom_call_target="tpu_custom_call", output_to_operand_aliasing={{0}: (13, {}), {1}: (14, {}), {2}: (15, {})} | custom-call | flops 1024 | bytes 1024 | tf_op jit(solution)/shard_map/pallas_call | solution.py:256
  (246 shorter events, 122.8 us)
Async XLA Ops:
  7.2 363.8 %reduce-scatter.2.cloned.1.call-start = ((), (), s32[]{:S(2)}) async-start(), calls=%async_computation.1 | async-start | bytes 10485760 | tf_op jit(solution)/shard_map/reduce_scatter | solution.py:338
  51.3 26.0 %collective-permute-start.3 = (bf16[32,32,256]{2,1,0:T(8,128)(2,1)}, bf16[32,32,256]{2,1,0:T(8,128)(2,1)S(1)}, u32[]{:S(2)}, u32[]{:S(2)}) collective-permute-start(bf16[32,32,256]{2,1,0:T(8,128)(2,1)} %get-tuple-element.168), channel_id=1, source_target_pairs={{0,6},{1,7},{2,4},{3,5},{4,2},{5,3},{6,0},{7,1},{8,14},{9,15},{10,... | collective-permute-start | bytes 1572872 | tf_op jit(solution)/shard_map/ppermute | solution.py:191
  54.3 30.3 %collective-permute-start.4 = (bf16[32,32,256]{2,1,0:T(8,128)(2,1)}, bf16[32,32,256]{2,1,0:T(8,128)(2,1)S(1)}, u32[]{:S(2)}, u32[]{:S(2)}) collective-permute-start(bf16[32,32,256]{2,1,0:T(8,128)(2,1)} %get-tuple-element.169), channel_id=1, source_target_pairs={{0,2},{1,3},{2,0},{3,1},{4,6},{5,7},{6,4},{7,5},{8,10},{9,11},{10,... | collective-permute-start | bytes 1572872 | tf_op jit(solution)/shard_map/ppermute | solution.py:191
  55.7 30.5 %collective-permute-start.5 = (bf16[32,32,256]{2,1,0:T(8,128)(2,1)}, bf16[32,32,256]{2,1,0:T(8,128)(2,1)S(1)}, u32[]{:S(2)}, u32[]{:S(2)}) collective-permute-start(bf16[32,32,256]{2,1,0:T(8,128)(2,1)} %get-tuple-element.170), channel_id=1, source_target_pairs={{0,4},{1,5},{2,6},{3,7},{4,0},{5,1},{6,2},{7,3},{8,12},{9,13},{10,... | collective-permute-start | bytes 1572872 | tf_op jit(solution)/shard_map/ppermute | solution.py:191
  62.0 33.1 %collective-permute-start.6 = (bf16[32,32,256]{2,1,0:T(8,128)(2,1)}, bf16[32,32,256]{2,1,0:T(8,128)(2,1)S(1)}, u32[]{:S(2)}, u32[]{:S(2)}) collective-permute-start(bf16[32,32,256]{2,1,0:T(8,128)(2,1)} %get-tuple-element.171), channel_id=1, source_target_pairs={{0,7},{1,6},{2,5},{3,4},{4,3},{5,2},{6,1},{7,0},{8,15},{9,14},{10,... | collective-permute-start | bytes 1572872 | tf_op jit(solution)/shard_map/ppermute | solution.py:191
  77.1 31.3 %collective-permute-start.7 = (bf16[32,32,256]{2,1,0:T(8,128)(2,1)}, bf16[32,32,256]{2,1,0:T(8,128)(2,1)S(1)}, u32[]{:S(2)}, u32[]{:S(2)}) collective-permute-start(bf16[32,32,256]{2,1,0:T(8,128)(2,1)} %get-tuple-element.172), channel_id=1, source_target_pairs={{0,3},{1,2},{2,1},{3,0},{4,7},{5,6},{6,5},{7,4},{8,11},{9,10},{10,... | collective-permute-start | bytes 1572872 | tf_op jit(solution)/shard_map/ppermute | solution.py:191
  77.3 40.6 %collective-permute-start.28 = (bf16[32,32,256]{2,1,0:T(8,128)(2,1)}, bf16[32,32,256]{2,1,0:T(8,128)(2,1)S(1)}, u32[]{:S(2)}, u32[]{:S(2)}) collective-permute-start(bf16[32,32,256]{2,1,0:T(8,128)(2,1)} %get-tuple-element.202), channel_id=1, source_target_pairs={{0,6},{1,7},{2,4},{3,5},{4,2},{5,3},{6,0},{7,1},{8,14},{9,15},{10,... | collective-permute-start | bytes 1572872 | tf_op jit(solution)/shard_map/ppermute | solution.py:191
  84.7 45.0 %collective-permute-start.29 = (bf16[32,32,256]{2,1,0:T(8,128)(2,1)}, bf16[32,32,256]{2,1,0:T(8,128)(2,1)S(1)}, u32[]{:S(2)}, u32[]{:S(2)}) collective-permute-start(bf16[32,32,256]{2,1,0:T(8,128)(2,1)} %get-tuple-element.203), channel_id=1, source_target_pairs={{0,2},{1,3},{2,0},{3,1},{4,6},{5,7},{6,4},{7,5},{8,10},{9,11},{10,... | collective-permute-start | bytes 1572872 | tf_op jit(solution)/shard_map/ppermute | solution.py:191
  86.2 43.5 %collective-permute-start.8 = (bf16[32,32,256]{2,1,0:T(8,128)(2,1)}, bf16[32,32,256]{2,1,0:T(8,128)(2,1)}, u32[]{:S(2)}, u32[]{:S(2)}) collective-permute-start(bf16[32,32,256]{2,1,0:T(8,128)(2,1)} %get-tuple-element.176), channel_id=1, source_target_pairs={{0,5},{1,4},{2,7},{3,6},{4,1},{5,0},{6,3},{7,2},{8,13},{9,12},{10,... | collective-permute-start | bytes 1572872 | tf_op jit(solution)/shard_map/ppermute | solution.py:191
  95.1 36.3 %collective-permute-start.9 = (bf16[32,32,256]{2,1,0:T(8,128)(2,1)}, bf16[32,32,256]{2,1,0:T(8,128)(2,1)}, u32[]{:S(2)}, u32[]{:S(2)}) collective-permute-start(bf16[32,32,256]{2,1,0:T(8,128)(2,1)} %get-tuple-element.177), channel_id=1, source_target_pairs={{0,1},{1,0},{2,3},{3,2},{4,5},{5,4},{6,7},{7,6},{8,9},{9,8},{10,11... | collective-permute-start | bytes 1572872 | tf_op jit(solution)/shard_map/ppermute | solution.py:191
  108.4 36.2 %collective-permute-start.30 = (bf16[32,32,256]{2,1,0:T(8,128)(2,1)}, bf16[32,32,256]{2,1,0:T(8,128)(2,1)S(1)}, u32[]{:S(2)}, u32[]{:S(2)}) collective-permute-start(bf16[32,32,256]{2,1,0:T(8,128)(2,1)} %get-tuple-element.204), channel_id=1, source_target_pairs={{0,4},{1,5},{2,6},{3,7},{4,0},{5,1},{6,2},{7,3},{8,12},{9,13},{10,... | collective-permute-start | bytes 1572872 | tf_op jit(solution)/shard_map/ppermute | solution.py:191
  117.9 28.3 %collective-permute-start.31 = (bf16[32,32,256]{2,1,0:T(8,128)(2,1)}, bf16[32,32,256]{2,1,0:T(8,128)(2,1)S(1)}, u32[]{:S(2)}, u32[]{:S(2)}) collective-permute-start(bf16[32,32,256]{2,1,0:T(8,128)(2,1)} %get-tuple-element.209), channel_id=1, source_target_pairs={{0,7},{1,6},{2,5},{3,4},{4,3},{5,2},{6,1},{7,0},{8,15},{9,14},{10,... | collective-permute-start | bytes 1572872 | tf_op jit(solution)/shard_map/ppermute | solution.py:191
  146.9 27.8 %collective-permute-start.1 = (bf16[32,32,256]{2,1,0:T(8,128)(2,1)}, bf16[32,32,256]{2,1,0:T(8,128)(2,1)S(1)}, u32[]{:S(2)}, u32[]{:S(2)}) collective-permute-start(bf16[32,32,256]{2,1,0:T(8,128)(2,1)} %get-tuple-element.161), channel_id=1, source_target_pairs={{0,2},{1,3},{2,0},{3,1},{4,6},{5,7},{6,4},{7,5},{8,10},{9,11},{10,... | collective-permute-start | bytes 1572872 | tf_op jit(solution)/shard_map/ppermute | solution.py:191
  151.8 33.3 %collective-permute-start.24 = (bf16[32,32,256]{2,1,0:T(8,128)(2,1)}, bf16[32,32,256]{2,1,0:T(8,128)(2,1)S(1)}, u32[]{:S(2)}, u32[]{:S(2)}) collective-permute-start(bf16[32,32,256]{2,1,0:T(8,128)(2,1)} %get-tuple-element.197), channel_id=1, source_target_pairs={{0,7},{1,6},{2,5},{3,4},{4,3},{5,2},{6,1},{7,0},{8,15},{9,14},{10,... | collective-permute-start | bytes 1572872 | tf_op jit(solution)/shard_map/ppermute | solution.py:191
  154.7 41.7 %collective-permute-start.25 = (bf16[32,32,256]{2,1,0:T(8,128)(2,1)}, bf16[32,32,256]{2,1,0:T(8,128)(2,1)S(1)}, u32[]{:S(2)}, u32[]{:S(2)}) collective-permute-start(bf16[32,32,256]{2,1,0:T(8,128)(2,1)} %get-tuple-element.198), channel_id=1, source_target_pairs={{0,3},{1,2},{2,1},{3,0},{4,7},{5,6},{6,5},{7,4},{8,11},{9,10},{10,... | collective-permute-start | bytes 1572872 | tf_op jit(solution)/shard_map/ppermute | solution.py:191
  168.0 29.7 %collective-permute-start.26 = (bf16[32,32,256]{2,1,0:T(8,128)(2,1)}, bf16[32,32,256]{2,1,0:T(8,128)(2,1)}, u32[]{:S(2)}, u32[]{:S(2)}) collective-permute-start(bf16[32,32,256]{2,1,0:T(8,128)(2,1)} %get-tuple-element.199), channel_id=1, source_target_pairs={{0,5},{1,4},{2,7},{3,6},{4,1},{5,0},{6,3},{7,2},{8,13},{9,12},{10,... | collective-permute-start | bytes 1572872 | tf_op jit(solution)/shard_map/ppermute | solution.py:191
  174.8 36.2 %collective-permute-start.35 = (bf16[32,32,256]{2,1,0:T(8,128)(2,1)}, bf16[32,32,256]{2,1,0:T(8,128)(2,1)S(1)}, u32[]{:S(2)}, u32[]{:S(2)}) collective-permute-start(bf16[32,32,256]{2,1,0:T(8,128)(2,1)} %get-tuple-element.237), channel_id=1, source_target_pairs={{0,6},{1,7},{2,4},{3,5},{4,2},{5,3},{6,0},{7,1},{8,14},{9,15},{10,... | collective-permute-start | bytes 1572872 | tf_op jit(solution)/shard_map/ppermute | solution.py:191
  185.1 33.5 %collective-permute-start.36 = (bf16[32,32,256]{2,1,0:T(8,128)(2,1)}, bf16[32,32,256]{2,1,0:T(8,128)(2,1)S(1)}, u32[]{:S(2)}, u32[]{:S(2)}) collective-permute-start(bf16[32,32,256]{2,1,0:T(8,128)(2,1)} %get-tuple-element.238), channel_id=1, source_target_pairs={{0,2},{1,3},{2,0},{3,1},{4,6},{5,7},{6,4},{7,5},{8,10},{9,11},{10,... | collective-permute-start | bytes 1572872 | tf_op jit(solution)/shard_map/ppermute | solution.py:191
  223.1 25.3 %collective-permute-start.40 = (bf16[32,32,256]{2,1,0:T(8,128)(2,1)}, bf16[32,32,256]{2,1,0:T(8,128)(2,1)}, u32[]{:S(2)}, u32[]{:S(2)}) collective-permute-start(bf16[32,32,256]{2,1,0:T(8,128)(2,1)} %get-tuple-element.242), channel_id=1, source_target_pairs={{0,5},{1,4},{2,7},{3,6},{4,1},{5,0},{6,3},{7,2},{8,13},{9,12},{10,... | collective-permute-start | bytes 1572872 | tf_op jit(solution)/shard_map/ppermute | solution.py:191
  223.3 27.1 %collective-permute-start.41 = (bf16[32,32,256]{2,1,0:T(8,128)(2,1)}, bf16[32,32,256]{2,1,0:T(8,128)(2,1)}, u32[]{:S(2)}, u32[]{:S(2)}) collective-permute-start(bf16[32,32,256]{2,1,0:T(8,128)(2,1)} %get-tuple-element.243), channel_id=1, source_target_pairs={{0,1},{1,0},{2,3},{3,2},{4,5},{5,4},{6,7},{7,6},{8,9},{9,8},{10,11... | collective-permute-start | bytes 1572872 | tf_op jit(solution)/shard_map/ppermute | solution.py:191
  223.9 38.5 %collective-permute-start.49 = (bf16[32,32,256]{2,1,0:T(8,128)(2,1)}, bf16[32,32,256]{2,1,0:T(8,128)(2,1)S(1)}, u32[]{:S(2)}, u32[]{:S(2)}) collective-permute-start(bf16[32,32,256]{2,1,0:T(8,128)(2,1)} %get-tuple-element.260), channel_id=1, source_target_pairs={{0,6},{1,7},{2,4},{3,5},{4,2},{5,3},{6,0},{7,1},{8,14},{9,15},{10,... | collective-permute-start | bytes 1572872 | tf_op jit(solution)/shard_map/ppermute | solution.py:191
  236.6 33.0 %collective-permute-start.50 = (bf16[32,32,256]{2,1,0:T(8,128)(2,1)}, bf16[32,32,256]{2,1,0:T(8,128)(2,1)S(1)}, u32[]{:S(2)}, u32[]{:S(2)}) collective-permute-start(bf16[32,32,256]{2,1,0:T(8,128)(2,1)} %get-tuple-element.261), channel_id=1, source_target_pairs={{0,2},{1,3},{2,0},{3,1},{4,6},{5,7},{6,4},{7,5},{8,10},{9,11},{10,... | collective-permute-start | bytes 1572872 | tf_op jit(solution)/shard_map/ppermute | solution.py:191
  248.4 32.5 %collective-permute-start.52 = (bf16[32,32,256]{2,1,0:T(8,128)(2,1)}, bf16[32,32,256]{2,1,0:T(8,128)(2,1)}, u32[]{:S(2)}, u32[]{:S(2)}) collective-permute-start(bf16[32,32,256]{2,1,0:T(8,128)(2,1)} %get-tuple-element.263), channel_id=1, source_target_pairs={{0,7},{1,6},{2,5},{3,4},{4,3},{5,2},{6,1},{7,0},{8,15},{9,14},{10,... | collective-permute-start | bytes 1572872 | tf_op jit(solution)/shard_map/ppermute | solution.py:191
  250.4 41.3 %collective-permute-start.53 = (bf16[32,32,256]{2,1,0:T(8,128)(2,1)}, bf16[32,32,256]{2,1,0:T(8,128)(2,1)}, u32[]{:S(2)}, u32[]{:S(2)}) collective-permute-start(bf16[32,32,256]{2,1,0:T(8,128)(2,1)} %get-tuple-element.264), channel_id=1, source_target_pairs={{0,3},{1,2},{2,1},{3,0},{4,7},{5,6},{6,5},{7,4},{8,11},{9,10},{10,... | collective-permute-start | bytes 1572872 | tf_op jit(solution)/shard_map/ppermute | solution.py:191
  262.5 30.2 %collective-permute-start.54 = (bf16[32,32,256]{2,1,0:T(8,128)(2,1)}, bf16[32,32,256]{2,1,0:T(8,128)(2,1)S(1)}, u32[]{:S(2)}, u32[]{:S(2)}) collective-permute-start(bf16[32,32,256]{2,1,0:T(8,128)(2,1)} %get-tuple-element.265), channel_id=1, source_target_pairs={{0,5},{1,4},{2,7},{3,6},{4,1},{5,0},{6,3},{7,2},{8,13},{9,12},{10,... | collective-permute-start | bytes 1572872 | tf_op jit(solution)/shard_map/ppermute | solution.py:191
  269.6 25.0 %collective-permute-start.55 = (bf16[32,32,256]{2,1,0:T(8,128)(2,1)}, bf16[32,32,256]{2,1,0:T(8,128)(2,1)S(1)}, u32[]{:S(2)}, u32[]{:S(2)}) collective-permute-start(bf16[32,32,256]{2,1,0:T(8,128)(2,1)} %get-tuple-element.266), channel_id=1, source_target_pairs={{0,1},{1,0},{2,3},{3,2},{4,5},{5,4},{6,7},{7,6},{8,9},{9,8},{10,11... | collective-permute-start | bytes 1572872 | tf_op jit(solution)/shard_map/ppermute | solution.py:191
  270.4 32.6 %collective-permute-start.42 = (bf16[32,32,256]{2,1,0:T(8,128)(2,1)}, bf16[32,32,256]{2,1,0:T(8,128)(2,1)S(1)}, u32[]{:S(2)}, u32[]{:S(2)}) collective-permute-start(bf16[32,32,256]{2,1,0:T(8,128)(2,1)} %get-tuple-element.245), channel_id=1, source_target_pairs={{0,6},{1,7},{2,4},{3,5},{4,2},{5,3},{6,0},{7,1},{8,14},{9,15},{10,... | collective-permute-start | bytes 1572872 | tf_op jit(solution)/shard_map/ppermute | solution.py:191
  280.9 33.7 %collective-permute-start.43 = (bf16[32,32,256]{2,1,0:T(8,128)(2,1)}, bf16[32,32,256]{2,1,0:T(8,128)(2,1)S(1)}, u32[]{:S(2)}, u32[]{:S(2)}) collective-permute-start(bf16[32,32,256]{2,1,0:T(8,128)(2,1)} %get-tuple-element.246), channel_id=1, source_target_pairs={{0,2},{1,3},{2,0},{3,1},{4,6},{5,7},{6,4},{7,5},{8,10},{9,11},{10,... | collective-permute-start | bytes 1572872 | tf_op jit(solution)/shard_map/ppermute | solution.py:191
  291.7 32.8 %collective-permute-start.44 = (bf16[32,32,256]{2,1,0:T(8,128)(2,1)}, bf16[32,32,256]{2,1,0:T(8,128)(2,1)S(1)}, u32[]{:S(2)}, u32[]{:S(2)}) collective-permute-start(bf16[32,32,256]{2,1,0:T(8,128)(2,1)} %get-tuple-element.247), channel_id=1, source_target_pairs={{0,4},{1,5},{2,6},{3,7},{4,0},{5,1},{6,2},{7,3},{8,12},{9,13},{10,... | collective-permute-start | bytes 1572872 | tf_op jit(solution)/shard_map/ppermute | solution.py:191
  292.7 33.5 %collective-permute-start.45 = (bf16[32,32,256]{2,1,0:T(8,128)(2,1)}, bf16[32,32,256]{2,1,0:T(8,128)(2,1)}, u32[]{:S(2)}, u32[]{:S(2)}) collective-permute-start(bf16[32,32,256]{2,1,0:T(8,128)(2,1)} %get-tuple-element.248), channel_id=1, source_target_pairs={{0,7},{1,6},{2,5},{3,4},{4,3},{5,2},{6,1},{7,0},{8,15},{9,14},{10,... | collective-permute-start | bytes 1572872 | tf_op jit(solution)/shard_map/ppermute | solution.py:191
  294.6 42.1 %collective-permute-start.46 = (bf16[32,32,256]{2,1,0:T(8,128)(2,1)}, bf16[32,32,256]{2,1,0:T(8,128)(2,1)}, u32[]{:S(2)}, u32[]{:S(2)}) collective-permute-start(bf16[32,32,256]{2,1,0:T(8,128)(2,1)} %get-tuple-element.249), channel_id=1, source_target_pairs={{0,3},{1,2},{2,1},{3,0},{4,7},{5,6},{6,5},{7,4},{8,11},{9,10},{10,... | collective-permute-start | bytes 1572872 | tf_op jit(solution)/shard_map/ppermute | solution.py:191
  303.0 34.7 %collective-permute-start.47 = (bf16[32,32,256]{2,1,0:T(8,128)(2,1)}, bf16[32,32,256]{2,1,0:T(8,128)(2,1)}, u32[]{:S(2)}, u32[]{:S(2)}) collective-permute-start(bf16[32,32,256]{2,1,0:T(8,128)(2,1)} %get-tuple-element.250), channel_id=1, source_target_pairs={{0,5},{1,4},{2,7},{3,6},{4,1},{5,0},{6,3},{7,2},{8,13},{9,12},{10,... | collective-permute-start | bytes 1572872 | tf_op jit(solution)/shard_map/ppermute | solution.py:191
  (95 other events, 1459.4 us)
Sparse Core Ops, SparseCore 0:
  219.7 145.3 reduce-scatter.1

commit v7 on v6

--- a/solution.py
+++ b/solution.py
@@ -10,6 +10,7 @@
 WIDTH = 128
 ROWS = 16
 VMEM_LIMIT = 60 * 1024 * 1024
+BACK_LIMIT = 40 * 1024 * 1024
 COST = pl.CostEstimate(flops=1024, bytes_accessed=1024, transcendentals=0)
 FIRST = 5
 EARLY = 3
@@ -150,6 +151,7 @@
     moves = moves_of(ranks)
     rank = lax.axis_index("seq").astype(jnp.int32).reshape(1)
     params = pltpu.CompilerParams(vmem_limit_bytes=VMEM_LIMIT)
+    back_params = pltpu.CompilerParams(vmem_limit_bytes=BACK_LIMIT)
     there = {q: 2 if q == 0 else 1 for q in range(chunks)}
     back = {q: 2 if q == chunks - 1 else 1 for q in range(chunks)}
 
@@ -250,6 +252,8 @@
             token,
         ]
         earlier = list(outputs) if outputs else []
+        operands = [pltpu.with_memory_space_constraint(x, pltpu.HBM) for x in (values, cotangent, left_factor)]
+        reduced = [pltpu.with_memory_space_constraint(x, pltpu.HBM) for x in reduced]
         terms = len(reduced)
         aliases = {4 + ranks + terms + n: n for n in range(len(earlier))}
         grad_spec = pl.BlockSpec((shard // steps, channels), lambda g, rank: (g, 0))
@@ -276,9 +280,9 @@
                 ],
             ),
             input_output_aliases=aliases,
-            compiler_params=pltpu.CompilerParams(vmem_limit_bytes=40 * 1024 * 1024),
+            compiler_params=back_params,
             cost_estimate=COST,
-        )(rank, values, cotangent, left_factor, *arrived, *reduced, *earlier, *after)
+        )(rank, *operands, *arrived, *reduced, *earlier, *after)
 
     received, sent, returned = {}, {}, {}
     left_tokens, right_tokens, back_tokens = [], {}, {}

time: 393 us -> 393 us (level)
  local copies, waits for them, and re-layouts: 23.2 us -> 12.7 us
  waiting for transfers between devices: 177 us -> 184 us
  Pallas kernels: 105 us -> 109 us
    unnamed x112 -> x102, local copies, waits for them, and re-layouts: 23.2 us -> 12.7 us
    ppermute x70, waiting for transfers between devices: 177 us -> 184 us  [exchange(): lax.ppermute(sends[n], 'seq', [(r, r ^ moves[n]) for r in range(ranks)])]
    pallas_call x5, Pallas kernels: 25.9 us -> 30 us  [left_back(): pl.pallas_call(functools.partial(left_back_kernel, ranks, terms), out_sha...]
  transfers between devices with their start and end apart: 71 -> 71, of which waited for: 29 -> 32; matrix products, arithmetic and copies ran while one was open for 0% -> 0% of each run, Pallas kernels for 25% -> 26%
where the time goes in v7:
time: 393 us
  waiting for transfers between devices  184 us (47%)
  Pallas kernels  109 us (28%)
  starting transfers between devices  71.9 us (18%)
  between operations  14.5 us (4%)
  local copies, waits for them, and re-layouts  12.7 us (3%)
    ppermute x70, waiting for transfers between devices, exchange(): lax.ppermute(sends[n], 'seq', [(r, r ^ moves[n]) for r in range(ranks)])  184 us
    ppermute x70, starting transfers between devices, exchange(): lax.ppermute(sends[n], 'seq', [(r, r ^ moves[n]) for r in range(ranks)])  71.9 us
    pallas_call x4, Pallas kernels, right_both(): pl.pallas_call(functools.partial(right_kernel, ranks, ins, outs), out_sha...  52.6 us
    pallas_call x5, Pallas kernels, left_back(): pl.pallas_call(functools.partial(left_back_kernel, ranks, terms), out_sha...  30 us
    pallas_call x5, Pallas kernels, left_forward(): pl.pallas_call(functools.partial(left_forward_kernel, ranks), out_shape=[...  26.7 us
    unnamed x102, local copies, waits for them, and re-layouts  12.7 us
  transfers between devices with their start and end apart: 71, of which 32 were waited for; matrix products, arithmetic and copies ran while one was open for 0% of the time, Pallas kernels for 26%

profile of v7, /device:TPU:0, one launch (start us, length us, event | category | flops | bytes accessed | tf_op | source)
XLA Modules:
  0.0 392.8 jit_solution(2592846442663491566)
XLA Ops:
  22.2 6.3 %collective-permute-done.11.refs_2_ = bf16[16,32,256]{2,1,0:T(8,128)(2,1)} collective-permute-done((bf16[16,32,256]{2,1,0:T(8,128)(2,1)}, bf16[16,32,256]{2,1,0:T(8,128)(2,1)}, u32[]{:S(2)}, u32[]{:S(2)}) %collective-permute-start.11) | collective-permute-done | bytes 262176 | tf_op jit(solution)/shard_map/ppermute | solution.py:193
  33.8 5.0 %collective-permute-done.14.refs_5_ = bf16[16,32,256]{2,1,0:T(8,128)(2,1)S(1)} collective-permute-done((bf16[16,32,256]{2,1,0:T(8,128)(2,1)}, bf16[16,32,256]{2,1,0:T(8,128)(2,1)S(1)}, u32[]{:S(2)}, u32[]{:S(2)}) %collective-permute-start.14) | collective-permute-done | bytes 262176 | tf_op jit(solution)/shard_map/ppermute | solution.py:193
  44.7 6.5 %shard_map.78 = (bf16[32,32,256]{2,1,0:T(8,128)(2,1)}, bf16[32,32,256]{2,1,0:T(8,128)(2,1)}, bf16[32,32,256]{2,1,0:T(8,128)(2,1)}, bf16[32,32,256]{2,1,0:T(8,128...) custom-call(s32[1]{0:T(128)} %bitcast.rank_ref, ...), custom_call_target="tpu_custom_call" | custom-call | flops 1024 | bytes 1024 | tf_op jit(solution)/shard_map/pallas_call | solution.py:176
  56.2 5.1 %collective-permute-done.21.refs_13_ = bf16[16,32,256]{2,1,0:T(8,128)(2,1)S(1)} collective-permute-done((bf16[16,32,256]{2,1,0:T(8,128)(2,1)}, bf16[16,32,256]{2,1,0:T(8,128)(2,1)S(1)}, u32[]{:S(2)}, u32[]{:S(2)}) %collective-permute-start.21) | collective-permute-done | bytes 262176 | tf_op jit(solution)/shard_map/ppermute | solution.py:193
  64.1 6.5 %shard_map.79 = (bf16[32,32,256]{2,1,0:T(8,128)(2,1)}, bf16[32,32,256]{2,1,0:T(8,128)(2,1)}, bf16[32,32,256]{2,1,0:T(8,128)(2,1)}, bf16[32,32,256]{2,1,0:T(8,128...) custom-call(s32[1]{0:T(128)} %bitcast.rank_ref, ...), custom_call_target="tpu_custom_call" | custom-call | flops 1024 | bytes 1024 | tf_op jit(solution)/shard_map/pallas_call | solution.py:176
  70.6 6.5 %shard_map.80 = (bf16[32,32,256]{2,1,0:T(8,128)(2,1)}, bf16[32,32,256]{2,1,0:T(8,128)(2,1)}, bf16[32,32,256]{2,1,0:T(8,128)(2,1)}, bf16[32,32,256]{2,1,0:T(8,128...) custom-call(s32[1]{0:T(128)} %bitcast.rank_ref, ...), custom_call_target="tpu_custom_call" | custom-call | flops 1024 | bytes 1024 | tf_op jit(solution)/shard_map/pallas_call | solution.py:176
  80.3 4.4 %collective-permute-done.4.refs_2_ = bf16[32,32,256]{2,1,0:T(8,128)(2,1)S(1)} collective-permute-done((bf16[32,32,256]{2,1,0:T(8,128)(2,1)}, bf16[32,32,256]{2,1,0:T(8,128)(2,1)S(1)}, u32[]{:S(2)}, u32[]{:S(2)}) %collective-permute-start.4) | collective-permute-done | bytes 524320 | tf_op jit(solution)/shard_map/ppermute | solution.py:193
  86.2 8.9 %collective-permute-done.6.refs_4_ = bf16[32,32,256]{2,1,0:T(8,128)(2,1)S(1)} collective-permute-done((bf16[32,32,256]{2,1,0:T(8,128)(2,1)}, bf16[32,32,256]{2,1,0:T(8,128)(2,1)S(1)}, u32[]{:S(2)}, u32[]{:S(2)}) %collective-permute-start.6) | collective-permute-done | bytes 524320 | tf_op jit(solution)/shard_map/ppermute | solution.py:193
  95.2 13.1 %shard_map.82 = (bf16[32,32,256]{2,1,0:T(8,128)(2,1)}, bf16[32,32,256]{2,1,0:T(8,128)(2,1)}, bf16[32,32,256]{2,1,0:T(8,128)(2,1)}, bf16[32,32,256]{2,1,0:T(8,128...) custom-call(s32[1]{0:T(128)} %bitcast.rank_ref, ...), custom_call_target="tpu_custom_call" | custom-call | flops 1024 | bytes 1024 | tf_op jit(solution)/shard_map/pallas_call | solution.py:205
  110.4 7.5 %collective-permute-done.28.refs_1_ = bf16[32,32,256]{2,1,0:T(8,128)(2,1)S(1)} collective-permute-done((bf16[32,32,256]{2,1,0:T(8,128)(2,1)}, bf16[32,32,256]{2,1,0:T(8,128)(2,1)S(1)}, u32[]{:S(2)}, u32[]{:S(2)}) %collective-permute-start.28) | collective-permute-done | bytes 524320 | tf_op jit(solution)/shard_map/ppermute | solution.py:193
  118.3 11.4 %collective-permute-done.29.refs_2_ = bf16[32,32,256]{2,1,0:T(8,128)(2,1)S(1)} collective-permute-done((bf16[32,32,256]{2,1,0:T(8,128)(2,1)}, bf16[32,32,256]{2,1,0:T(8,128)(2,1)S(1)}, u32[]{:S(2)}, u32[]{:S(2)}) %collective-permute-start.29) | collective-permute-done | bytes 524320 | tf_op jit(solution)/shard_map/ppermute | solution.py:193
  131.4 13.1 %shard_map.83 = (bf16[32,32,256]{2,1,0:T(8,128)(2,1)}, bf16[32,32,256]{2,1,0:T(8,128)(2,1)}, bf16[32,32,256]{2,1,0:T(8,128)(2,1)}, bf16[32,32,256]{2,1,0:T(8,128...) custom-call(s32[1]{0:T(128)} %bitcast.rank_ref, ...), custom_call_target="tpu_custom_call", output_to_operand_aliasing={{8}: (11, {})} | custom-call | flops 1024 | bytes 1024 | tf_op jit(solution)/shard_map/pallas_call | solution.py:205
  154.8 13.3 %shard_map.86 = (bf16[32,32,256]{2,1,0:T(8,128)(2,1)}, bf16[32,32,256]{2,1,0:T(8,128)(2,1)}, bf16[32,32,256]{2,1,0:T(8,128)(2,1)}, bf16[32,32,256]{2,1,0:T(8,128...) custom-call(s32[1]{0:T(128)} %bitcast.rank_ref, ...), custom_call_target="tpu_custom_call", output_to_operand_aliasing={{8}: (11, {})} | custom-call | flops 1024 | bytes 1024 | tf_op jit(solution)/shard_map/pallas_call | solution.py:205
  168.5 6.2 %collective-permute-done.1.refs_2_ = bf16[32,32,256]{2,1,0:T(8,128)(2,1)S(1)} collective-permute-done((bf16[32,32,256]{2,1,0:T(8,128)(2,1)}, bf16[32,32,256]{2,1,0:T(8,128)(2,1)S(1)}, u32[]{:S(2)}, u32[]{:S(2)}) %collective-permute-start.1) | collective-permute-done | bytes 524320 | tf_op jit(solution)/shard_map/ppermute | solution.py:193
  176.9 8.3 %collective-permute-done.24.refs_4_ = bf16[32,32,256]{2,1,0:T(8,128)(2,1)S(1)} collective-permute-done((bf16[32,32,256]{2,1,0:T(8,128)(2,1)}, bf16[32,32,256]{2,1,0:T(8,128)(2,1)S(1)}, u32[]{:S(2)}, u32[]{:S(2)}) %collective-permute-start.24) | collective-permute-done | bytes 524320 | tf_op jit(solution)/shard_map/ppermute | solution.py:193
  185.7 10.7 %collective-permute-done.25.refs_5_ = bf16[32,32,256]{2,1,0:T(8,128)(2,1)S(1)} collective-permute-done((bf16[32,32,256]{2,1,0:T(8,128)(2,1)}, bf16[32,32,256]{2,1,0:T(8,128)(2,1)S(1)}, u32[]{:S(2)}, u32[]{:S(2)}) %collective-permute-start.25) | collective-permute-done | bytes 524320 | tf_op jit(solution)/shard_map/ppermute | solution.py:193
  197.7 13.2 %shard_map.87 = (bf16[16,32,256]{2,1,0:T(8,128)(2,1)}, bf16[16,32,256]{2,1,0:T(8,128)(2,1)}, bf16[16,32,256]{2,1,0:T(8,128)(2,1)}, bf16[16,32,256]{2,1,0:T(8,128...) custom-call(s32[1]{0:T(128)} %bitcast.rank_ref, ...), custom_call_target="tpu_custom_call", output_to_operand_aliasing={{16}: (11, {})} | custom-call | flops 1024 | bytes 1024 | tf_op jit(solution)/shard_map/pallas_call | solution.py:205
  210.9 7.7 %collective-permute-done.36.refs_2_ = bf16[32,32,256]{2,1,0:T(8,128)(2,1)S(1)} collective-permute-done((bf16[32,32,256]{2,1,0:T(8,128)(2,1)}, bf16[32,32,256]{2,1,0:T(8,128)(2,1)S(1)}, u32[]{:S(2)}, u32[]{:S(2)}) %collective-permute-start.36) | collective-permute-done | bytes 524320 | tf_op jit(solution)/shard_map/ppermute | solution.py:193
  226.1 9.7 %collective-permute-done.38.refs_4_ = bf16[32,32,256]{2,1,0:T(8,128)(2,1)S(1)} collective-permute-done((bf16[32,32,256]{2,1,0:T(8,128)(2,1)S(1)}, bf16[32,32,256]{2,1,0:T(8,128)(2,1)S(1)}, u32[]{:S(2)}, u32[]{:S(2)}) %collective-permute-start.38) | collective-permute-done | bytes 524320 | tf_op jit(solution)/shard_map/ppermute | solution.py:193
  238.1 8.4 %collective-permute-done.39.refs_5_ = bf16[32,32,256]{2,1,0:T(8,128)(2,1)S(1)} collective-permute-done((bf16[32,32,256]{2,1,0:T(8,128)(2,1)}, bf16[32,32,256]{2,1,0:T(8,128)(2,1)S(1)}, u32[]{:S(2)}, u32[]{:S(2)}) %collective-permute-start.39) | collective-permute-done | bytes 524320 | tf_op jit(solution)/shard_map/ppermute | solution.py:193
  253.7 6.9 %shard_map.89 = (bf16[1,8192,512]{2,1,0:T(8,128)(2,1)}, bf16[1,8192,512]{2,1,0:T(8,128)(2,1)}, f32[2048,512]{1,0:T(8,128)}, f32[8,128]{1,0:T(8,128)S(1)}) custom-call(s32[1]{0:T(128)} %bitcast.rank_ref, bf16[1,8192,512]{2,1,0:T(8,128)(2,1)} %values_ref.19, bf16[1,8192,512]{2,1,0:T(8,128)(2,1)} %cotangent_ref.19, bf16[32,256,256]{2,1,0:T(8,128)(2,1)} %left_ref.19, ...), custom_call_target="tpu_custom_call" | custom-call | flops 1024 | bytes 1024 | tf_op jit(solution)/shard_map/pallas_call | solution.py:260
  261.7 7.9 %collective-permute-done.50.refs_2_ = bf16[32,32,256]{2,1,0:T(8,128)(2,1)S(1)} collective-permute-done((bf16[32,32,256]{2,1,0:T(8,128)(2,1)}, bf16[32,32,256]{2,1,0:T(8,128)(2,1)S(1)}, u32[]{:S(2)}, u32[]{:S(2)}) %collective-permute-start.50) | collective-permute-done | bytes 524320 | tf_op jit(solution)/shard_map/ppermute | solution.py:193
  272.8 8.1 %collective-permute-done.52.refs_4_ = bf16[32,32,256]{2,1,0:T(8,128)(2,1)} collective-permute-done((bf16[32,32,256]{2,1,0:T(8,128)(2,1)}, bf16[32,32,256]{2,1,0:T(8,128)(2,1)}, u32[]{:S(2)}, u32[]{:S(2)}) %collective-permute-start.52) | collective-permute-done | bytes 524320 | tf_op jit(solution)/shard_map/ppermute | solution.py:193
  282.5 9.2 %collective-permute-done.53.refs_5_ = bf16[32,32,256]{2,1,0:T(8,128)(2,1)} collective-permute-done((bf16[32,32,256]{2,1,0:T(8,128)(2,1)}, bf16[32,32,256]{2,1,0:T(8,128)(2,1)}, u32[]{:S(2)}, u32[]{:S(2)}) %collective-permute-start.53) | collective-permute-done | bytes 524320 | tf_op jit(solution)/shard_map/ppermute | solution.py:193
  294.9 8.1 %collective-permute-done.42.refs_1_ = bf16[32,32,256]{2,1,0:T(8,128)(2,1)S(1)} collective-permute-done((bf16[32,32,256]{2,1,0:T(8,128)(2,1)}, bf16[32,32,256]{2,1,0:T(8,128)(2,1)S(1)}, u32[]{:S(2)}, u32[]{:S(2)}) %collective-permute-start.42) | collective-permute-done | bytes 524320 | tf_op jit(solution)/shard_map/ppermute | solution.py:193
  304.0 10.6 %collective-permute-done.43.refs_2_ = bf16[32,32,256]{2,1,0:T(8,128)(2,1)S(1)} collective-permute-done((bf16[32,32,256]{2,1,0:T(8,128)(2,1)}, bf16[32,32,256]{2,1,0:T(8,128)(2,1)S(1)}, u32[]{:S(2)}, u32[]{:S(2)}) %collective-permute-start.43) | collective-permute-done | bytes 524320 | tf_op jit(solution)/shard_map/ppermute | solution.py:193
  315.7 6.9 %shard_map.92 = (bf16[1,8192,512]{2,1,0:T(8,128)(2,1)}, bf16[1,8192,512]{2,1,0:T(8,128)(2,1)}, f32[2048,512]{1,0:T(8,128)}, f32[8,128]{1,0:T(8,128)S(1)}) custom-call(s32[1]{0:T(128)} %bitcast.rank_ref, bf16[1,8192,512]{2,1,0:T(8,128)(2,1)} %values_ref.19, ...), custom_call_target="tpu_custom_call", output_to_operand_aliasing={{0}: (12, {}), {1}: (13, {}), {2}: (14, {})} | custom-call | flops 1024 | bytes 1024 | tf_op jit(solution)/shard_map/pallas_call | solution.py:260
  327.5 9.2 %collective-permute-done.46.refs_5_ = bf16[32,32,256]{2,1,0:T(8,128)(2,1)} collective-permute-done((bf16[32,32,256]{2,1,0:T(8,128)(2,1)}, bf16[32,32,256]{2,1,0:T(8,128)(2,1)}, u32[]{:S(2)}, u32[]{:S(2)}) %collective-permute-start.46) | collective-permute-done | bytes 524320 | tf_op jit(solution)/shard_map/ppermute | solution.py:193
  339.9 7.1 %shard_map.93 = (bf16[1,8192,512]{2,1,0:T(8,128)(2,1)}, bf16[1,8192,512]{2,1,0:T(8,128)(2,1)}, f32[2048,512]{1,0:T(8,128)}, f32[8,128]{1,0:T(8,128)S(1)}) custom-call(s32[1]{0:T(128)} %bitcast.rank_ref, bf16[1,8192,512]{2,1,0:T(8,128)(2,1)} %values_ref.19, ...), custom_call_target="tpu_custom_call", output_to_operand_aliasing={{0}: (12, {}), {1}: (13, {}), {2}: (14, {})} | custom-call | flops 1024 | bytes 1024 | tf_op jit(solution)/shard_map/pallas_call | solution.py:260
  366.0 5.0 %collective-permute-done.57.refs_2_ = bf16[16,32,256]{2,1,0:T(8,128)(2,1)S(1)} collective-permute-done((bf16[16,32,256]{2,1,0:T(8,128)(2,1)}, bf16[16,32,256]{2,1,0:T(8,128)(2,1)S(1)}, u32[]{:S(2)}, u32[]{:S(2)}) %collective-permute-start.57) | collective-permute-done | bytes 262176 | tf_op jit(solution)/shard_map/ppermute | solution.py:193
  371.0 5.2 %shard_map.97 = (bf16[1,8192,512]{2,1,0:T(8,128)(2,1)}, bf16[1,8192,512]{2,1,0:T(8,128)(2,1)}, f32[2048,512]{1,0:T(8,128)}, f32[8,128]{1,0:T(8,128)}) custom-call(s32[1]{0:T(128)} %bitcast.rank_ref, bf16[1,8192,512]{2,1,0:T(8,128)(2,1)} %values_ref.19, ...), custom_call_target="tpu_custom_call", output_to_operand_aliasing={{0}: (13, {}), {1}: (14, {}), {2}: (15, {})} | custom-call | flops 1024 | bytes 1024 | tf_op jit(solution)/shard_map/pallas_call | solution.py:260
  376.6 5.2 %collective-permute-done.60.refs_5_ = bf16[16,32,256]{2,1,0:T(8,128)(2,1)} collective-permute-done((bf16[16,32,256]{2,1,0:T(8,128)(2,1)}, bf16[16,32,256]{2,1,0:T(8,128)(2,1)}, u32[]{:S(2)}, u32[]{:S(2)}) %collective-permute-start.60) | collective-permute-done | bytes 262176 | tf_op jit(solution)/shard_map/ppermute | solution.py:193
  (236 shorter events, 117.2 us)
Async XLA Ops:
  7.2 363.8 %reduce-scatter.2.cloned.1.call-start = ((), (), s32[]{:S(2)}) async-start(), calls=%async_computation.1 | async-start | bytes 10485760 | tf_op jit(solution)/shard_map/reduce_scatter | solution.py:342
  51.3 26.0 %collective-permute-start.3 = (bf16[32,32,256]{2,1,0:T(8,128)(2,1)}, bf16[32,32,256]{2,1,0:T(8,128)(2,1)S(1)}, u32[]{:S(2)}, u32[]{:S(2)}) collective-permute-start(bf16[32,32,256]{2,1,0:T(8,128)(2,1)} %get-tuple-element.168), channel_id=1, source_target_pairs={{0,6},{1,7},{2,4},{3,5},{4,2},{5,3},{6,0},{7,1},{8,14},{9,15},{10,... | collective-permute-start | bytes 1572872 | tf_op jit(solution)/shard_map/ppermute | solution.py:193
  54.4 30.3 %collective-permute-start.4 = (bf16[32,32,256]{2,1,0:T(8,128)(2,1)}, bf16[32,32,256]{2,1,0:T(8,128)(2,1)S(1)}, u32[]{:S(2)}, u32[]{:S(2)}) collective-permute-start(bf16[32,32,256]{2,1,0:T(8,128)(2,1)} %get-tuple-element.169), channel_id=1, source_target_pairs={{0,2},{1,3},{2,0},{3,1},{4,6},{5,7},{6,4},{7,5},{8,10},{9,11},{10,... | collective-permute-start | bytes 1572872 | tf_op jit(solution)/shard_map/ppermute | solution.py:193
  55.7 30.5 %collective-permute-start.5 = (bf16[32,32,256]{2,1,0:T(8,128)(2,1)}, bf16[32,32,256]{2,1,0:T(8,128)(2,1)S(1)}, u32[]{:S(2)}, u32[]{:S(2)}) collective-permute-start(bf16[32,32,256]{2,1,0:T(8,128)(2,1)} %get-tuple-element.170), channel_id=1, source_target_pairs={{0,4},{1,5},{2,6},{3,7},{4,0},{5,1},{6,2},{7,3},{8,12},{9,13},{10,... | collective-permute-start | bytes 1572872 | tf_op jit(solution)/shard_map/ppermute | solution.py:193
  62.0 33.1 %collective-permute-start.6 = (bf16[32,32,256]{2,1,0:T(8,128)(2,1)}, bf16[32,32,256]{2,1,0:T(8,128)(2,1)S(1)}, u32[]{:S(2)}, u32[]{:S(2)}) collective-permute-start(bf16[32,32,256]{2,1,0:T(8,128)(2,1)} %get-tuple-element.171), channel_id=1, source_target_pairs={{0,7},{1,6},{2,5},{3,4},{4,3},{5,2},{6,1},{7,0},{8,15},{9,14},{10,... | collective-permute-start | bytes 1572872 | tf_op jit(solution)/shard_map/ppermute | solution.py:193
  77.1 31.2 %collective-permute-start.7 = (bf16[32,32,256]{2,1,0:T(8,128)(2,1)}, bf16[32,32,256]{2,1,0:T(8,128)(2,1)S(1)}, u32[]{:S(2)}, u32[]{:S(2)}) collective-permute-start(bf16[32,32,256]{2,1,0:T(8,128)(2,1)} %get-tuple-element.172), channel_id=1, source_target_pairs={{0,3},{1,2},{2,1},{3,0},{4,7},{5,6},{6,5},{7,4},{8,11},{9,10},{10,... | collective-permute-start | bytes 1572872 | tf_op jit(solution)/shard_map/ppermute | solution.py:193
  77.3 40.6 %collective-permute-start.28 = (bf16[32,32,256]{2,1,0:T(8,128)(2,1)}, bf16[32,32,256]{2,1,0:T(8,128)(2,1)S(1)}, u32[]{:S(2)}, u32[]{:S(2)}) collective-permute-start(bf16[32,32,256]{2,1,0:T(8,128)(2,1)} %get-tuple-element.202), channel_id=1, source_target_pairs={{0,6},{1,7},{2,4},{3,5},{4,2},{5,3},{6,0},{7,1},{8,14},{9,15},{10,... | collective-permute-start | bytes 1572872 | tf_op jit(solution)/shard_map/ppermute | solution.py:193
  84.7 45.0 %collective-permute-start.29 = (bf16[32,32,256]{2,1,0:T(8,128)(2,1)}, bf16[32,32,256]{2,1,0:T(8,128)(2,1)S(1)}, u32[]{:S(2)}, u32[]{:S(2)}) collective-permute-start(bf16[32,32,256]{2,1,0:T(8,128)(2,1)} %get-tuple-element.203), channel_id=1, source_target_pairs={{0,2},{1,3},{2,0},{3,1},{4,6},{5,7},{6,4},{7,5},{8,10},{9,11},{10,... | collective-permute-start | bytes 1572872 | tf_op jit(solution)/shard_map/ppermute | solution.py:193
  86.2 43.5 %collective-permute-start.8 = (bf16[32,32,256]{2,1,0:T(8,128)(2,1)}, bf16[32,32,256]{2,1,0:T(8,128)(2,1)}, u32[]{:S(2)}, u32[]{:S(2)}) collective-permute-start(bf16[32,32,256]{2,1,0:T(8,128)(2,1)} %get-tuple-element.176), channel_id=1, source_target_pairs={{0,5},{1,4},{2,7},{3,6},{4,1},{5,0},{6,3},{7,2},{8,13},{9,12},{10,... | collective-permute-start | bytes 1572872 | tf_op jit(solution)/shard_map/ppermute | solution.py:193
  95.1 36.3 %collective-permute-start.9 = (bf16[32,32,256]{2,1,0:T(8,128)(2,1)}, bf16[32,32,256]{2,1,0:T(8,128)(2,1)}, u32[]{:S(2)}, u32[]{:S(2)}) collective-permute-start(bf16[32,32,256]{2,1,0:T(8,128)(2,1)} %get-tuple-element.177), channel_id=1, source_target_pairs={{0,1},{1,0},{2,3},{3,2},{4,5},{5,4},{6,7},{7,6},{8,9},{9,8},{10,11... | collective-permute-start | bytes 1572872 | tf_op jit(solution)/shard_map/ppermute | solution.py:193
  108.3 36.2 %collective-permute-start.30 = (bf16[32,32,256]{2,1,0:T(8,128)(2,1)}, bf16[32,32,256]{2,1,0:T(8,128)(2,1)S(1)}, u32[]{:S(2)}, u32[]{:S(2)}) collective-permute-start(bf16[32,32,256]{2,1,0:T(8,128)(2,1)} %get-tuple-element.204), channel_id=1, source_target_pairs={{0,4},{1,5},{2,6},{3,7},{4,0},{5,1},{6,2},{7,3},{8,12},{9,13},{10,... | collective-permute-start | bytes 1572872 | tf_op jit(solution)/shard_map/ppermute | solution.py:193
  117.9 28.3 %collective-permute-start.31 = (bf16[32,32,256]{2,1,0:T(8,128)(2,1)}, bf16[32,32,256]{2,1,0:T(8,128)(2,1)S(1)}, u32[]{:S(2)}, u32[]{:S(2)}) collective-permute-start(bf16[32,32,256]{2,1,0:T(8,128)(2,1)} %get-tuple-element.209), channel_id=1, source_target_pairs={{0,7},{1,6},{2,5},{3,4},{4,3},{5,2},{6,1},{7,0},{8,15},{9,14},{10,... | collective-permute-start | bytes 1572872 | tf_op jit(solution)/shard_map/ppermute | solution.py:193
  147.0 27.8 %collective-permute-start.1 = (bf16[32,32,256]{2,1,0:T(8,128)(2,1)}, bf16[32,32,256]{2,1,0:T(8,128)(2,1)S(1)}, u32[]{:S(2)}, u32[]{:S(2)}) collective-permute-start(bf16[32,32,256]{2,1,0:T(8,128)(2,1)} %get-tuple-element.161), channel_id=1, source_target_pairs={{0,2},{1,3},{2,0},{3,1},{4,6},{5,7},{6,4},{7,5},{8,10},{9,11},{10,... | collective-permute-start | bytes 1572872 | tf_op jit(solution)/shard_map/ppermute | solution.py:193
  151.8 33.3 %collective-permute-start.24 = (bf16[32,32,256]{2,1,0:T(8,128)(2,1)}, bf16[32,32,256]{2,1,0:T(8,128)(2,1)S(1)}, u32[]{:S(2)}, u32[]{:S(2)}) collective-permute-start(bf16[32,32,256]{2,1,0:T(8,128)(2,1)} %get-tuple-element.197), channel_id=1, source_target_pairs={{0,7},{1,6},{2,5},{3,4},{4,3},{5,2},{6,1},{7,0},{8,15},{9,14},{10,... | collective-permute-start | bytes 1572872 | tf_op jit(solution)/shard_map/ppermute | solution.py:193
  154.7 41.7 %collective-permute-start.25 = (bf16[32,32,256]{2,1,0:T(8,128)(2,1)}, bf16[32,32,256]{2,1,0:T(8,128)(2,1)S(1)}, u32[]{:S(2)}, u32[]{:S(2)}) collective-permute-start(bf16[32,32,256]{2,1,0:T(8,128)(2,1)} %get-tuple-element.198), channel_id=1, source_target_pairs={{0,3},{1,2},{2,1},{3,0},{4,7},{5,6},{6,5},{7,4},{8,11},{9,10},{10,... | collective-permute-start | bytes 1572872 | tf_op jit(solution)/shard_map/ppermute | solution.py:193
  168.1 29.6 %collective-permute-start.26 = (bf16[32,32,256]{2,1,0:T(8,128)(2,1)}, bf16[32,32,256]{2,1,0:T(8,128)(2,1)}, u32[]{:S(2)}, u32[]{:S(2)}) collective-permute-start(bf16[32,32,256]{2,1,0:T(8,128)(2,1)} %get-tuple-element.199), channel_id=1, source_target_pairs={{0,5},{1,4},{2,7},{3,6},{4,1},{5,0},{6,3},{7,2},{8,13},{9,12},{10,... | collective-permute-start | bytes 1572872 | tf_op jit(solution)/shard_map/ppermute | solution.py:193
  174.8 36.1 %collective-permute-start.35 = (bf16[32,32,256]{2,1,0:T(8,128)(2,1)}, bf16[32,32,256]{2,1,0:T(8,128)(2,1)S(1)}, u32[]{:S(2)}, u32[]{:S(2)}) collective-permute-start(bf16[32,32,256]{2,1,0:T(8,128)(2,1)} %get-tuple-element.237), channel_id=1, source_target_pairs={{0,6},{1,7},{2,4},{3,5},{4,2},{5,3},{6,0},{7,1},{8,14},{9,15},{10,... | collective-permute-start | bytes 1572872 | tf_op jit(solution)/shard_map/ppermute | solution.py:193
  185.2 33.5 %collective-permute-start.36 = (bf16[32,32,256]{2,1,0:T(8,128)(2,1)}, bf16[32,32,256]{2,1,0:T(8,128)(2,1)S(1)}, u32[]{:S(2)}, u32[]{:S(2)}) collective-permute-start(bf16[32,32,256]{2,1,0:T(8,128)(2,1)} %get-tuple-element.238), channel_id=1, source_target_pairs={{0,2},{1,3},{2,0},{3,1},{4,6},{5,7},{6,4},{7,5},{8,10},{9,11},{10,... | collective-permute-start | bytes 1572872 | tf_op jit(solution)/shard_map/ppermute | solution.py:193
  223.1 25.3 %collective-permute-start.40 = (bf16[32,32,256]{2,1,0:T(8,128)(2,1)}, bf16[32,32,256]{2,1,0:T(8,128)(2,1)}, u32[]{:S(2)}, u32[]{:S(2)}) collective-permute-start(bf16[32,32,256]{2,1,0:T(8,128)(2,1)} %get-tuple-element.242), channel_id=1, source_target_pairs={{0,5},{1,4},{2,7},{3,6},{4,1},{5,0},{6,3},{7,2},{8,13},{9,12},{10,... | collective-permute-start | bytes 1572872 | tf_op jit(solution)/shard_map/ppermute | solution.py:193
  223.3 27.0 %collective-permute-start.41 = (bf16[32,32,256]{2,1,0:T(8,128)(2,1)}, bf16[32,32,256]{2,1,0:T(8,128)(2,1)}, u32[]{:S(2)}, u32[]{:S(2)}) collective-permute-start(bf16[32,32,256]{2,1,0:T(8,128)(2,1)} %get-tuple-element.243), channel_id=1, source_target_pairs={{0,1},{1,0},{2,3},{3,2},{4,5},{5,4},{6,7},{7,6},{8,9},{9,8},{10,11... | collective-permute-start | bytes 1572872 | tf_op jit(solution)/shard_map/ppermute | solution.py:193
  224.0 37.2 %collective-permute-start.49 = (bf16[32,32,256]{2,1,0:T(8,128)(2,1)}, bf16[32,32,256]{2,1,0:T(8,128)(2,1)S(1)}, u32[]{:S(2)}, u32[]{:S(2)}) collective-permute-start(bf16[32,32,256]{2,1,0:T(8,128)(2,1)} %get-tuple-element.260), channel_id=1, source_target_pairs={{0,6},{1,7},{2,4},{3,5},{4,2},{5,3},{6,0},{7,1},{8,14},{9,15},{10,... | collective-permute-start | bytes 1572872 | tf_op jit(solution)/shard_map/ppermute | solution.py:193
  236.6 33.0 %collective-permute-start.50 = (bf16[32,32,256]{2,1,0:T(8,128)(2,1)}, bf16[32,32,256]{2,1,0:T(8,128)(2,1)S(1)}, u32[]{:S(2)}, u32[]{:S(2)}) collective-permute-start(bf16[32,32,256]{2,1,0:T(8,128)(2,1)} %get-tuple-element.261), channel_id=1, source_target_pairs={{0,2},{1,3},{2,0},{3,1},{4,6},{5,7},{6,4},{7,5},{8,10},{9,11},{10,... | collective-permute-start | bytes 1572872 | tf_op jit(solution)/shard_map/ppermute | solution.py:193
  248.4 32.5 %collective-permute-start.52 = (bf16[32,32,256]{2,1,0:T(8,128)(2,1)}, bf16[32,32,256]{2,1,0:T(8,128)(2,1)}, u32[]{:S(2)}, u32[]{:S(2)}) collective-permute-start(bf16[32,32,256]{2,1,0:T(8,128)(2,1)} %get-tuple-element.263), channel_id=1, source_target_pairs={{0,7},{1,6},{2,5},{3,4},{4,3},{5,2},{6,1},{7,0},{8,15},{9,14},{10,... | collective-permute-start | bytes 1572872 | tf_op jit(solution)/shard_map/ppermute | solution.py:193
  250.4 41.3 %collective-permute-start.53 = (bf16[32,32,256]{2,1,0:T(8,128)(2,1)}, bf16[32,32,256]{2,1,0:T(8,128)(2,1)}, u32[]{:S(2)}, u32[]{:S(2)}) collective-permute-start(bf16[32,32,256]{2,1,0:T(8,128)(2,1)} %get-tuple-element.264), channel_id=1, source_target_pairs={{0,3},{1,2},{2,1},{3,0},{4,7},{5,6},{6,5},{7,4},{8,11},{9,10},{10,... | collective-permute-start | bytes 1572872 | tf_op jit(solution)/shard_map/ppermute | solution.py:193
  261.2 31.6 %collective-permute-start.54 = (bf16[32,32,256]{2,1,0:T(8,128)(2,1)}, bf16[32,32,256]{2,1,0:T(8,128)(2,1)S(1)}, u32[]{:S(2)}, u32[]{:S(2)}) collective-permute-start(bf16[32,32,256]{2,1,0:T(8,128)(2,1)} %get-tuple-element.265), channel_id=1, source_target_pairs={{0,5},{1,4},{2,7},{3,6},{4,1},{5,0},{6,3},{7,2},{8,13},{9,12},{10,... | collective-permute-start | bytes 1572872 | tf_op jit(solution)/shard_map/ppermute | solution.py:193
  269.6 25.0 %collective-permute-start.55 = (bf16[32,32,256]{2,1,0:T(8,128)(2,1)}, bf16[32,32,256]{2,1,0:T(8,128)(2,1)S(1)}, u32[]{:S(2)}, u32[]{:S(2)}) collective-permute-start(bf16[32,32,256]{2,1,0:T(8,128)(2,1)} %get-tuple-element.266), channel_id=1, source_target_pairs={{0,1},{1,0},{2,3},{3,2},{4,5},{5,4},{6,7},{7,6},{8,9},{9,8},{10,11... | collective-permute-start | bytes 1572872 | tf_op jit(solution)/shard_map/ppermute | solution.py:193
  270.4 32.6 %collective-permute-start.42 = (bf16[32,32,256]{2,1,0:T(8,128)(2,1)}, bf16[32,32,256]{2,1,0:T(8,128)(2,1)S(1)}, u32[]{:S(2)}, u32[]{:S(2)}) collective-permute-start(bf16[32,32,256]{2,1,0:T(8,128)(2,1)} %get-tuple-element.245), channel_id=1, source_target_pairs={{0,6},{1,7},{2,4},{3,5},{4,2},{5,3},{6,0},{7,1},{8,14},{9,15},{10,... | collective-permute-start | bytes 1572872 | tf_op jit(solution)/shard_map/ppermute | solution.py:193
  280.9 33.7 %collective-permute-start.43 = (bf16[32,32,256]{2,1,0:T(8,128)(2,1)}, bf16[32,32,256]{2,1,0:T(8,128)(2,1)S(1)}, u32[]{:S(2)}, u32[]{:S(2)}) collective-permute-start(bf16[32,32,256]{2,1,0:T(8,128)(2,1)} %get-tuple-element.246), channel_id=1, source_target_pairs={{0,2},{1,3},{2,0},{3,1},{4,6},{5,7},{6,4},{7,5},{8,10},{9,11},{10,... | collective-permute-start | bytes 1572872 | tf_op jit(solution)/shard_map/ppermute | solution.py:193
  291.7 31.6 %collective-permute-start.44 = (bf16[32,32,256]{2,1,0:T(8,128)(2,1)}, bf16[32,32,256]{2,1,0:T(8,128)(2,1)S(1)}, u32[]{:S(2)}, u32[]{:S(2)}) collective-permute-start(bf16[32,32,256]{2,1,0:T(8,128)(2,1)} %get-tuple-element.247), channel_id=1, source_target_pairs={{0,4},{1,5},{2,6},{3,7},{4,0},{5,1},{6,2},{7,3},{8,12},{9,13},{10,... | collective-permute-start | bytes 1572872 | tf_op jit(solution)/shard_map/ppermute | solution.py:193
  292.7 33.2 %collective-permute-start.45 = (bf16[32,32,256]{2,1,0:T(8,128)(2,1)}, bf16[32,32,256]{2,1,0:T(8,128)(2,1)}, u32[]{:S(2)}, u32[]{:S(2)}) collective-permute-start(bf16[32,32,256]{2,1,0:T(8,128)(2,1)} %get-tuple-element.248), channel_id=1, source_target_pairs={{0,7},{1,6},{2,5},{3,4},{4,3},{5,2},{6,1},{7,0},{8,15},{9,14},{10,... | collective-permute-start | bytes 1572872 | tf_op jit(solution)/shard_map/ppermute | solution.py:193
  294.6 42.1 %collective-permute-start.46 = (bf16[32,32,256]{2,1,0:T(8,128)(2,1)}, bf16[32,32,256]{2,1,0:T(8,128)(2,1)}, u32[]{:S(2)}, u32[]{:S(2)}) collective-permute-start(bf16[32,32,256]{2,1,0:T(8,128)(2,1)} %get-tuple-element.249), channel_id=1, source_target_pairs={{0,3},{1,2},{2,1},{3,0},{4,7},{5,6},{6,5},{7,4},{8,11},{9,10},{10,... | collective-permute-start | bytes 1572872 | tf_op jit(solution)/shard_map/ppermute | solution.py:193
  303.0 34.7 %collective-permute-start.47 = (bf16[32,32,256]{2,1,0:T(8,128)(2,1)}, bf16[32,32,256]{2,1,0:T(8,128)(2,1)}, u32[]{:S(2)}, u32[]{:S(2)}) collective-permute-start(bf16[32,32,256]{2,1,0:T(8,128)(2,1)} %get-tuple-element.250), channel_id=1, source_target_pairs={{0,5},{1,4},{2,7},{3,6},{4,1},{5,0},{6,3},{7,2},{8,13},{9,12},{10,... | collective-permute-start | bytes 1572872 | tf_op jit(solution)/shard_map/ppermute | solution.py:193
  (90 other events, 1457.4 us)
Sparse Core Ops, SparseCore 0:
  219.8 145.3 reduce-scatter.1

commit v8 on v7

--- a/solution.py
+++ b/solution.py
@@ -228,7 +228,7 @@
             cost_estimate=COST,
         )(rank, kernel, right_factor, *arrived, *held, *after)
 
-    def gate(held, after):
+    def gate(held, after, grant=params):
         return list(
             pl.pallas_call(
                 gate_kernel,
@@ -236,9 +236,9 @@
                 in_specs=unread(held) + unread(after),
                 out_specs=unread(held),
                 input_output_aliases={n: n for n in range(len(held))},
-                compiler_params=params,
+                compiler_params=grant,
                 cost_estimate=COST,
-            )(*held, *after)
+            )(*[pltpu.with_memory_space_constraint(x, pltpu.HBM) for x in held], *after)
         )
 
     def left_back(q, part, arrived, reduced, outputs, after):
@@ -338,7 +338,7 @@
             if q >= 1 and part == 0:
                 back_step(q - 1)
         if q == 0:
-            (terms,) = gate([terms], returned[0][1 : 1 + EARLY])
+            (terms,) = gate([terms], returned[0][1 : 1 + EARLY], back_params)
             reduced = lax.psum_scatter(terms, "dp", scatter_dimension=0, tiled=True)
     back_step(chunks - 1)
     return tuple(outputs)

time: 393 us -> 393 us (level)
    unnamed x102 -> x90, local copies, waits for them, and re-layouts: 12.7 us -> 11.8 us
where the time goes in v8:
time: 393 us; the launch traced here: 392 us
  waiting for transfers between devices  186 us (47%)
  Pallas kernels  109 us (28%)
  starting transfers between devices  70.3 us (18%)
  between operations  14.5 us (4%)
  local copies, waits for them, and re-layouts  11.8 us (3%)
    ppermute x70, waiting for transfers between devices, exchange(): lax.ppermute(sends[n], 'seq', [(r, r ^ moves[n]) for r in range(ranks)])  186 us
    ppermute x70, starting transfers between devices, exchange(): lax.ppermute(sends[n], 'seq', [(r, r ^ moves[n]) for r in range(ranks)])  70.2 us
    pallas_call x4, Pallas kernels, right_both(): pl.pallas_call(functools.partial(right_kernel, ranks, ins, outs), out_sha...  52.6 us
    pallas_call x5, Pallas kernels, left_back(): pl.pallas_call(functools.partial(left_back_kernel, ranks, terms), out_sha...  30 us
    pallas_call x5, Pallas kernels, left_forward(): pl.pallas_call(functools.partial(left_forward_kernel, ranks), out_shape=[...  26.6 us
    unnamed x90, local copies, waits for them, and re-layouts  11.8 us
  transfers between devices with their start and end apart: 71, of which 32 were waited for; matrix products, arithmetic and copies ran while one was open for 0% of the time, Pallas kernels for 26%

profile of v8, /device:TPU:0, one launch (start us, length us, event | category | flops | bytes accessed | tf_op | source)
XLA Modules:
  0.0 392.0 jit_solution(7813280740558487567)
XLA Ops:
  22.2 6.3 %collective-permute-done.11.refs_2_ = bf16[16,32,256]{2,1,0:T(8,128)(2,1)} collective-permute-done((bf16[16,32,256]{2,1,0:T(8,128)(2,1)}, bf16[16,32,256]{2,1,0:T(8,128)(2,1)}, u32[]{:S(2)}, u32[]{:S(2)}) %collective-permute-start.11) | collective-permute-done | bytes 262176 | tf_op jit(solution)/shard_map/ppermute | solution.py:193
  33.8 5.0 %collective-permute-done.14.refs_5_ = bf16[16,32,256]{2,1,0:T(8,128)(2,1)S(1)} collective-permute-done((bf16[16,32,256]{2,1,0:T(8,128)(2,1)}, bf16[16,32,256]{2,1,0:T(8,128)(2,1)S(1)}, u32[]{:S(2)}, u32[]{:S(2)}) %collective-permute-start.14) | collective-permute-done | bytes 262176 | tf_op jit(solution)/shard_map/ppermute | solution.py:193
  44.7 6.5 %shard_map.78 = (bf16[32,32,256]{2,1,0:T(8,128)(2,1)}, bf16[32,32,256]{2,1,0:T(8,128)(2,1)}, bf16[32,32,256]{2,1,0:T(8,128)(2,1)}, bf16[32,32,256]{2,1,0:T(8,128...) custom-call(s32[1]{0:T(128)} %bitcast.rank_ref, ...), custom_call_target="tpu_custom_call" | custom-call | flops 1024 | bytes 1024 | tf_op jit(solution)/shard_map/pallas_call | solution.py:176
  56.2 5.1 %collective-permute-done.21.refs_13_ = bf16[16,32,256]{2,1,0:T(8,128)(2,1)S(1)} collective-permute-done((bf16[16,32,256]{2,1,0:T(8,128)(2,1)}, bf16[16,32,256]{2,1,0:T(8,128)(2,1)S(1)}, u32[]{:S(2)}, u32[]{:S(2)}) %collective-permute-start.21) | collective-permute-done | bytes 262176 | tf_op jit(solution)/shard_map/ppermute | solution.py:193
  64.1 6.4 %shard_map.79 = (bf16[32,32,256]{2,1,0:T(8,128)(2,1)}, bf16[32,32,256]{2,1,0:T(8,128)(2,1)}, bf16[32,32,256]{2,1,0:T(8,128)(2,1)}, bf16[32,32,256]{2,1,0:T(8,128...) custom-call(s32[1]{0:T(128)} %bitcast.rank_ref, ...), custom_call_target="tpu_custom_call" | custom-call | flops 1024 | bytes 1024 | tf_op jit(solution)/shard_map/pallas_call | solution.py:176
  70.5 6.5 %shard_map.80 = (bf16[32,32,256]{2,1,0:T(8,128)(2,1)}, bf16[32,32,256]{2,1,0:T(8,128)(2,1)}, bf16[32,32,256]{2,1,0:T(8,128)(2,1)}, bf16[32,32,256]{2,1,0:T(8,128...) custom-call(s32[1]{0:T(128)} %bitcast.rank_ref, ...), custom_call_target="tpu_custom_call" | custom-call | flops 1024 | bytes 1024 | tf_op jit(solution)/shard_map/pallas_call | solution.py:176
  80.2 4.5 %collective-permute-done.4.refs_2_ = bf16[32,32,256]{2,1,0:T(8,128)(2,1)S(1)} collective-permute-done((bf16[32,32,256]{2,1,0:T(8,128)(2,1)}, bf16[32,32,256]{2,1,0:T(8,128)(2,1)S(1)}, u32[]{:S(2)}, u32[]{:S(2)}) %collective-permute-start.4) | collective-permute-done | bytes 524320 | tf_op jit(solution)/shard_map/ppermute | solution.py:193
  86.2 8.9 %collective-permute-done.6.refs_4_ = bf16[32,32,256]{2,1,0:T(8,128)(2,1)S(1)} collective-permute-done((bf16[32,32,256]{2,1,0:T(8,128)(2,1)}, bf16[32,32,256]{2,1,0:T(8,128)(2,1)S(1)}, u32[]{:S(2)}, u32[]{:S(2)}) %collective-permute-start.6) | collective-permute-done | bytes 524320 | tf_op jit(solution)/shard_map/ppermute | solution.py:193
  95.2 13.1 %shard_map.82 = (bf16[32,32,256]{2,1,0:T(8,128)(2,1)}, bf16[32,32,256]{2,1,0:T(8,128)(2,1)}, bf16[32,32,256]{2,1,0:T(8,128)(2,1)}, bf16[32,32,256]{2,1,0:T(8,128...) custom-call(s32[1]{0:T(128)} %bitcast.rank_ref, ...), custom_call_target="tpu_custom_call" | custom-call | flops 1024 | bytes 1024 | tf_op jit(solution)/shard_map/pallas_call | solution.py:205
  110.4 7.5 %collective-permute-done.28.refs_1_ = bf16[32,32,256]{2,1,0:T(8,128)(2,1)S(1)} collective-permute-done((bf16[32,32,256]{2,1,0:T(8,128)(2,1)}, bf16[32,32,256]{2,1,0:T(8,128)(2,1)S(1)}, u32[]{:S(2)}, u32[]{:S(2)}) %collective-permute-start.28) | collective-permute-done | bytes 524320 | tf_op jit(solution)/shard_map/ppermute | solution.py:193
  118.3 11.4 %collective-permute-done.29.refs_2_ = bf16[32,32,256]{2,1,0:T(8,128)(2,1)S(1)} collective-permute-done((bf16[32,32,256]{2,1,0:T(8,128)(2,1)}, bf16[32,32,256]{2,1,0:T(8,128)(2,1)S(1)}, u32[]{:S(2)}, u32[]{:S(2)}) %collective-permute-start.29) | collective-permute-done | bytes 524320 | tf_op jit(solution)/shard_map/ppermute | solution.py:193
  131.4 13.1 %shard_map.83 = (bf16[32,32,256]{2,1,0:T(8,128)(2,1)}, bf16[32,32,256]{2,1,0:T(8,128)(2,1)}, bf16[32,32,256]{2,1,0:T(8,128)(2,1)}, bf16[32,32,256]{2,1,0:T(8,128...) custom-call(s32[1]{0:T(128)} %bitcast.rank_ref, ...), custom_call_target="tpu_custom_call", output_to_operand_aliasing={{8}: (11, {})} | custom-call | flops 1024 | bytes 1024 | tf_op jit(solution)/shard_map/pallas_call | solution.py:205
  154.7 13.3 %shard_map.86 = (bf16[32,32,256]{2,1,0:T(8,128)(2,1)}, bf16[32,32,256]{2,1,0:T(8,128)(2,1)}, bf16[32,32,256]{2,1,0:T(8,128)(2,1)}, bf16[32,32,256]{2,1,0:T(8,128...) custom-call(s32[1]{0:T(128)} %bitcast.rank_ref, ...), custom_call_target="tpu_custom_call", output_to_operand_aliasing={{8}: (11, {})} | custom-call | flops 1024 | bytes 1024 | tf_op jit(solution)/shard_map/pallas_call | solution.py:205
  168.6 6.2 %collective-permute-done.1.refs_2_ = bf16[32,32,256]{2,1,0:T(8,128)(2,1)S(1)} collective-permute-done((bf16[32,32,256]{2,1,0:T(8,128)(2,1)}, bf16[32,32,256]{2,1,0:T(8,128)(2,1)S(1)}, u32[]{:S(2)}, u32[]{:S(2)}) %collective-permute-start.1) | collective-permute-done | bytes 524320 | tf_op jit(solution)/shard_map/ppermute | solution.py:193
  176.9 8.3 %collective-permute-done.24.refs_4_ = bf16[32,32,256]{2,1,0:T(8,128)(2,1)S(1)} collective-permute-done((bf16[32,32,256]{2,1,0:T(8,128)(2,1)}, bf16[32,32,256]{2,1,0:T(8,128)(2,1)S(1)}, u32[]{:S(2)}, u32[]{:S(2)}) %collective-permute-start.24) | collective-permute-done | bytes 524320 | tf_op jit(solution)/shard_map/ppermute | solution.py:193
  185.7 10.7 %collective-permute-done.25.refs_5_ = bf16[32,32,256]{2,1,0:T(8,128)(2,1)S(1)} collective-permute-done((bf16[32,32,256]{2,1,0:T(8,128)(2,1)}, bf16[32,32,256]{2,1,0:T(8,128)(2,1)S(1)}, u32[]{:S(2)}, u32[]{:S(2)}) %collective-permute-start.25) | collective-permute-done | bytes 524320 | tf_op jit(solution)/shard_map/ppermute | solution.py:193
  197.7 13.1 %shard_map.87 = (bf16[16,32,256]{2,1,0:T(8,128)(2,1)}, bf16[16,32,256]{2,1,0:T(8,128)(2,1)}, bf16[16,32,256]{2,1,0:T(8,128)(2,1)}, bf16[16,32,256]{2,1,0:T(8,128...) custom-call(s32[1]{0:T(128)} %bitcast.rank_ref, ...), custom_call_target="tpu_custom_call", output_to_operand_aliasing={{16}: (11, {})} | custom-call | flops 1024 | bytes 1024 | tf_op jit(solution)/shard_map/pallas_call | solution.py:205
  210.9 7.7 %collective-permute-done.36.refs_2_ = bf16[32,32,256]{2,1,0:T(8,128)(2,1)S(1)} collective-permute-done((bf16[32,32,256]{2,1,0:T(8,128)(2,1)}, bf16[32,32,256]{2,1,0:T(8,128)(2,1)S(1)}, u32[]{:S(2)}, u32[]{:S(2)}) %collective-permute-start.36) | collective-permute-done | bytes 524320 | tf_op jit(solution)/shard_map/ppermute | solution.py:193
  225.3 9.6 %collective-permute-done.38.refs_4_ = bf16[32,32,256]{2,1,0:T(8,128)(2,1)S(1)} collective-permute-done((bf16[32,32,256]{2,1,0:T(8,128)(2,1)S(1)}, bf16[32,32,256]{2,1,0:T(8,128)(2,1)S(1)}, u32[]{:S(2)}, u32[]{:S(2)}) %collective-permute-start.38) | collective-permute-done | bytes 524320 | tf_op jit(solution)/shard_map/ppermute | solution.py:193
  237.1 8.7 %collective-permute-done.39.refs_5_ = bf16[32,32,256]{2,1,0:T(8,128)(2,1)S(1)} collective-permute-done((bf16[32,32,256]{2,1,0:T(8,128)(2,1)}, bf16[32,32,256]{2,1,0:T(8,128)(2,1)S(1)}, u32[]{:S(2)}, u32[]{:S(2)}) %collective-permute-start.39) | collective-permute-done | bytes 524320 | tf_op jit(solution)/shard_map/ppermute | solution.py:193
  252.9 6.9 %shard_map.89 = (bf16[1,8192,512]{2,1,0:T(8,128)(2,1)}, bf16[1,8192,512]{2,1,0:T(8,128)(2,1)}, f32[2048,512]{1,0:T(8,128)}, f32[8,128]{1,0:T(8,128)S(1)}) custom-call(s32[1]{0:T(128)} %bitcast.rank_ref, bf16[1,8192,512]{2,1,0:T(8,128)(2,1)} %values_ref.19, bf16[1,8192,512]{2,1,0:T(8,128)(2,1)} %cotangent_ref.19, bf16[32,256,256]{2,1,0:T(8,128)(2,1)} %left_ref.19, ...), custom_call_target="tpu_custom_call" | custom-call | flops 1024 | bytes 1024 | tf_op jit(solution)/shard_map/pallas_call | solution.py:260
  260.8 8.0 %collective-permute-done.50.refs_2_ = bf16[32,32,256]{2,1,0:T(8,128)(2,1)S(1)} collective-permute-done((bf16[32,32,256]{2,1,0:T(8,128)(2,1)}, bf16[32,32,256]{2,1,0:T(8,128)(2,1)S(1)}, u32[]{:S(2)}, u32[]{:S(2)}) %collective-permute-start.50) | collective-permute-done | bytes 524320 | tf_op jit(solution)/shard_map/ppermute | solution.py:193
  272.0 8.0 %collective-permute-done.52.refs_4_ = bf16[32,32,256]{2,1,0:T(8,128)(2,1)} collective-permute-done((bf16[32,32,256]{2,1,0:T(8,128)(2,1)}, bf16[32,32,256]{2,1,0:T(8,128)(2,1)}, u32[]{:S(2)}, u32[]{:S(2)}) %collective-permute-start.52) | collective-permute-done | bytes 524320 | tf_op jit(solution)/shard_map/ppermute | solution.py:193
  281.4 9.5 %collective-permute-done.53.refs_5_ = bf16[32,32,256]{2,1,0:T(8,128)(2,1)} collective-permute-done((bf16[32,32,256]{2,1,0:T(8,128)(2,1)}, bf16[32,32,256]{2,1,0:T(8,128)(2,1)}, u32[]{:S(2)}, u32[]{:S(2)}) %collective-permute-start.53) | collective-permute-done | bytes 524320 | tf_op jit(solution)/shard_map/ppermute | solution.py:193
  294.1 8.3 %collective-permute-done.42.refs_1_ = bf16[32,32,256]{2,1,0:T(8,128)(2,1)S(1)} collective-permute-done((bf16[32,32,256]{2,1,0:T(8,128)(2,1)}, bf16[32,32,256]{2,1,0:T(8,128)(2,1)S(1)}, u32[]{:S(2)}, u32[]{:S(2)}) %collective-permute-start.42) | collective-permute-done | bytes 524320 | tf_op jit(solution)/shard_map/ppermute | solution.py:193
  303.2 10.6 %collective-permute-done.43.refs_2_ = bf16[32,32,256]{2,1,0:T(8,128)(2,1)S(1)} collective-permute-done((bf16[32,32,256]{2,1,0:T(8,128)(2,1)}, bf16[32,32,256]{2,1,0:T(8,128)(2,1)S(1)}, u32[]{:S(2)}, u32[]{:S(2)}) %collective-permute-start.43) | collective-permute-done | bytes 524320 | tf_op jit(solution)/shard_map/ppermute | solution.py:193
  314.9 6.9 %shard_map.92 = (bf16[1,8192,512]{2,1,0:T(8,128)(2,1)}, bf16[1,8192,512]{2,1,0:T(8,128)(2,1)}, f32[2048,512]{1,0:T(8,128)}, f32[8,128]{1,0:T(8,128)S(1)}) custom-call(s32[1]{0:T(128)} %bitcast.rank_ref, bf16[1,8192,512]{2,1,0:T(8,128)(2,1)} %values_ref.19, ...), custom_call_target="tpu_custom_call", output_to_operand_aliasing={{0}: (12, {}), {1}: (13, {}), {2}: (14, {})} | custom-call | flops 1024 | bytes 1024 | tf_op jit(solution)/shard_map/pallas_call | solution.py:260
  326.4 9.5 %collective-permute-done.46.refs_5_ = bf16[32,32,256]{2,1,0:T(8,128)(2,1)} collective-permute-done((bf16[32,32,256]{2,1,0:T(8,128)(2,1)}, bf16[32,32,256]{2,1,0:T(8,128)(2,1)}, u32[]{:S(2)}, u32[]{:S(2)}) %collective-permute-start.46) | collective-permute-done | bytes 524320 | tf_op jit(solution)/shard_map/ppermute | solution.py:193
  339.1 7.1 %shard_map.93 = (bf16[1,8192,512]{2,1,0:T(8,128)(2,1)}, bf16[1,8192,512]{2,1,0:T(8,128)(2,1)}, f32[2048,512]{1,0:T(8,128)}, f32[8,128]{1,0:T(8,128)S(1)}) custom-call(s32[1]{0:T(128)} %bitcast.rank_ref, bf16[1,8192,512]{2,1,0:T(8,128)(2,1)} %values_ref.19, ...), custom_call_target="tpu_custom_call", output_to_operand_aliasing={{0}: (12, {}), {1}: (13, {}), {2}: (14, {})} | custom-call | flops 1024 | bytes 1024 | tf_op jit(solution)/shard_map/pallas_call | solution.py:260
  365.2 5.0 %collective-permute-done.57.refs_2_ = bf16[16,32,256]{2,1,0:T(8,128)(2,1)S(1)} collective-permute-done((bf16[16,32,256]{2,1,0:T(8,128)(2,1)}, bf16[16,32,256]{2,1,0:T(8,128)(2,1)S(1)}, u32[]{:S(2)}, u32[]{:S(2)}) %collective-permute-start.57) | collective-permute-done | bytes 262176 | tf_op jit(solution)/shard_map/ppermute | solution.py:193
  370.2 5.2 %shard_map.97 = (bf16[1,8192,512]{2,1,0:T(8,128)(2,1)}, bf16[1,8192,512]{2,1,0:T(8,128)(2,1)}, f32[2048,512]{1,0:T(8,128)}, f32[8,128]{1,0:T(8,128)}) custom-call(s32[1]{0:T(128)} %bitcast.rank_ref, bf16[1,8192,512]{2,1,0:T(8,128)(2,1)} %values_ref.19, ...), custom_call_target="tpu_custom_call", output_to_operand_aliasing={{0}: (13, {}), {1}: (14, {}), {2}: (15, {})} | custom-call | flops 1024 | bytes 1024 | tf_op jit(solution)/shard_map/pallas_call | solution.py:260
  375.7 5.4 %collective-permute-done.60.refs_5_ = bf16[16,32,256]{2,1,0:T(8,128)(2,1)} collective-permute-done((bf16[16,32,256]{2,1,0:T(8,128)(2,1)}, bf16[16,32,256]{2,1,0:T(8,128)(2,1)}, u32[]{:S(2)}, u32[]{:S(2)}) %collective-permute-start.60) | collective-permute-done | bytes 262176 | tf_op jit(solution)/shard_map/ppermute | solution.py:193
  (224 shorter events, 115.2 us)
Async XLA Ops:
  7.2 363.0 %reduce-scatter.2.cloned.1.call-start = ((), (), s32[]{:S(2)}) async-start(), calls=%async_computation.1 | async-start | bytes 10485760 | tf_op jit(solution)/shard_map/reduce_scatter | solution.py:342
  51.3 25.9 %collective-permute-start.3 = (bf16[32,32,256]{2,1,0:T(8,128)(2,1)}, bf16[32,32,256]{2,1,0:T(8,128)(2,1)S(1)}, u32[]{:S(2)}, u32[]{:S(2)}) collective-permute-start(bf16[32,32,256]{2,1,0:T(8,128)(2,1)} %get-tuple-element.168), channel_id=1, source_target_pairs={{0,6},{1,7},{2,4},{3,5},{4,2},{5,3},{6,0},{7,1},{8,14},{9,15},{10,... | collective-permute-start | bytes 1572872 | tf_op jit(solution)/shard_map/ppermute | solution.py:193
  54.4 30.3 %collective-permute-start.4 = (bf16[32,32,256]{2,1,0:T(8,128)(2,1)}, bf16[32,32,256]{2,1,0:T(8,128)(2,1)S(1)}, u32[]{:S(2)}, u32[]{:S(2)}) collective-permute-start(bf16[32,32,256]{2,1,0:T(8,128)(2,1)} %get-tuple-element.169), channel_id=1, source_target_pairs={{0,2},{1,3},{2,0},{3,1},{4,6},{5,7},{6,4},{7,5},{8,10},{9,11},{10,... | collective-permute-start | bytes 1572872 | tf_op jit(solution)/shard_map/ppermute | solution.py:193
  55.7 30.5 %collective-permute-start.5 = (bf16[32,32,256]{2,1,0:T(8,128)(2,1)}, bf16[32,32,256]{2,1,0:T(8,128)(2,1)S(1)}, u32[]{:S(2)}, u32[]{:S(2)}) collective-permute-start(bf16[32,32,256]{2,1,0:T(8,128)(2,1)} %get-tuple-element.170), channel_id=1, source_target_pairs={{0,4},{1,5},{2,6},{3,7},{4,0},{5,1},{6,2},{7,3},{8,12},{9,13},{10,... | collective-permute-start | bytes 1572872 | tf_op jit(solution)/shard_map/ppermute | solution.py:193
  62.0 33.1 %collective-permute-start.6 = (bf16[32,32,256]{2,1,0:T(8,128)(2,1)}, bf16[32,32,256]{2,1,0:T(8,128)(2,1)S(1)}, u32[]{:S(2)}, u32[]{:S(2)}) collective-permute-start(bf16[32,32,256]{2,1,0:T(8,128)(2,1)} %get-tuple-element.171), channel_id=1, source_target_pairs={{0,7},{1,6},{2,5},{3,4},{4,3},{5,2},{6,1},{7,0},{8,15},{9,14},{10,... | collective-permute-start | bytes 1572872 | tf_op jit(solution)/shard_map/ppermute | solution.py:193
  77.0 31.3 %collective-permute-start.7 = (bf16[32,32,256]{2,1,0:T(8,128)(2,1)}, bf16[32,32,256]{2,1,0:T(8,128)(2,1)S(1)}, u32[]{:S(2)}, u32[]{:S(2)}) collective-permute-start(bf16[32,32,256]{2,1,0:T(8,128)(2,1)} %get-tuple-element.172), channel_id=1, source_target_pairs={{0,3},{1,2},{2,1},{3,0},{4,7},{5,6},{6,5},{7,4},{8,11},{9,10},{10,... | collective-permute-start | bytes 1572872 | tf_op jit(solution)/shard_map/ppermute | solution.py:193
  77.2 40.7 %collective-permute-start.28 = (bf16[32,32,256]{2,1,0:T(8,128)(2,1)}, bf16[32,32,256]{2,1,0:T(8,128)(2,1)S(1)}, u32[]{:S(2)}, u32[]{:S(2)}) collective-permute-start(bf16[32,32,256]{2,1,0:T(8,128)(2,1)} %get-tuple-element.202), channel_id=1, source_target_pairs={{0,6},{1,7},{2,4},{3,5},{4,2},{5,3},{6,0},{7,1},{8,14},{9,15},{10,... | collective-permute-start | bytes 1572872 | tf_op jit(solution)/shard_map/ppermute | solution.py:193
  84.7 45.0 %collective-permute-start.29 = (bf16[32,32,256]{2,1,0:T(8,128)(2,1)}, bf16[32,32,256]{2,1,0:T(8,128)(2,1)S(1)}, u32[]{:S(2)}, u32[]{:S(2)}) collective-permute-start(bf16[32,32,256]{2,1,0:T(8,128)(2,1)} %get-tuple-element.203), channel_id=1, source_target_pairs={{0,2},{1,3},{2,0},{3,1},{4,6},{5,7},{6,4},{7,5},{8,10},{9,11},{10,... | collective-permute-start | bytes 1572872 | tf_op jit(solution)/shard_map/ppermute | solution.py:193
  86.2 43.5 %collective-permute-start.8 = (bf16[32,32,256]{2,1,0:T(8,128)(2,1)}, bf16[32,32,256]{2,1,0:T(8,128)(2,1)}, u32[]{:S(2)}, u32[]{:S(2)}) collective-permute-start(bf16[32,32,256]{2,1,0:T(8,128)(2,1)} %get-tuple-element.176), channel_id=1, source_target_pairs={{0,5},{1,4},{2,7},{3,6},{4,1},{5,0},{6,3},{7,2},{8,13},{9,12},{10,... | collective-permute-start | bytes 1572872 | tf_op jit(solution)/shard_map/ppermute | solution.py:193
  95.1 36.3 %collective-permute-start.9 = (bf16[32,32,256]{2,1,0:T(8,128)(2,1)}, bf16[32,32,256]{2,1,0:T(8,128)(2,1)}, u32[]{:S(2)}, u32[]{:S(2)}) collective-permute-start(bf16[32,32,256]{2,1,0:T(8,128)(2,1)} %get-tuple-element.177), channel_id=1, source_target_pairs={{0,1},{1,0},{2,3},{3,2},{4,5},{5,4},{6,7},{7,6},{8,9},{9,8},{10,11... | collective-permute-start | bytes 1572872 | tf_op jit(solution)/shard_map/ppermute | solution.py:193
  108.3 36.3 %collective-permute-start.30 = (bf16[32,32,256]{2,1,0:T(8,128)(2,1)}, bf16[32,32,256]{2,1,0:T(8,128)(2,1)S(1)}, u32[]{:S(2)}, u32[]{:S(2)}) collective-permute-start(bf16[32,32,256]{2,1,0:T(8,128)(2,1)} %get-tuple-element.204), channel_id=1, source_target_pairs={{0,4},{1,5},{2,6},{3,7},{4,0},{5,1},{6,2},{7,3},{8,12},{9,13},{10,... | collective-permute-start | bytes 1572872 | tf_op jit(solution)/shard_map/ppermute | solution.py:193
  117.9 28.3 %collective-permute-start.31 = (bf16[32,32,256]{2,1,0:T(8,128)(2,1)}, bf16[32,32,256]{2,1,0:T(8,128)(2,1)S(1)}, u32[]{:S(2)}, u32[]{:S(2)}) collective-permute-start(bf16[32,32,256]{2,1,0:T(8,128)(2,1)} %get-tuple-element.209), channel_id=1, source_target_pairs={{0,7},{1,6},{2,5},{3,4},{4,3},{5,2},{6,1},{7,0},{8,15},{9,14},{10,... | collective-permute-start | bytes 1572872 | tf_op jit(solution)/shard_map/ppermute | solution.py:193
  147.0 27.7 %collective-permute-start.1 = (bf16[32,32,256]{2,1,0:T(8,128)(2,1)}, bf16[32,32,256]{2,1,0:T(8,128)(2,1)S(1)}, u32[]{:S(2)}, u32[]{:S(2)}) collective-permute-start(bf16[32,32,256]{2,1,0:T(8,128)(2,1)} %get-tuple-element.161), channel_id=1, source_target_pairs={{0,2},{1,3},{2,0},{3,1},{4,6},{5,7},{6,4},{7,5},{8,10},{9,11},{10,... | collective-permute-start | bytes 1572872 | tf_op jit(solution)/shard_map/ppermute | solution.py:193
  151.8 33.3 %collective-permute-start.24 = (bf16[32,32,256]{2,1,0:T(8,128)(2,1)}, bf16[32,32,256]{2,1,0:T(8,128)(2,1)S(1)}, u32[]{:S(2)}, u32[]{:S(2)}) collective-permute-start(bf16[32,32,256]{2,1,0:T(8,128)(2,1)} %get-tuple-element.197), channel_id=1, source_target_pairs={{0,7},{1,6},{2,5},{3,4},{4,3},{5,2},{6,1},{7,0},{8,15},{9,14},{10,... | collective-permute-start | bytes 1572872 | tf_op jit(solution)/shard_map/ppermute | solution.py:193
  154.7 41.7 %collective-permute-start.25 = (bf16[32,32,256]{2,1,0:T(8,128)(2,1)}, bf16[32,32,256]{2,1,0:T(8,128)(2,1)S(1)}, u32[]{:S(2)}, u32[]{:S(2)}) collective-permute-start(bf16[32,32,256]{2,1,0:T(8,128)(2,1)} %get-tuple-element.198), channel_id=1, source_target_pairs={{0,3},{1,2},{2,1},{3,0},{4,7},{5,6},{6,5},{7,4},{8,11},{9,10},{10,... | collective-permute-start | bytes 1572872 | tf_op jit(solution)/shard_map/ppermute | solution.py:193
  168.1 29.6 %collective-permute-start.26 = (bf16[32,32,256]{2,1,0:T(8,128)(2,1)}, bf16[32,32,256]{2,1,0:T(8,128)(2,1)}, u32[]{:S(2)}, u32[]{:S(2)}) collective-permute-start(bf16[32,32,256]{2,1,0:T(8,128)(2,1)} %get-tuple-element.199), channel_id=1, source_target_pairs={{0,5},{1,4},{2,7},{3,6},{4,1},{5,0},{6,3},{7,2},{8,13},{9,12},{10,... | collective-permute-start | bytes 1572872 | tf_op jit(solution)/shard_map/ppermute | solution.py:193
  174.8 36.1 %collective-permute-start.35 = (bf16[32,32,256]{2,1,0:T(8,128)(2,1)}, bf16[32,32,256]{2,1,0:T(8,128)(2,1)S(1)}, u32[]{:S(2)}, u32[]{:S(2)}) collective-permute-start(bf16[32,32,256]{2,1,0:T(8,128)(2,1)} %get-tuple-element.237), channel_id=1, source_target_pairs={{0,6},{1,7},{2,4},{3,5},{4,2},{5,3},{6,0},{7,1},{8,14},{9,15},{10,... | collective-permute-start | bytes 1572872 | tf_op jit(solution)/shard_map/ppermute | solution.py:193
  185.2 33.5 %collective-permute-start.36 = (bf16[32,32,256]{2,1,0:T(8,128)(2,1)}, bf16[32,32,256]{2,1,0:T(8,128)(2,1)S(1)}, u32[]{:S(2)}, u32[]{:S(2)}) collective-permute-start(bf16[32,32,256]{2,1,0:T(8,128)(2,1)} %get-tuple-element.238), channel_id=1, source_target_pairs={{0,2},{1,3},{2,0},{3,1},{4,6},{5,7},{6,4},{7,5},{8,10},{9,11},{10,... | collective-permute-start | bytes 1572872 | tf_op jit(solution)/shard_map/ppermute | solution.py:193
  222.3 25.1 %collective-permute-start.40 = (bf16[32,32,256]{2,1,0:T(8,128)(2,1)}, bf16[32,32,256]{2,1,0:T(8,128)(2,1)}, u32[]{:S(2)}, u32[]{:S(2)}) collective-permute-start(bf16[32,32,256]{2,1,0:T(8,128)(2,1)} %get-tuple-element.242), channel_id=1, source_target_pairs={{0,5},{1,4},{2,7},{3,6},{4,1},{5,0},{6,3},{7,2},{8,13},{9,12},{10,... | collective-permute-start | bytes 1572872 | tf_op jit(solution)/shard_map/ppermute | solution.py:193
  222.4 27.2 %collective-permute-start.41 = (bf16[32,32,256]{2,1,0:T(8,128)(2,1)}, bf16[32,32,256]{2,1,0:T(8,128)(2,1)}, u32[]{:S(2)}, u32[]{:S(2)}) collective-permute-start(bf16[32,32,256]{2,1,0:T(8,128)(2,1)} %get-tuple-element.243), channel_id=1, source_target_pairs={{0,1},{1,0},{2,3},{3,2},{4,5},{5,4},{6,7},{7,6},{8,9},{9,8},{10,11... | collective-permute-start | bytes 1572872 | tf_op jit(solution)/shard_map/ppermute | solution.py:193
  223.0 37.4 %collective-permute-start.49 = (bf16[32,32,256]{2,1,0:T(8,128)(2,1)}, bf16[32,32,256]{2,1,0:T(8,128)(2,1)S(1)}, u32[]{:S(2)}, u32[]{:S(2)}) collective-permute-start(bf16[32,32,256]{2,1,0:T(8,128)(2,1)} %get-tuple-element.260), channel_id=1, source_target_pairs={{0,6},{1,7},{2,4},{3,5},{4,2},{5,3},{6,0},{7,1},{8,14},{9,15},{10,... | collective-permute-start | bytes 1572872 | tf_op jit(solution)/shard_map/ppermute | solution.py:193
  235.7 33.1 %collective-permute-start.50 = (bf16[32,32,256]{2,1,0:T(8,128)(2,1)}, bf16[32,32,256]{2,1,0:T(8,128)(2,1)S(1)}, u32[]{:S(2)}, u32[]{:S(2)}) collective-permute-start(bf16[32,32,256]{2,1,0:T(8,128)(2,1)} %get-tuple-element.261), channel_id=1, source_target_pairs={{0,2},{1,3},{2,0},{3,1},{4,6},{5,7},{6,4},{7,5},{8,10},{9,11},{10,... | collective-permute-start | bytes 1572872 | tf_op jit(solution)/shard_map/ppermute | solution.py:193
  247.4 32.6 %collective-permute-start.52 = (bf16[32,32,256]{2,1,0:T(8,128)(2,1)}, bf16[32,32,256]{2,1,0:T(8,128)(2,1)}, u32[]{:S(2)}, u32[]{:S(2)}) collective-permute-start(bf16[32,32,256]{2,1,0:T(8,128)(2,1)} %get-tuple-element.263), channel_id=1, source_target_pairs={{0,7},{1,6},{2,5},{3,4},{4,3},{5,2},{6,1},{7,0},{8,15},{9,14},{10,... | collective-permute-start | bytes 1572872 | tf_op jit(solution)/shard_map/ppermute | solution.py:193
  249.6 41.3 %collective-permute-start.53 = (bf16[32,32,256]{2,1,0:T(8,128)(2,1)}, bf16[32,32,256]{2,1,0:T(8,128)(2,1)}, u32[]{:S(2)}, u32[]{:S(2)}) collective-permute-start(bf16[32,32,256]{2,1,0:T(8,128)(2,1)} %get-tuple-element.264), channel_id=1, source_target_pairs={{0,3},{1,2},{2,1},{3,0},{4,7},{5,6},{6,5},{7,4},{8,11},{9,10},{10,... | collective-permute-start | bytes 1572872 | tf_op jit(solution)/shard_map/ppermute | solution.py:193
  260.3 31.4 %collective-permute-start.54 = (bf16[32,32,256]{2,1,0:T(8,128)(2,1)}, bf16[32,32,256]{2,1,0:T(8,128)(2,1)S(1)}, u32[]{:S(2)}, u32[]{:S(2)}) collective-permute-start(bf16[32,32,256]{2,1,0:T(8,128)(2,1)} %get-tuple-element.265), channel_id=1, source_target_pairs={{0,5},{1,4},{2,7},{3,6},{4,1},{5,0},{6,3},{7,2},{8,13},{9,12},{10,... | collective-permute-start | bytes 1572872 | tf_op jit(solution)/shard_map/ppermute | solution.py:193
  268.8 25.0 %collective-permute-start.55 = (bf16[32,32,256]{2,1,0:T(8,128)(2,1)}, bf16[32,32,256]{2,1,0:T(8,128)(2,1)S(1)}, u32[]{:S(2)}, u32[]{:S(2)}) collective-permute-start(bf16[32,32,256]{2,1,0:T(8,128)(2,1)} %get-tuple-element.266), channel_id=1, source_target_pairs={{0,1},{1,0},{2,3},{3,2},{4,5},{5,4},{6,7},{7,6},{8,9},{9,8},{10,11... | collective-permute-start | bytes 1572872 | tf_op jit(solution)/shard_map/ppermute | solution.py:193
  269.6 32.8 %collective-permute-start.42 = (bf16[32,32,256]{2,1,0:T(8,128)(2,1)}, bf16[32,32,256]{2,1,0:T(8,128)(2,1)S(1)}, u32[]{:S(2)}, u32[]{:S(2)}) collective-permute-start(bf16[32,32,256]{2,1,0:T(8,128)(2,1)} %get-tuple-element.245), channel_id=1, source_target_pairs={{0,6},{1,7},{2,4},{3,5},{4,2},{5,3},{6,0},{7,1},{8,14},{9,15},{10,... | collective-permute-start | bytes 1572872 | tf_op jit(solution)/shard_map/ppermute | solution.py:193
  280.0 33.8 %collective-permute-start.43 = (bf16[32,32,256]{2,1,0:T(8,128)(2,1)}, bf16[32,32,256]{2,1,0:T(8,128)(2,1)S(1)}, u32[]{:S(2)}, u32[]{:S(2)}) collective-permute-start(bf16[32,32,256]{2,1,0:T(8,128)(2,1)} %get-tuple-element.246), channel_id=1, source_target_pairs={{0,2},{1,3},{2,0},{3,1},{4,6},{5,7},{6,4},{7,5},{8,10},{9,11},{10,... | collective-permute-start | bytes 1572872 | tf_op jit(solution)/shard_map/ppermute | solution.py:193
  290.9 31.6 %collective-permute-start.44 = (bf16[32,32,256]{2,1,0:T(8,128)(2,1)}, bf16[32,32,256]{2,1,0:T(8,128)(2,1)S(1)}, u32[]{:S(2)}, u32[]{:S(2)}) collective-permute-start(bf16[32,32,256]{2,1,0:T(8,128)(2,1)} %get-tuple-element.247), channel_id=1, source_target_pairs={{0,4},{1,5},{2,6},{3,7},{4,0},{5,1},{6,2},{7,3},{8,12},{9,13},{10,... | collective-permute-start | bytes 1572872 | tf_op jit(solution)/shard_map/ppermute | solution.py:193
  291.8 33.3 %collective-permute-start.45 = (bf16[32,32,256]{2,1,0:T(8,128)(2,1)}, bf16[32,32,256]{2,1,0:T(8,128)(2,1)}, u32[]{:S(2)}, u32[]{:S(2)}) collective-permute-start(bf16[32,32,256]{2,1,0:T(8,128)(2,1)} %get-tuple-element.248), channel_id=1, source_target_pairs={{0,7},{1,6},{2,5},{3,4},{4,3},{5,2},{6,1},{7,0},{8,15},{9,14},{10,... | collective-permute-start | bytes 1572872 | tf_op jit(solution)/shard_map/ppermute | solution.py:193
  293.8 42.1 %collective-permute-start.46 = (bf16[32,32,256]{2,1,0:T(8,128)(2,1)}, bf16[32,32,256]{2,1,0:T(8,128)(2,1)}, u32[]{:S(2)}, u32[]{:S(2)}) collective-permute-start(bf16[32,32,256]{2,1,0:T(8,128)(2,1)} %get-tuple-element.249), channel_id=1, source_target_pairs={{0,3},{1,2},{2,1},{3,0},{4,7},{5,6},{6,5},{7,4},{8,11},{9,10},{10,... | collective-permute-start | bytes 1572872 | tf_op jit(solution)/shard_map/ppermute | solution.py:193
  302.4 34.4 %collective-permute-start.47 = (bf16[32,32,256]{2,1,0:T(8,128)(2,1)}, bf16[32,32,256]{2,1,0:T(8,128)(2,1)}, u32[]{:S(2)}, u32[]{:S(2)}) collective-permute-start(bf16[32,32,256]{2,1,0:T(8,128)(2,1)} %get-tuple-element.250), channel_id=1, source_target_pairs={{0,5},{1,4},{2,7},{3,6},{4,1},{5,0},{6,3},{7,2},{8,13},{9,12},{10,... | collective-permute-start | bytes 1572872 | tf_op jit(solution)/shard_map/ppermute | solution.py:193
  (84 other events, 1355.4 us)
Sparse Core Ops, SparseCore 0:
  218.8 145.5 reduce-scatter.1
